TPU v7x, 256 devices: a whole 4x4x8 slice. The times are simulated.
256 devices in a mesh: inst: 8 (over y, z_hi), cell: 32 (over x, z_lo, core).
Axes of the slice: x: 4, y: 4, z: 8 (z_hi: 2, z_lo: 4; z = z_hi * 4 + z_lo), core: 2. Of those that a mesh axis runs over, the one named last changes fastest.
Arguments:
- adjoint: bfloat16 [16, 5, 64, 64, 256], P('inst', None, 'cell'), may hold values from -6 to 6
- flux_jac: bfloat16 [16, 5, 3, 64, 64, 256], P('inst', None, None, 'cell'), may hold values from -0.625 to 0.625
- shift: float32 [64, 64, 256], P('cell', 'inst'), may hold values from 0.1 to 2
Outputs:
- mesh_adjoint: float32 [3, 64, 64, 256], P(None, 'cell', 'inst')
- residual: float32 [3, 64, 64, 256], P(None, 'cell', 'inst')
All inputs are finite; a program needn't handle non-finite values.
Results may differ from a plain program's by a relative error of at most 0.0003.
Values may be sent and summed in bfloat16 or wider, within the bound.
No kernel may reach another device: no remote copies, remote signals or barrier semaphores. Data moves between devices by JAX's collectives and lax.ppermute only.
A program may use at most 64 MiB of HBM per device.

v0:
```python
import jax
import jax.numpy as jnp
from jax import lax
from jax.sharding import PartitionSpec as P

ITERS = 3


mu_shear = 1.0
lame_first = 1.5


def padded_2(block, sides, width):
    for axis, dim in sides:
        count = lax.axis_size(axis)
        forward = [(i, i + 1) for i in range(count - 1)]
        backward = [(target, source) for source, target in forward]
        low = lax.ppermute(
            lax.slice_in_dim(block, block.shape[dim] - width, None, axis=dim), axis, forward
        )
        high = lax.ppermute(lax.slice_in_dim(block, 0, width, axis=dim), axis, backward)
        block = jnp.concatenate([low, block, high], axis=dim)
    return block


def operate(field, shift):
    padded = padded_2(field, (("inst", 2), ("cell", 1)), 1)
    padded = jnp.pad(padded, ((0, 0), (0, 0), (0, 0), (1, 1)))
    center = padded[:, 1:-1, 1:-1, 1:-1]
    beside = padded[:, 2:, 1:-1, 1:-1] + padded[:, :-2, 1:-1, 1:-1]
    beside = beside + padded[:, 1:-1, 2:, 1:-1] + padded[:, 1:-1, :-2, 1:-1]
    beside = beside + padded[:, 1:-1, 1:-1, 2:] + padded[:, 1:-1, 1:-1, :-2]
    corner = padded[:, :-1, :-1, :-1]
    diverge = (
        padded[0, 1:, :-1, :-1]
        - corner[0]
        + (padded[1, :-1, 1:, :-1] - corner[1])
        + (padded[2, :-1, :-1, 1:] - corner[2])
    )
    cell_first = lax.axis_index("cell") == 0
    inst_first = lax.axis_index("inst") == 0
    keep_rows = jnp.where((jnp.arange(diverge.shape[0]) == 0) & cell_first, 0.0, 1.0).astype(
        jnp.float32
    )
    keep_cols = jnp.where((jnp.arange(diverge.shape[1]) == 0) & inst_first, 0.0, 1.0).astype(
        jnp.float32
    )
    keep_depth = jnp.where(jnp.arange(diverge.shape[2]) == 0, 0.0, 1.0).astype(jnp.float32)
    diverge = (
        diverge * keep_rows[:, None, None] * keep_cols[None, :, None] * keep_depth[None, None, :]
    )
    inner = diverge[1:, 1:, 1:]
    grad_part = jnp.stack(
        [diverge[:-1, 1:, 1:] - inner, diverge[1:, :-1, 1:] - inner, diverge[1:, 1:, :-1] - inner]
    )
    return mu_shear * (6.0 * center - beside) + shift * center + lame_first * grad_part


def squares(residual):
    return lax.psum(jnp.sum(residual * residual), ("inst", "cell"))


def local(adjoint, flux_jac, shift):
    padded = padded_2(adjoint, (("cell", 2),), 1)
    upper = jnp.einsum(
        "ivkxyz,ivxyz->kxyz", flux_jac, padded[:, :, 2:], preferred_element_type=jnp.float32
    )
    lower = jnp.einsum(
        "ivkxyz,ivxyz->kxyz", flux_jac, padded[:, :, :-2], preferred_element_type=jnp.float32
    )
    partial_sum = upper - lower
    block_cols = shift.shape[1]
    totals = lax.psum(partial_sum, "inst")
    sens = lax.dynamic_slice_in_dim(totals, lax.axis_index("inst") * block_cols, block_cols, 2)
    mesh_adjoint = jnp.zeros_like(sens)
    residual = sens
    direction = sens
    norm_now = squares(residual)
    for sweep in range(ITERS):
        image = operate(direction, shift)
        alpha = norm_now / lax.psum(jnp.sum(direction * image), ("inst", "cell"))
        mesh_adjoint = mesh_adjoint + alpha * direction
        residual = residual - alpha * image
        norm_next = squares(residual)
        direction = residual + norm_next / norm_now * direction
        norm_now = norm_next
    return (mesh_adjoint, residual)


def solution(mesh):
    placed = (
        P("inst", None, "cell", None, None),
        P("inst", None, None, "cell", None, None),
        P("cell", "inst", None),
    )
    return jax.shard_map(
        local,
        mesh=mesh,
        in_specs=placed,
        out_specs=(P(None, "cell", "inst", None), P(None, "cell", "inst", None)),
        check_vma=False,
    )
```

profile of v0, /device:TPU:1, one launch (start us, length us, event | category | flops | bytes accessed | tf_op | source)
XLA Modules:
  0.0 597.7 jit_solution(2994830070937485772)
XLA Ops:
  7.2 0.0 all-reduce.6.cloned.1.call-start
  7.2 1.1 fusion.56
  8.3 5.1 collective-permute-start
  13.5 0.0 copy-start
  13.5 2.1 collective-permute-start.1
  15.6 2.5 collective-permute-done
  18.0 1.5 collective-permute-done.1
  19.6 1.3 fusion.5
  20.8 0.0 copy-done
  20.8 0.7 fusion.1
  21.5 0.0 copy-start.2
  21.5 0.8 subtract_bitcast_fusion
  22.3 0.0 all-reduce.6.cloned.1.call-update
  22.4 111.1 %all-reduce.6.cloned.1.call-done = f32[3,2,64,256]{3,2,1,0:T(8,128)} async-done(((f32[3,2,64,256]{3,2,1,0:T(8,128)}), f32[3,2,64,256]{3,2,1,0:T(8,128)}) %all-reduce.6.cloned.1.call-update) | async-done | bytes 393232 | tf_op jit(solution)/shard_map/psum | solution.py:73
  133.5 0.0 copy-start.1
  133.5 1.0 constant_dynamic-slice_fusion.1
  134.4 1.3 collective-permute-start.2
  135.8 1.3 collective-permute-start.3
  137.1 0.8 constant_dynamic-slice_fusion.2
  137.9 0.0 collective-permute-done.2
  137.9 7.1 %collective-permute-done.3 = f32[3,2,1,256]{3,2,1,0:T(1,128)S(1)} collective-permute-done((f32[3,2,1,256]{3,2,1,0:T(1,128)S(1)}, f32[3,2,1,256]{3,2,1,0:T(1,128)S(1)}, u32[]{:S(2)}, u32[]{:S(2)}) %collective-permute-start.3) | collective-permute-done | bytes 6176 | tf_op jit(solution)/shard_map/ppermute | solution.py:21
  145.0 7.9 %collective-permute-start.4 = (f32[3,1,10,256]{3,2,1,0:T(8,128)S(1)}, f32[3,1,10,256]{3,2,1,0:T(8,128)S(1)}, u32[]{:S(2)}, u32[]{:S(2)}) collective-permute-start(f32[3,1,10,256]{3,2,1,0:T(8,128)S(1)} %get-tuple-element.26), channel_id=1, source_target_pairs={{1,0},{2,1},{3,2},{4,3},{5,4},{6,5},{7,6},{8,7},{9,8},{10,9},{11,1... | collective-permute-start | bytes 92168 | tf_op jit(solution)/shard_map/ppermute | solution.py:21
  152.9 2.5 collective-permute-start.5
  155.5 0.0 collective-permute-done.4
  155.5 1.1 collective-permute-done.5
  156.6 0.2 select_maximum_fusion.8
  156.8 0.1 fusion.23
  156.9 0.1 fusion.51
  157.0 0.0 copy-done.2
  157.0 0.7 multiply_reduce_fusion.4
  157.7 79.7 %all-reduce.3 = (f32[]{:T(128)}, f32[]{:T(128)}) all-reduce(f32[]{:T(128)} %get-tuple-element.5, f32[]{:T(128)} %get-tuple-element.4), channel_id=1, replica_groups=mesh['inst'=8,'cell'=32] {'inst','cell'}, use_global_device_ids=true, to_apply=%region_2.0 | all-reduce | flops 2 | bytes 16 | tf_op jit(solution)/shard_map/psum | solution.py:60
  238.7 0.0 copy-done.1
  238.7 0.6 multiply_reduce_fusion.3
  239.4 74.3 %psum.52 = f32[]{:T(128)} all-reduce(f32[]{:T(128)} %multiply_reduce_fusion.3), channel_id=1, replica_groups=mesh['inst'=8,'cell'=32] {'inst','cell'}, use_global_device_ids=true, to_apply=%region_6.7 | all-reduce | flops 1 | bytes 8 | tf_op jit(solution)/shard_map/psum | solution.py:60
  315.0 5.2 collective-permute-start.6
  320.2 1.3 collective-permute-start.7
  321.5 0.0 collective-permute-done.6
  321.6 7.0 %collective-permute-done.7 = f32[3,2,1,256]{3,2,1,0:T(1,128)S(1)} collective-permute-done((f32[3,2,1,256]{3,2,1,0:T(1,128)S(1)}, f32[3,2,1,256]{3,2,1,0:T(1,128)S(1)}, u32[]{:S(2)}, u32[]{:S(2)}) %collective-permute-start.7) | collective-permute-done | bytes 6176 | tf_op jit(solution)/shard_map/ppermute | solution.py:21
  328.6 4.0 collective-permute-start.8
  332.6 2.7 collective-permute-start.9
  335.3 0.0 collective-permute-done.8
  335.3 1.1 collective-permute-done.9
  336.4 0.2 select_maximum_fusion.4
  336.6 0.1 fusion.17
  336.7 0.1 fusion.48
  336.8 0.7 multiply_reduce_fusion.2
  337.5 76.2 %psum.53 = f32[]{:T(128)} all-reduce(f32[]{:T(128)} %get-tuple-element.12), channel_id=1, replica_groups=mesh['inst'=8,'cell'=32] {'inst','cell'}, use_global_device_ids=true, to_apply=%region_8.9 | all-reduce | flops 1 | bytes 8 | tf_op jit(solution)/shard_map/psum | solution.py:81
  415.0 0.6 multiply_reduce_fusion.1
  415.6 73.3 %psum.54 = f32[]{:T(128)} all-reduce(f32[]{:T(128)} %get-tuple-element.10), channel_id=1, replica_groups=mesh['inst'=8,'cell'=32] {'inst','cell'}, use_global_device_ids=true, to_apply=%region_10.11 | all-reduce | flops 1 | bytes 8 | tf_op jit(solution)/shard_map/psum | solution.py:60
  490.3 4.9 collective-permute-start.10
  495.2 1.3 collective-permute-start.11
  496.5 0.0 collective-permute-done.10
  496.5 7.0 %collective-permute-done.11 = f32[3,2,1,256]{3,2,1,0:T(1,128)S(1)} collective-permute-done((f32[3,2,1,256]{3,2,1,0:T(1,128)S(1)}, f32[3,2,1,256]{3,2,1,0:T(1,128)S(1)}, u32[]{:S(2)}, u32[]{:S(2)}) %collective-permute-start.11) | collective-permute-done | bytes 6176 | tf_op jit(solution)/shard_map/ppermute | solution.py:21
  503.5 4.0 collective-permute-start.12
  507.5 2.7 collective-permute-start.13
  510.3 0.0 collective-permute-done.12
  510.3 1.1 collective-permute-done.13
  511.4 0.2 select_maximum_fusion
  511.6 0.1 fusion.11
  511.7 0.1 fusion.45
  511.8 0.7 multiply_reduce_fusion
  512.5 76.3 %psum.55 = f32[]{:T(128)} all-reduce(f32[]{:T(128)} %get-tuple-element.8), channel_id=1, replica_groups=mesh['inst'=8,'cell'=32] {'inst','cell'}, use_global_device_ids=true, to_apply=%region_12.13 | all-reduce | flops 1 | bytes 8 | tf_op jit(solution)/shard_map/psum | solution.py:81
  590.2 0.7 multiply_subtract_fusion
  (13 shorter events, 0.2 us)
Async XLA Ops:
  7.2 126.3 %all-reduce.6.cloned.1.call-start = ((), (), s32[]{:S(2)}) async-start(), calls=%async_computation | async-start | bytes 786432 | tf_op jit(solution)/shard_map/psum | solution.py:73
  8.3 9.7 %collective-permute-start = (bf16[2,5,1,64,256]{4,3,2,1,0:T(8,128)(2,1)S(1)}, bf16[2,5,1,64,256]{4,3,2,1,0:T(8,128)(2,1)S(1)}, u32[]{:S(2)}, u32[]{:S(2)}) collective-permute-start(bf16[2,5,1,64,256]{4,3,2,1,0:T(8,128)(2,1)S(1)} %get-tuple-element.17), channel_id=1, source_target_pairs={{1,0},{2,1},{3,2},{4,3},{5,4},{6,5},{7,6},{8,7},{9,8},{10,9},{11,1... | collective-permute-start | bytes 983048 | tf_op jit(solution)/shard_map/ppermute | solution.py:21
  13.5 7.3 %copy-start = (bf16[2,5,3,2,64,256]{5,4,3,2,1,0:T(8,128)(2,1)S(1)}, bf16[2,5,3,2,64,256]{5,4,3,2,1,0:T(8,128)(2,1)}, u32[]{:S(2)}) copy-start(bf16[2,5,3,2,64,256]{5,4,3,2,1,0:T(8,128)(2,1)} %param.4) | copy-start | bytes 5898244
  13.5 6.1 %collective-permute-start.1 = (bf16[2,5,1,64,256]{4,3,2,1,0:T(8,128)(2,1)S(1)}, bf16[2,5,1,64,256]{4,3,2,1,0:T(8,128)(2,1)S(1)}, u32[]{:S(2)}, u32[]{:S(2)}) collective-permute-start(bf16[2,5,1,64,256]{4,3,2,1,0:T(8,128)(2,1)S(1)} %get-tuple-element.18), channel_id=1, source_target_pairs={{0,1},{1,2},{2,3},{3,4},{4,5},{5,6},{6,7},{7,8},{8,9},{9,10},{10,1... | collective-permute-start | bytes 983048 | tf_op jit(solution)/shard_map/ppermute | solution.py:18
  21.5 135.5 %copy-start.2 = (f32[2,8,256]{2,1,0:T(8,128)S(1)}, f32[2,8,256]{2,1,0:T(8,128)}, u32[]{:S(2)}) copy-start(f32[2,8,256]{2,1,0:T(8,128)} %param.5) | copy-start | bytes 49156
  133.5 105.3 %copy-start.1 = (f32[3,2,64,256]{3,2,1,0:T(8,128)S(1)}, f32[3,2,64,256]{3,2,1,0:T(8,128)}, u32[]{:S(2)}) copy-start(f32[3,2,64,256]{3,2,1,0:T(8,128)} %all-reduce.6.cloned.1.call-done) | copy-start | bytes 1179652
  134.4 3.5 collective-permute-start.2
  135.8 9.2 %collective-permute-start.3 = (f32[3,2,1,256]{3,2,1,0:T(1,128)S(1)}, f32[3,2,1,256]{3,2,1,0:T(1,128)S(1)}, u32[]{:S(2)}, u32[]{:S(2)}) collective-permute-start(f32[3,2,1,256]{3,2,1,0:T(1,128)S(1)} %get-tuple-element.20), channel_id=1, source_target_pairs={{32,0},{64,32},{96,64},{128,96},{160,128},{192,160},{224,192},{33,... | collective-permute-start | bytes 18440 | tf_op jit(solution)/shard_map/ppermute | solution.py:21
  145.0 10.4 %collective-permute-start.4 = (f32[3,1,10,256]{3,2,1,0:T(8,128)S(1)}, f32[3,1,10,256]{3,2,1,0:T(8,128)S(1)}, u32[]{:S(2)}, u32[]{:S(2)}) collective-permute-start(f32[3,1,10,256]{3,2,1,0:T(8,128)S(1)} %get-tuple-element.26), channel_id=1, source_target_pairs={{1,0},{2,1},{3,2},{4,3},{5,4},{6,5},{7,6},{8,7},{9,8},{10,9},{11,1... | collective-permute-start | bytes 92168 | tf_op jit(solution)/shard_map/ppermute | solution.py:21
  152.9 3.6 collective-permute-start.5
  315.0 6.5 %collective-permute-start.6 = (f32[3,2,1,256]{3,2,1,0:T(1,128)S(1)}, f32[3,2,1,256]{3,2,1,0:T(1,128)S(1)}, u32[]{:S(2)}, u32[]{:S(2)}) collective-permute-start(f32[3,2,1,256]{3,2,1,0:T(1,128)S(1)} %get-tuple-element.38), channel_id=1, source_target_pairs={{0,32},{32,64},{64,96},{96,128},{128,160},{160,192},{192,224},{1,3... | collective-permute-start | bytes 18440 | tf_op jit(solution)/shard_map/ppermute | solution.py:18
  320.2 8.3 %collective-permute-start.7 = (f32[3,2,1,256]{3,2,1,0:T(1,128)S(1)}, f32[3,2,1,256]{3,2,1,0:T(1,128)S(1)}, u32[]{:S(2)}, u32[]{:S(2)}) collective-permute-start(f32[3,2,1,256]{3,2,1,0:T(1,128)S(1)} %get-tuple-element.39), channel_id=1, source_target_pairs={{32,0},{64,32},{96,64},{128,96},{160,128},{192,160},{224,192},{33,... | collective-permute-start | bytes 18440 | tf_op jit(solution)/shard_map/ppermute | solution.py:21
  328.6 6.7 %collective-permute-start.8 = (f32[3,1,10,256]{3,2,1,0:T(8,128)S(1)}, f32[3,1,10,256]{3,2,1,0:T(8,128)S(1)}, u32[]{:S(2)}, u32[]{:S(2)}) collective-permute-start(f32[3,1,10,256]{3,2,1,0:T(8,128)S(1)} %get-tuple-element.24), channel_id=1, source_target_pairs={{1,0},{2,1},{3,2},{4,3},{5,4},{6,5},{7,6},{8,7},{9,8},{10,9},{11,1... | collective-permute-start | bytes 92168 | tf_op jit(solution)/shard_map/ppermute | solution.py:21
  332.6 3.9 collective-permute-start.9
  490.3 6.2 %collective-permute-start.10 = (f32[3,2,1,256]{3,2,1,0:T(1,128)S(1)}, f32[3,2,1,256]{3,2,1,0:T(1,128)S(1)}, u32[]{:S(2)}, u32[]{:S(2)}) collective-permute-start(f32[3,2,1,256]{3,2,1,0:T(1,128)S(1)} %get-tuple-element.36), channel_id=1, source_target_pairs={{0,32},{32,64},{64,96},{96,128},{128,160},{160,192},{192,224},{1,3... | collective-permute-start | bytes 18440 | tf_op jit(solution)/shard_map/ppermute | solution.py:18
  495.2 8.3 %collective-permute-start.11 = (f32[3,2,1,256]{3,2,1,0:T(1,128)S(1)}, f32[3,2,1,256]{3,2,1,0:T(1,128)S(1)}, u32[]{:S(2)}, u32[]{:S(2)}) collective-permute-start(f32[3,2,1,256]{3,2,1,0:T(1,128)S(1)} %get-tuple-element.37), channel_id=1, source_target_pairs={{32,0},{64,32},{96,64},{128,96},{160,128},{192,160},{224,192},{33,... | collective-permute-start | bytes 18440 | tf_op jit(solution)/shard_map/ppermute | solution.py:21
  503.5 6.7 %collective-permute-start.12 = (f32[3,1,10,256]{3,2,1,0:T(8,128)S(1)}, f32[3,1,10,256]{3,2,1,0:T(8,128)S(1)}, u32[]{:S(2)}, u32[]{:S(2)}) collective-permute-start(f32[3,1,10,256]{3,2,1,0:T(8,128)S(1)} %get-tuple-element.22), channel_id=1, source_target_pairs={{1,0},{2,1},{3,2},{4,3},{5,4},{6,5},{7,6},{8,7},{9,8},{10,9},{11,1... | collective-permute-start | bytes 92168 | tf_op jit(solution)/shard_map/ppermute | solution.py:21
  507.5 3.9 collective-permute-start.13
Sparse Core Ops, SparseCore 0:
  22.5 110.9 all-reduce.5
where the time goes:
time: 599 us; the launch traced here: 598 us
  blocking collectives  380 us (63%)
  waiting for transfers between devices  140 us (23%)
  starting transfers between devices  46.3 us (8%)
  between operations  21.1 us (4%)
  other arithmetic  7.89 us (1%)
    psum x3, blocking collectives, squares(): return lax.psum(jnp.sum(residual * residual), ('inst', 'cell'))  227 us
    psum x2, blocking collectives, local(): alpha = norm_now / lax.psum(jnp.sum(direction * image), ('inst', 'cell'))  153 us
    psum x1, waiting for transfers between devices, local(): totals = lax.psum(partial_sum, 'inst')  111 us
    ppermute x7, starting transfers between devices, padded_2(): lax.ppermute(lax.slice_in_dim(block, 0, width, axis=dim), axis, backward)  24.9 us
    ppermute x7, waiting for transfers between devices, padded_2(): lax.ppermute(lax.slice_in_dim(block, 0, width, axis=dim), axis, backward)  23.5 us
    ppermute x7, starting transfers between devices, padded_2(): lax.ppermute(lax.slice_in_dim(block, block.shape[dim] - width, None, axis...  21.4 us
  transfers between devices with their start and end apart: 15, of which 9 were waited for; matrix products, arithmetic and copies ran while one was open for 0% of the time, Pallas kernels for 0%

commit v1 on v0

v1 whole, which is shorter than its diff:
```python
import jax
import jax.numpy as jnp
import numpy as np
from jax import lax
from jax.sharding import PartitionSpec as P

ITERS = 3
MU = 1.0
LAME = 1.5
NYC, NZH, NXC, NZL, NCORE = 4, 2, 4, 4, 2
BOTH = ("inst", "cell")


def flat(y, zh, x, zl, core):
    return (((y * NZH + zh) * NXC + x) * NZL + zl) * NCORE + core


def perm_of(move):
    pairs = []
    for y, zh, x, zl, core in np.ndindex(NYC, NZH, NXC, NZL, NCORE):
        pairs.append((flat(y, zh, x, zl, core), flat(*move(y, zh, x, zl, core))))
    return pairs


def send_core(v):
    return lax.ppermute(v, "cell", [(c, c ^ 1) for c in range(32)])


def send_x(v, d):
    return lax.ppermute(v, "cell", [(c, (c + 8 * d) % 32) for c in range(32)])


def send_y(v, d):
    return lax.ppermute(v, "inst", [(i, (i + 2 * d) % 8) for i in range(8)])


def send_zh(v):
    return lax.ppermute(v, "inst", [(i, i ^ 1) for i in range(8)])


def send_z(v, d):
    def move(y, zh, x, zl, core):
        z = (zh * NZL + zl + d) % (NZH * NZL)
        return y, z // NZL, x, z % NZL, core

    return lax.ppermute(v, BOTH, perm_of(move))


def send_cell(v, d):
    return lax.ppermute(v, "cell", [(c, c + d) for c in range(32) if 0 <= c + d < 32])


def send_inst(v, d):
    return lax.ppermute(v, "inst", [(i, i + d) for i in range(8) if 0 <= i + d < 8])


def all_sum(v):
    v = v + send_core(v)
    v = v + send_y(v, 1) + send_y(v, -1) + send_y(v, 2)
    v = v + send_x(v, 1) + send_x(v, -1) + send_x(v, 2)
    low, high = send_z(v, 1), send_z(v, -1)
    pair = low + v
    triple = pair + high
    return triple + send_z(triple, 3) + send_z(pair, -3)


def operate(u, shift, x0, y0, rows, cols):
    p = jnp.pad(u, ((0, 0), (0, 0), (0, 0), (1, 1)))
    center = p[:, 1:-1, 1:-1, 1:-1]
    beside = p[:, 2:, 1:-1, 1:-1] + p[:, :-2, 1:-1, 1:-1]
    beside = beside + p[:, 1:-1, 2:, 1:-1] + p[:, 1:-1, :-2, 1:-1]
    beside = beside + p[:, 1:-1, 1:-1, 2:] + p[:, 1:-1, 1:-1, :-2]
    corner = p[:, :-1, :-1, :-1]
    dv = (
        (p[0, 1:, :-1, :-1] - corner[0])
        + (p[1, :-1, 1:, :-1] - corner[1])
        + (p[2, :-1, :-1, 1:] - corner[2])
    )
    nx, ny, nz = dv.shape
    gx = x0 + jnp.arange(nx)
    gy = y0 + jnp.arange(ny)
    gz = jnp.arange(nz) - 1
    inside_x = (gx >= 0) & (gx < rows)
    inside_y = (gy >= 0) & (gy < cols)
    inside = inside_x[:, None, None] & inside_y[None, :, None]
    dv = jnp.where(inside & (gz >= 0)[None, None, :], dv, 0.0)
    inner = dv[1:, 1:, 1:]
    grad = jnp.stack([dv[:-1, 1:, 1:] - inner, dv[1:, :-1, 1:] - inner, dv[1:, 1:, :-1] - inner])
    image = MU * (6.0 * center - beside) + shift * center + LAME * grad
    return jnp.where(inside[1:, 1:], image, 0.0)


def cg_coefficients(m):
    zero = jnp.zeros_like(m[0])
    one = zero + 1.0

    def dot(u, v):
        return sum(u[i] * v[j] * m[i + j] for i in range(4) for j in range(4) if i + j < 6)

    r, p, x = [one, zero, zero, zero], [one, zero, zero, zero], [zero] * 4
    now = m[0]
    for sweep in range(ITERS):
        q = [zero] + p[:3]
        alpha = now / dot(p, q)
        x = [a + alpha * b for a, b in zip(x, p)]
        r = [a - alpha * b for a, b in zip(r, q)]
        if sweep < ITERS - 1:
            new = dot(r, r)
            p = [a + new / now * b for a, b in zip(r, p)]
            now = new
    return x[:3], r


def local(adjoint, flux_jac, shift):
    nx, ny, nz = shift.shape
    cell = lax.axis_index("cell")
    inst = lax.axis_index("inst")
    y, zh = inst // 2, inst % 2
    rows, cols = nx * 32, ny * 8

    low = send_cell(adjoint[:, :, -1:], 1)
    high = send_cell(adjoint[:, :, :1], -1)
    padded = jnp.concatenate([low, adjoint, high], axis=2).astype(jnp.float32)
    step = padded[:, :, 2:] - padded[:, :, :-2]
    part = jnp.sum(flux_jac.astype(jnp.float32) * step[:, :, None], axis=(0, 1))

    sy = jnp.concatenate([send_inst(shift[:, -2:], 1), shift, send_inst(shift[:, :2], -1)], axis=1)
    shift_ext = jnp.concatenate([send_cell(sy, 1), sy, send_cell(sy, -1)], axis=0)

    wide = jnp.pad(part, ((0, 0), (0, 0), (3, 3), (0, 0)))

    def chunk(d):
        return lax.dynamic_slice_in_dim(wide, 2 * ny * ((y + d) % 4), 2 * ny + 6, 2)

    total = chunk(0)
    for d in (2, 1, 3):
        total = total + send_y(chunk(d), d)
    mine = lax.dynamic_slice_in_dim(total, ny * zh, ny + 6, 2)
    other = lax.dynamic_slice_in_dim(total, ny * (1 - zh), ny + 6, 2)
    block = mine + send_zh(other)
    field = jnp.concatenate(
        [send_cell(block[:, 1:], 2), send_cell(block, 1), block, send_cell(block, -1), send_cell(block[:, :1], -2)],
        axis=1,
    )
    x0, y0 = cell * nx - 3, inst * ny - 3
    w0 = field
    w1 = operate(w0, shift_ext, x0, y0, rows, cols)
    w2 = operate(w1, shift_ext[1:-1, 1:-1], x0 + 1, y0 + 1, rows, cols)
    w3 = operate(w2, shift, x0 + 2, y0 + 2, rows, cols)
    w = [w0[:, 3:-3, 3:-3], w1[:, 2:-2, 2:-2], w2[:, 1:-1, 1:-1], w3]
    pairs = ((0, 0), (0, 1), (1, 1), (1, 2), (2, 2), (2, 3))
    lanes = jnp.stack([jnp.sum((w[i] * w[j]).reshape(-1, 128), axis=0) for i, j in pairs])
    moments = jnp.sum(all_sum(lanes), axis=1)
    cx, cr = cg_coefficients([moments[k] for k in range(6)])
    mesh_adjoint = cx[0] * w[0] + cx[1] * w[1] + cx[2] * w[2]
    residual = cr[0] * w[0] + cr[1] * w[1] + cr[2] * w[2] + cr[3] * w[3]
    return mesh_adjoint, residual


def solution(mesh):
    placed = (
        P("inst", None, "cell", None, None),
        P("inst", None, None, "cell", None, None),
        P("cell", "inst", None),
    )
    return jax.shard_map(
        local,
        mesh=mesh,
        in_specs=placed,
        out_specs=(P(None, "cell", "inst", None), P(None, "cell", "inst", None)),
        check_vma=False,
    )
```

time: 599 us -> 132 us (0.22)
  the two profiles are of different devices: /device:TPU:1 before, /device:TPU:0 now
where the time goes in v1:
time: 132 us
  starting transfers between devices  57.9 us (44%)
  between operations  33.4 us (25%)
  waiting for transfers between devices  32.6 us (25%)
  other arithmetic  4.06 us (3%)
  local copies, waits for them, and re-layouts  3.65 us (3%)
    ppermute x8, starting transfers between devices, send_cell(): lax.ppermute(v, 'cell', [(c, c + d) for c in range(32) if 0 <= c + d < 32])  16.4 us
    ppermute x3, starting transfers between devices, send_x(): return lax.ppermute(v, 'cell', [(c, (c + 8 * d) % 32) for c in range(32)])  12.7 us
    ppermute x6, waiting for transfers between devices, send_y(): return lax.ppermute(v, 'inst', [(i, (i + 2 * d) % 8) for i in range(8)])  12.1 us
    ppermute x2, starting transfers between devices, send_inst(): lax.ppermute(v, 'inst', [(i, i + d) for i in range(8) if 0 <= i + d < 8])  9.75 us
    ppermute x4, waiting for transfers between devices, send_z(): return lax.ppermute(v, BOTH, perm_of(move))  8.32 us
    ppermute x6, starting transfers between devices, send_y(): return lax.ppermute(v, 'inst', [(i, (i + 2 * d) % 8) for i in range(8)])  7.7 us
    ppermute x8, waiting for transfers between devices, send_cell(): lax.ppermute(v, 'cell', [(c, c + d) for c in range(32) if 0 <= c + d < 32])  7.01 us
    ppermute x4, starting transfers between devices, send_z(): return lax.ppermute(v, BOTH, perm_of(move))  5.85 us
  transfers between devices with their start and end apart: 25, of which 13 were waited for; matrix products, arithmetic and copies ran while one was open for 1% of the time, Pallas kernels for 0%

profile of v1, /device:TPU:0, one launch (start us, length us, event | category | flops | bytes accessed | tf_op | source)
XLA Modules:
  0.0 131.5 jit_solution(7897191801845478566)
XLA Ops:
  0.6 1.2 fusion.54
  1.8 1.3 collective-permute-start.1
  3.1 3.1 %collective-permute-start = (bf16[2,5,1,64,256]{4,3,2,1,0:T(8,128)(2,1)S(1)}, bf16[2,5,1,64,256]{4,3,2,1,0:T(8,128)(2,1)S(1)}, u32[]{:S(2)}, u32[]{:S(2)}) collective-permute-start(bf16[2,5,1,64,256]{4,3,2,1,0:T(8,128)(2,1)S(1)} %get-tuple-element.6), channel_id=1, source_target_pairs={{0,1},{1,2},{2,3},{3,4},{4,5},{5,6},{6,7},{7,8},{8,9},{9,10},{10,1... | collective-permute-start | bytes 983048 | tf_op jit(solution)/shard_map/ppermute | solution.py:50
  6.2 1.3 collective-permute-start.11
  7.5 8.5 %collective-permute-start.10 = (f32[2,2,256]{2,1,0:T(2,128)S(1)}, f32[2,2,256]{2,1,0:T(2,128)S(1)}, u32[]{:S(2)}, u32[]{:S(2)}) collective-permute-start(f32[2,2,256]{2,1,0:T(2,128)S(1)} %get-tuple-element.32), channel_id=1, source_target_pairs={{0,32},{32,64},{64,96},{96,128},{128,160},{160,192},{192,224},{1,3... | collective-permute-start | bytes 12296 | tf_op jit(solution)/shard_map/ppermute | solution.py:54
  16.0 0.1 broadcast_and_fusion.2
  16.1 0.1 broadcast_and_fusion.3
  16.2 0.1 broadcast_and_fusion
  16.3 0.1 broadcast_and_fusion.1
  16.4 0.1 broadcast_and_fusion.4
  16.4 0.1 broadcast_and_fusion.5
  16.5 0.1 slice_bitcast_fusion.2
  16.6 0.1 slice_bitcast_fusion
  16.7 0.2 maximum_convert_fusion
  16.9 0.2 slice_subtract_fusion
  17.1 1.4 %copy-done.1 = bf16[2,5,3,2,64,256]{5,4,3,2,1,0:T(8,128)(2,1)S(1)} copy-done((bf16[2,5,3,2,64,256]{5,4,3,2,1,0:T(8,128)(2,1)S(1)}, bf16[2,5,3,2,64,256]{5,4,3,2,1,0:T(8,128)(2,1)}, u32[]{:S(2)}) %copy-start.1) | copy-done | bytes 1966104
  18.4 0.4 multiply_reduce_fusion
  18.9 0.1 pad_dynamic-slice_fusion.2
  18.9 2.8 %collective-permute-start.4 = (f32[3,2,22,256]{3,2,1,0:T(8,128)S(1)}, f32[3,2,22,256]{3,2,1,0:T(8,128)S(1)}, u32[]{:S(2)}, u32[]{:S(2)}) collective-permute-start(f32[3,2,22,256]{3,2,1,0:T(8,128)S(1)} %get-tuple-element.12), channel_id=1, source_target_pairs={{0,192},{32,224},{64,0},{96,32},{128,64},{160,96},{192,128},{224,1... | collective-permute-start | bytes 405512 | tf_op jit(solution)/shard_map/ppermute | solution.py:34
  21.7 2.0 %collective-permute-start.2 = (f32[3,2,22,256]{3,2,1,0:T(8,128)S(1)}, f32[3,2,22,256]{3,2,1,0:T(8,128)S(1)}, u32[]{:S(2)}, u32[]{:S(2)}) collective-permute-start(f32[3,2,22,256]{3,2,1,0:T(8,128)S(1)} %get-tuple-element.10), channel_id=1, source_target_pairs={{0,128},{32,160},{64,192},{96,224},{128,0},{160,32},{192,64},{224,... | collective-permute-start | bytes 405512 | tf_op jit(solution)/shard_map/ppermute | solution.py:34
  23.8 0.1 slice_bitcast_fusion.1
  23.9 2.0 %collective-permute-done.4 = f32[3,2,22,256]{3,2,1,0:T(8,128)S(1)} collective-permute-done((f32[3,2,22,256]{3,2,1,0:T(8,128)S(1)}, f32[3,2,22,256]{3,2,1,0:T(8,128)S(1)}, u32[]{:S(2)}, u32[]{:S(2)}) %collective-permute-start.4) | collective-permute-done | bytes 135200 | tf_op jit(solution)/shard_map/ppermute | solution.py:34
  25.8 6.5 %collective-permute-done.3 = f32[3,2,22,256]{3,2,1,0:T(8,128)S(1)} collective-permute-done((f32[3,2,22,256]{3,2,1,0:T(8,128)S(1)}, f32[3,2,22,256]{3,2,1,0:T(8,128)S(1)}, u32[]{:S(2)}, u32[]{:S(2)}) %collective-permute-start.3) | collective-permute-done | bytes 135200 | tf_op jit(solution)/shard_map/ppermute | solution.py:34
  32.4 5.4 %collective-permute-start.5 = (f32[3,2,14,256]{3,2,1,0:T(8,128)S(1)}, f32[3,2,14,256]{3,2,1,0:T(8,128)S(1)}, u32[]{:S(2)}, u32[]{:S(2)}) collective-permute-start(f32[3,2,14,256]{3,2,1,0:T(8,128)S(1)} %constant_dynamic-slice_fusion), channel_id=1, source_target_pairs={{0,32},{32,0},{64,96},{96,64},{128,160},{160,128},{192,224},{224,1... | collective-permute-start | bytes 258056 | tf_op jit(solution)/shard_map/ppermute | solution.py:38
  37.9 1.3 collective-permute-start.13
  39.2 3.0 %collective-permute-start.12 = (f32[2,12,256]{2,1,0:T(8,128)S(1)}, f32[2,12,256]{2,1,0:T(8,128)S(1)}, u32[]{:S(2)}, u32[]{:S(2)}) collective-permute-start(f32[2,12,256]{2,1,0:T(8,128)S(1)} %pad_maximum_fusion.8), channel_id=1, source_target_pairs={{0,1},{1,2},{2,3},{3,4},{4,5},{5,6},{6,7},{7,8},{8,9},{9,10},{10,1... | collective-permute-start | bytes 73736 | tf_op jit(solution)/shard_map/ppermute | solution.py:50
  42.3 3.8 %collective-permute-start.9 = (f32[3,1,14,256]{3,2,1,0:T(8,128)S(1)}, f32[3,1,14,256]{3,2,1,0:T(8,128)S(1)}, u32[]{:S(2)}, u32[]{:S(2)}) collective-permute-start(f32[3,1,14,256]{3,2,1,0:T(8,128)S(1)} %get-tuple-element.28), channel_id=1, source_target_pairs={{0,2},{1,3},{2,4},{3,5},{4,6},{5,7},{6,8},{7,9},{8,10},{9,11},{10,... | collective-permute-start | bytes 129032 | tf_op jit(solution)/shard_map/ppermute | solution.py:50
  46.2 1.4 %collective-permute-start.6 = (f32[3,2,14,256]{3,2,1,0:T(8,128)S(1)}, f32[3,2,14,256]{3,2,1,0:T(8,128)S(1)}, u32[]{:S(2)}, u32[]{:S(2)}) collective-permute-start(f32[3,2,14,256]{3,2,1,0:T(8,128)S(1)} %dynamic-slice_add_fusion), channel_id=1, source_target_pairs={{0,1},{1,2},{2,3},{3,4},{4,5},{5,6},{6,7},{7,8},{8,9},{9,10},{10,1... | collective-permute-start | bytes 258056 | tf_op jit(solution)/shard_map/ppermute | solution.py:50
  47.5 1.3 collective-permute-start.7
  48.8 1.3 collective-permute-start.8
  50.2 2.2 %collective-permute-done.7 = f32[3,2,14,256]{3,2,1,0:T(8,128)S(1)} collective-permute-done((f32[3,2,14,256]{3,2,1,0:T(8,128)S(1)}, f32[3,2,14,256]{3,2,1,0:T(8,128)S(1)}, u32[]{:S(2)}, u32[]{:S(2)}) %collective-permute-start.7) | collective-permute-done | bytes 86048 | tf_op jit(solution)/shard_map/ppermute | solution.py:50
  52.4 4.8 %collective-permute-done.8 = f32[3,1,14,256]{3,2,1,0:T(8,128)S(1)} collective-permute-done((f32[3,1,14,256]{3,2,1,0:T(8,128)S(1)}, f32[3,1,14,256]{3,2,1,0:T(8,128)S(1)}, u32[]{:S(2)}, u32[]{:S(2)}) %collective-permute-start.8) | collective-permute-done | bytes 43040 | tf_op jit(solution)/shard_map/ppermute | solution.py:50
  57.2 0.3 fusion.17
  57.5 0.1 fusion.32
  57.7 0.3 fusion.5
  58.0 0.2 fusion.27
  58.3 0.1 fusion.42
  58.4 0.2 fusion.12
  58.6 0.2 fusion.37
  58.8 0.1 fusion.51
  58.9 0.1 slice_multiply_fusion.4
  59.2 0.1 collective-permute-start.14
  59.3 1.2 collective-permute-done.14
  60.5 0.8 collective-permute-start.17
  61.3 0.8 collective-permute-start.16
  62.2 1.2 collective-permute-start.15
  63.4 2.2 %collective-permute-done.17 = f32[6,128]{1,0:T(8,128)S(1)} collective-permute-done((f32[6,128]{1,0:T(8,128)S(1)}, f32[6,128]{1,0:T(8,128)S(1)}, u32[]{:S(2)}, u32[]{:S(2)}) %collective-permute-start.17) | collective-permute-done | bytes 3104 | tf_op jit(solution)/shard_map/ppermute | solution.py:34
  65.6 1.4 %collective-permute-done.15 = f32[6,128]{1,0:T(8,128)S(1)} collective-permute-done((f32[6,128]{1,0:T(8,128)S(1)}, f32[6,128]{1,0:T(8,128)S(1)}, u32[]{:S(2)}, u32[]{:S(2)}) %collective-permute-start.15) | collective-permute-done | bytes 3104 | tf_op jit(solution)/shard_map/ppermute | solution.py:34
  67.0 10.6 %collective-permute-start.20 = (f32[6,128]{1,0:T(8,128)S(1)}, f32[6,128]{1,0:T(8,128)S(1)}, u32[]{:S(2)}, u32[]{:S(2)}) collective-permute-start(f32[6,128]{1,0:T(8,128)S(1)} %add_add_fusion.1), channel_id=1, source_target_pairs={{0,16},{1,17},{2,18},{3,19},{4,20},{5,21},{6,22},{7,23},{8,24},{9,... | collective-permute-start | bytes 9224 | tf_op jit(solution)/shard_map/ppermute | solution.py:30
  77.6 1.1 collective-permute-start.19
  78.8 0.9 collective-permute-start.18
  79.7 1.6 %collective-permute-done.19 = f32[6,128]{1,0:T(8,128)S(1)} collective-permute-done((f32[6,128]{1,0:T(8,128)S(1)}, f32[6,128]{1,0:T(8,128)S(1)}, u32[]{:S(2)}, u32[]{:S(2)}) %collective-permute-start.19) | collective-permute-done | bytes 3104 | tf_op jit(solution)/shard_map/ppermute | solution.py:30
  81.2 2.4 %collective-permute-done.18 = f32[6,128]{1,0:T(8,128)S(1)} collective-permute-done((f32[6,128]{1,0:T(8,128)S(1)}, f32[6,128]{1,0:T(8,128)S(1)}, u32[]{:S(2)}, u32[]{:S(2)}) %collective-permute-start.18) | collective-permute-done | bytes 3104 | tf_op jit(solution)/shard_map/ppermute | solution.py:30
  83.6 1.1 collective-permute-start.22
  84.7 0.9 collective-permute-start.21
  85.6 1.6 %collective-permute-done.22 = f32[6,128]{1,0:T(8,128)S(1)} collective-permute-done((f32[6,128]{1,0:T(8,128)S(1)}, f32[6,128]{1,0:T(8,128)S(1)}, u32[]{:S(2)}, u32[]{:S(2)}) %collective-permute-start.22) | collective-permute-done | bytes 3104 | tf_op jit(solution)/shard_map/ppermute | solution.py:46
  87.2 2.3 %collective-permute-done.21 = f32[6,128]{1,0:T(8,128)S(1)} collective-permute-done((f32[6,128]{1,0:T(8,128)S(1)}, f32[6,128]{1,0:T(8,128)S(1)}, u32[]{:S(2)}, u32[]{:S(2)}) %collective-permute-start.21) | collective-permute-done | bytes 3104 | tf_op jit(solution)/shard_map/ppermute | solution.py:46
  89.5 1.7 %collective-permute-start.24 = (f32[6,128]{1,0:T(8,128)S(1)}, f32[6,128]{1,0:T(8,128)S(1)}, u32[]{:S(2)}, u32[]{:S(2)}) collective-permute-start(f32[6,128]{1,0:T(8,128)S(1)} %get-tuple-element.3), channel_id=1, source_target_pairs={{0,34},{1,35},{2,36},{3,37},{4,38},{5,39},{6,0},{7,1},{8,42},{9,43... | collective-permute-start | bytes 9224 | tf_op jit(solution)/shard_map/ppermute | solution.py:46
  91.2 2.2 %collective-permute-start.23 = (f32[6,128]{1,0:T(8,128)S(1)}, f32[6,128]{1,0:T(8,128)S(1)}, u32[]{:S(2)}, u32[]{:S(2)}) collective-permute-start(f32[6,128]{1,0:T(8,128)S(1)} %get-tuple-element.2), channel_id=1, source_target_pairs={{0,6},{1,7},{2,32},{3,33},{4,34},{5,35},{6,36},{7,37},{8,14},{9,15... | collective-permute-start | bytes 9224 | tf_op jit(solution)/shard_map/ppermute | solution.py:46
  93.3 1.6 %collective-permute-done.24 = f32[6,128]{1,0:T(8,128)S(1)} collective-permute-done((f32[6,128]{1,0:T(8,128)S(1)}, f32[6,128]{1,0:T(8,128)S(1)}, u32[]{:S(2)}, u32[]{:S(2)}) %collective-permute-start.24) | collective-permute-done | bytes 3104 | tf_op jit(solution)/shard_map/ppermute | solution.py:46
  94.9 2.9 %collective-permute-done.23 = f32[6,128]{1,0:T(8,128)S(1)} collective-permute-done((f32[6,128]{1,0:T(8,128)S(1)}, f32[6,128]{1,0:T(8,128)S(1)}, u32[]{:S(2)}, u32[]{:S(2)}) %collective-permute-start.23) | collective-permute-done | bytes 3104 | tf_op jit(solution)/shard_map/ppermute | solution.py:46
  97.8 0.1 add_reduce_fusion
  97.9 0.7 fusion.57
  130.9 0.7 multiply_add_fusion
  (56 shorter events, 0.5 us)
Async XLA Ops:
  0.6 16.0 %copy-start = (bf16[2,5,2,64,256]{4,3,2,1,0:T(8,128)(2,1)S(1)}, bf16[2,5,2,64,256]{4,3,2,1,0:T(8,128)(2,1)}, u32[]{:S(2)}) copy-start(bf16[2,5,2,64,256]{4,3,2,1,0:T(8,128)(2,1)} %param.3) | copy-start | bytes 1966084
  0.6 5.6 %copy-start.2 = (f32[2,8,256]{2,1,0:T(8,128)S(1)}, f32[2,8,256]{2,1,0:T(8,128)}, u32[]{:S(2)}) copy-start(f32[2,8,256]{2,1,0:T(8,128)} %param.5) | copy-start | bytes 49156
  1.8 14.8 %collective-permute-start.1 = (bf16[2,5,1,64,256]{4,3,2,1,0:T(8,128)(2,1)S(1)}, bf16[2,5,1,64,256]{4,3,2,1,0:T(8,128)(2,1)S(1)}, u32[]{:S(2)}, u32[]{:S(2)}) collective-permute-start(bf16[2,5,1,64,256]{4,3,2,1,0:T(8,128)(2,1)S(1)} %get-tuple-element.7), channel_id=1, source_target_pairs={{1,0},{2,1},{3,2},{4,3},{5,4},{6,5},{7,6},{8,7},{9,8},{10,9},{11,1... | collective-permute-start | bytes 983048 | tf_op jit(solution)/shard_map/ppermute | solution.py:50
  3.1 13.5 %collective-permute-start = (bf16[2,5,1,64,256]{4,3,2,1,0:T(8,128)(2,1)S(1)}, bf16[2,5,1,64,256]{4,3,2,1,0:T(8,128)(2,1)S(1)}, u32[]{:S(2)}, u32[]{:S(2)}) collective-permute-start(bf16[2,5,1,64,256]{4,3,2,1,0:T(8,128)(2,1)S(1)} %get-tuple-element.6), channel_id=1, source_target_pairs={{0,1},{1,2},{2,3},{3,4},{4,5},{5,6},{6,7},{7,8},{8,9},{9,10},{10,1... | collective-permute-start | bytes 983048 | tf_op jit(solution)/shard_map/ppermute | solution.py:50
  6.2 31.6 %collective-permute-start.11 = (f32[2,2,256]{2,1,0:T(2,128)S(1)}, f32[2,2,256]{2,1,0:T(2,128)S(1)}, u32[]{:S(2)}, u32[]{:S(2)}) collective-permute-start(f32[2,2,256]{2,1,0:T(2,128)S(1)} %get-tuple-element.33), channel_id=1, source_target_pairs={{32,0},{64,32},{96,64},{128,96},{160,128},{192,160},{224,192},{33,... | collective-permute-start | bytes 12296 | tf_op jit(solution)/shard_map/ppermute | solution.py:54
  7.5 30.3 %collective-permute-start.10 = (f32[2,2,256]{2,1,0:T(2,128)S(1)}, f32[2,2,256]{2,1,0:T(2,128)S(1)}, u32[]{:S(2)}, u32[]{:S(2)}) collective-permute-start(f32[2,2,256]{2,1,0:T(2,128)S(1)} %get-tuple-element.32), channel_id=1, source_target_pairs={{0,32},{32,64},{64,96},{96,128},{128,160},{160,192},{192,224},{1,3... | collective-permute-start | bytes 12296 | tf_op jit(solution)/shard_map/ppermute | solution.py:54
  16.9 1.5 %copy-start.1 = (bf16[2,5,3,2,64,256]{5,4,3,2,1,0:T(8,128)(2,1)S(1)}, bf16[2,5,3,2,64,256]{5,4,3,2,1,0:T(8,128)(2,1)}, u32[]{:S(2)}) copy-start(bf16[2,5,3,2,64,256]{5,4,3,2,1,0:T(8,128)(2,1)} %param.4) | copy-start | bytes 5898244
  18.9 6.9 %collective-permute-start.4 = (f32[3,2,22,256]{3,2,1,0:T(8,128)S(1)}, f32[3,2,22,256]{3,2,1,0:T(8,128)S(1)}, u32[]{:S(2)}, u32[]{:S(2)}) collective-permute-start(f32[3,2,22,256]{3,2,1,0:T(8,128)S(1)} %get-tuple-element.12), channel_id=1, source_target_pairs={{0,192},{32,224},{64,0},{96,32},{128,64},{160,96},{192,128},{224,1... | collective-permute-start | bytes 405512 | tf_op jit(solution)/shard_map/ppermute | solution.py:34
  21.7 10.6 %collective-permute-start.3 = (f32[3,2,22,256]{3,2,1,0:T(8,128)S(1)}, f32[3,2,22,256]{3,2,1,0:T(8,128)S(1)}, u32[]{:S(2)}, u32[]{:S(2)}) collective-permute-start(f32[3,2,22,256]{3,2,1,0:T(8,128)S(1)} %get-tuple-element.11), channel_id=1, source_target_pairs={{0,64},{32,96},{64,128},{96,160},{128,192},{160,224},{192,0},{224,... | collective-permute-start | bytes 405512 | tf_op jit(solution)/shard_map/ppermute | solution.py:34
  21.7 10.6 %collective-permute-start.2 = (f32[3,2,22,256]{3,2,1,0:T(8,128)S(1)}, f32[3,2,22,256]{3,2,1,0:T(8,128)S(1)}, u32[]{:S(2)}, u32[]{:S(2)}) collective-permute-start(f32[3,2,22,256]{3,2,1,0:T(8,128)S(1)} %get-tuple-element.10), channel_id=1, source_target_pairs={{0,128},{32,160},{64,192},{96,224},{128,0},{160,32},{192,64},{224,... | collective-permute-start | bytes 405512 | tf_op jit(solution)/shard_map/ppermute | solution.py:34
  32.4 9.8 %collective-permute-start.5 = (f32[3,2,14,256]{3,2,1,0:T(8,128)S(1)}, f32[3,2,14,256]{3,2,1,0:T(8,128)S(1)}, u32[]{:S(2)}, u32[]{:S(2)}) collective-permute-start(f32[3,2,14,256]{3,2,1,0:T(8,128)S(1)} %constant_dynamic-slice_fusion), channel_id=1, source_target_pairs={{0,32},{32,0},{64,96},{96,64},{128,160},{160,128},{192,224},{224,1... | collective-permute-start | bytes 258056 | tf_op jit(solution)/shard_map/ppermute | solution.py:38
  37.9 8.2 %collective-permute-start.13 = (f32[2,12,256]{2,1,0:T(8,128)S(1)}, f32[2,12,256]{2,1,0:T(8,128)S(1)}, u32[]{:S(2)}, u32[]{:S(2)}) collective-permute-start(f32[2,12,256]{2,1,0:T(8,128)S(1)} %pad_maximum_fusion.8), channel_id=1, source_target_pairs={{1,0},{2,1},{3,2},{4,3},{5,4},{6,5},{7,6},{8,7},{9,8},{10,9},{11,1... | collective-permute-start | bytes 73736 | tf_op jit(solution)/shard_map/ppermute | solution.py:50
  39.2 6.9 %collective-permute-start.12 = (f32[2,12,256]{2,1,0:T(8,128)S(1)}, f32[2,12,256]{2,1,0:T(8,128)S(1)}, u32[]{:S(2)}, u32[]{:S(2)}) collective-permute-start(f32[2,12,256]{2,1,0:T(8,128)S(1)} %pad_maximum_fusion.8), channel_id=1, source_target_pairs={{0,1},{1,2},{2,3},{3,4},{4,5},{5,6},{6,7},{7,8},{8,9},{9,10},{10,1... | collective-permute-start | bytes 73736 | tf_op jit(solution)/shard_map/ppermute | solution.py:50
  42.3 7.9 %collective-permute-start.9 = (f32[3,1,14,256]{3,2,1,0:T(8,128)S(1)}, f32[3,1,14,256]{3,2,1,0:T(8,128)S(1)}, u32[]{:S(2)}, u32[]{:S(2)}) collective-permute-start(f32[3,1,14,256]{3,2,1,0:T(8,128)S(1)} %get-tuple-element.28), channel_id=1, source_target_pairs={{0,2},{1,3},{2,4},{3,5},{4,6},{5,7},{6,8},{7,9},{8,10},{9,11},{10,... | collective-permute-start | bytes 129032 | tf_op jit(solution)/shard_map/ppermute | solution.py:50
  46.2 4.0 %collective-permute-start.6 = (f32[3,2,14,256]{3,2,1,0:T(8,128)S(1)}, f32[3,2,14,256]{3,2,1,0:T(8,128)S(1)}, u32[]{:S(2)}, u32[]{:S(2)}) collective-permute-start(f32[3,2,14,256]{3,2,1,0:T(8,128)S(1)} %dynamic-slice_add_fusion), channel_id=1, source_target_pairs={{0,1},{1,2},{2,3},{3,4},{4,5},{5,6},{6,7},{7,8},{8,9},{9,10},{10,1... | collective-permute-start | bytes 258056 | tf_op jit(solution)/shard_map/ppermute | solution.py:50
  47.5 4.8 %collective-permute-start.7 = (f32[3,2,14,256]{3,2,1,0:T(8,128)S(1)}, f32[3,2,14,256]{3,2,1,0:T(8,128)S(1)}, u32[]{:S(2)}, u32[]{:S(2)}) collective-permute-start(f32[3,2,14,256]{3,2,1,0:T(8,128)S(1)} %dynamic-slice_add_fusion), channel_id=1, source_target_pairs={{1,0},{2,1},{3,2},{4,3},{5,4},{6,5},{7,6},{8,7},{9,8},{10,9},{11,1... | collective-permute-start | bytes 258056 | tf_op jit(solution)/shard_map/ppermute | solution.py:50
  48.8 8.4 %collective-permute-start.8 = (f32[3,1,14,256]{3,2,1,0:T(8,128)S(1)}, f32[3,1,14,256]{3,2,1,0:T(8,128)S(1)}, u32[]{:S(2)}, u32[]{:S(2)}) collective-permute-start(f32[3,1,14,256]{3,2,1,0:T(8,128)S(1)} %get-tuple-element.27), channel_id=1, source_target_pairs={{2,0},{3,1},{4,2},{5,3},{6,4},{7,5},{8,6},{9,7},{10,8},{11,9},{12,... | collective-permute-start | bytes 129032 | tf_op jit(solution)/shard_map/ppermute | solution.py:50
  59.2 1.2 collective-permute-start.14
  60.5 5.1 %collective-permute-start.17 = (f32[6,128]{1,0:T(8,128)S(1)}, f32[6,128]{1,0:T(8,128)S(1)}, u32[]{:S(2)}, u32[]{:S(2)}) collective-permute-start(f32[6,128]{1,0:T(8,128)S(1)} %add.606), channel_id=1, source_target_pairs={{0,128},{32,160},{64,192},{96,224},{128,0},{160,32},{192,64},{224,... | collective-permute-start | bytes 9224 | tf_op jit(solution)/shard_map/ppermute | solution.py:34
  61.3 4.3 %collective-permute-start.16 = (f32[6,128]{1,0:T(8,128)S(1)}, f32[6,128]{1,0:T(8,128)S(1)}, u32[]{:S(2)}, u32[]{:S(2)}) collective-permute-start(f32[6,128]{1,0:T(8,128)S(1)} %add.606), channel_id=1, source_target_pairs={{0,192},{32,224},{64,0},{96,32},{128,64},{160,96},{192,128},{224,1... | collective-permute-start | bytes 9224 | tf_op jit(solution)/shard_map/ppermute | solution.py:34
  62.2 4.8 %collective-permute-start.15 = (f32[6,128]{1,0:T(8,128)S(1)}, f32[6,128]{1,0:T(8,128)S(1)}, u32[]{:S(2)}, u32[]{:S(2)}) collective-permute-start(f32[6,128]{1,0:T(8,128)S(1)} %add.606), channel_id=1, source_target_pairs={{0,64},{32,96},{64,128},{96,160},{128,192},{160,224},{192,0},{224,... | collective-permute-start | bytes 9224 | tf_op jit(solution)/shard_map/ppermute | solution.py:34
  67.0 12.7 %collective-permute-start.20 = (f32[6,128]{1,0:T(8,128)S(1)}, f32[6,128]{1,0:T(8,128)S(1)}, u32[]{:S(2)}, u32[]{:S(2)}) collective-permute-start(f32[6,128]{1,0:T(8,128)S(1)} %add_add_fusion.1), channel_id=1, source_target_pairs={{0,16},{1,17},{2,18},{3,19},{4,20},{5,21},{6,22},{7,23},{8,24},{9,... | collective-permute-start | bytes 9224 | tf_op jit(solution)/shard_map/ppermute | solution.py:30
  77.6 3.6 %collective-permute-start.19 = (f32[6,128]{1,0:T(8,128)S(1)}, f32[6,128]{1,0:T(8,128)S(1)}, u32[]{:S(2)}, u32[]{:S(2)}) collective-permute-start(f32[6,128]{1,0:T(8,128)S(1)} %add_add_fusion.1), channel_id=1, source_target_pairs={{0,24},{1,25},{2,26},{3,27},{4,28},{5,29},{6,30},{7,31},{8,0},{9,1... | collective-permute-start | bytes 9224 | tf_op jit(solution)/shard_map/ppermute | solution.py:30
  78.8 4.8 %collective-permute-start.18 = (f32[6,128]{1,0:T(8,128)S(1)}, f32[6,128]{1,0:T(8,128)S(1)}, u32[]{:S(2)}, u32[]{:S(2)}) collective-permute-start(f32[6,128]{1,0:T(8,128)S(1)} %add_add_fusion.1), channel_id=1, source_target_pairs={{0,8},{1,9},{2,10},{3,11},{4,12},{5,13},{6,14},{7,15},{8,16},{9,17... | collective-permute-start | bytes 9224 | tf_op jit(solution)/shard_map/ppermute | solution.py:30
  83.6 3.6 %collective-permute-start.22 = (f32[6,128]{1,0:T(8,128)S(1)}, f32[6,128]{1,0:T(8,128)S(1)}, u32[]{:S(2)}, u32[]{:S(2)}) collective-permute-start(f32[6,128]{1,0:T(8,128)S(1)} %add_add_fusion), channel_id=1, source_target_pairs={{0,38},{1,39},{2,0},{3,1},{4,2},{5,3},{6,4},{7,5},{8,46},{9,47},{1... | collective-permute-start | bytes 9224 | tf_op jit(solution)/shard_map/ppermute | solution.py:46
  84.7 4.8 %collective-permute-start.21 = (f32[6,128]{1,0:T(8,128)S(1)}, f32[6,128]{1,0:T(8,128)S(1)}, u32[]{:S(2)}, u32[]{:S(2)}) collective-permute-start(f32[6,128]{1,0:T(8,128)S(1)} %add_add_fusion), channel_id=1, source_target_pairs={{0,2},{1,3},{2,4},{3,5},{4,6},{5,7},{6,32},{7,33},{8,10},{9,11},{1... | collective-permute-start | bytes 9224 | tf_op jit(solution)/shard_map/ppermute | solution.py:46
  89.5 5.4 %collective-permute-start.24 = (f32[6,128]{1,0:T(8,128)S(1)}, f32[6,128]{1,0:T(8,128)S(1)}, u32[]{:S(2)}, u32[]{:S(2)}) collective-permute-start(f32[6,128]{1,0:T(8,128)S(1)} %get-tuple-element.3), channel_id=1, source_target_pairs={{0,34},{1,35},{2,36},{3,37},{4,38},{5,39},{6,0},{7,1},{8,42},{9,43... | collective-permute-start | bytes 9224 | tf_op jit(solution)/shard_map/ppermute | solution.py:46
  91.2 6.6 %collective-permute-start.23 = (f32[6,128]{1,0:T(8,128)S(1)}, f32[6,128]{1,0:T(8,128)S(1)}, u32[]{:S(2)}, u32[]{:S(2)}) collective-permute-start(f32[6,128]{1,0:T(8,128)S(1)} %get-tuple-element.2), channel_id=1, source_target_pairs={{0,6},{1,7},{2,32},{3,33},{4,34},{5,35},{6,36},{7,37},{8,14},{9,15... | collective-permute-start | bytes 9224 | tf_op jit(solution)/shard_map/ppermute | solution.py:46

commit v2 on v0

v2 whole, which is shorter than its diff:
```python
import jax
import jax.numpy as jnp
import numpy as np
from jax import lax
from jax.experimental import pallas as pl
from jax.experimental.pallas import tpu as pltpu
from jax.sharding import Mesh, PartitionSpec as P

ITERS = 3
MU = 1.0
LAME = 1.5
AXES = ("y", "zh", "x", "zl", "core")
SIZES = (4, 2, 4, 4, 2)
F32 = jnp.float32


def flat(at):
    index = 0
    for size, k in zip(SIZES, at):
        index = index * size + k
    return index


def send(v, move):
    pairs = []
    for at in np.ndindex(*SIZES):
        to = move(*at)
        if to is not None:
            pairs.append((flat(at), flat(to)))
    return lax.ppermute(v, AXES, pairs)


def send_y(v, d):
    return send(v, lambda y, zh, x, zl, core: ((y + d) % 4, zh, x, zl, core))


def send_zh(v):
    return send(v, lambda y, zh, x, zl, core: (y, 1 - zh, x, zl, core))


def send_core(v):
    return send(v, lambda y, zh, x, zl, core: (y, zh, x, zl, 1 - core))


def send_cell(v, d):
    def move(y, zh, x, zl, core):
        c = x * 8 + zl * 2 + core + d
        return (y, zh, c // 8, c // 2 % 4, c % 2) if 0 <= c < 32 else None

    return send(v, move)


def send_chip(v, low_core):
    def move(y, zh, x, zl, core):
        q = x * 4 + zl + (low_core if core == 0 else -low_core)
        return (y, zh, q // 4, q % 4, core) if 0 <= q < 16 else None

    return send(v, move)


VMEM = pl.BlockSpec(memory_space=pltpu.VMEM)
SMEM = pl.BlockSpec(memory_space=pltpu.SMEM)


def call(kernel, outs, args, scratch=()):
    return pl.pallas_call(
        kernel,
        out_shape=[jax.ShapeDtypeStruct(s, F32) for s in outs],
        in_specs=[SMEM] + [VMEM] * (len(args) - 1),
        out_specs=[VMEM] * len(outs),
        scratch_shapes=list(scratch),
        compiler_params=pltpu.CompilerParams(vmem_limit_bytes=24 * 1024 * 1024),
    )(*args)


def sens_kernel(pos, f, a, lo, hi, shift, m0, m1, m2, m3, wide):
    y = pos[0]
    zero = jnp.zeros((8, 256), F32)
    for s in range(6):
        wide[s, 0:8, :] = zero
        wide[s, 64:72, :] = zero
    for rows in range(0, 64, 16):
        span = slice(rows, rows + 16)
        for x in range(2):
            total = [None] * 3
            for i in range(2):
                for v in range(5):
                    if x == 0:
                        up, down = a[i, v, 1, span, :], lo[i, v, 0, span, :]
                    else:
                        up, down = hi[i, v, 0, span, :], a[i, v, 0, span, :]
                    step = up.astype(F32) - down.astype(F32)
                    for k in range(3):
                        term = f[i, v, k, x, span, :].astype(F32) * step
                        total[k] = term if total[k] is None else total[k] + term
            for k in range(3):
                wide[k * 2 + x, rows + 3 : rows + 19, :] = total[k]
    for d, out in ((0, m0), (1, m1), (2, m2), (3, m3)):
        first = pl.multiple_of(lax.rem(y + d, 4) * 16, 16)
        for s in range(6):
            out[s * 3 : s * 3 + 3] = wide[s, pl.ds(first, 24), :].reshape(3, 8, 256)
    for out in (m1, m3):
        out[18:20] = shift[...]


def sum_y_kernel(pos, m0, r1, r2, r3, shift, own, out):
    zh = pos[1]
    for s in range(6):
        for g in range(2):
            for half, to in ((zh, own), (1 - zh, out)):
                k = s * 3 + half + g
                to[s * 2 + g] = (m0[k] + r1[k]) + (r2[k] + r3[k])
    low = zh == 0
    for x in range(2):
        below = jnp.where(low, shift[x, 6:8, :], r1[18 + x, 6:8, :])
        above = jnp.where(low, r3[18 + x, 0:2, :], shift[x, 0:2, :])
        out[12, x * 4 : x * 4 + 2, :] = below
        out[12, x * 4 + 2 : x * 4 + 4, :] = above


def block_kernel(pos, own, got, shift, block):
    for s in range(6):
        for g in range(2):
            block[s // 2, s % 2, g * 8 : g * 8 + 8, :] = own[s * 2 + g] + got[s * 2 + g]
    for x in range(2):
        block[3, x, 0:8, :] = jnp.zeros((8, 256), F32)
        block[3, x, 8:16, :] = jnp.zeros((8, 256), F32)
        block[3, x, 3:11, :] = shift[x]
        block[3, x, 1:3, :] = got[12, x * 4 : x * 4 + 2, :]
        block[3, x, 11:13, :] = got[12, x * 4 + 2 : x * 4 + 4, :]


def krylov_kernel(pos, own, mate, far, near, basis, moments, w1, w2):
    inst, cell, core = pos[2], pos[3], pos[4]
    even = core == 0

    def pick(p, q):
        return jnp.where(even, p, q)

    def start(k, x):
        if x in (3, 4):
            return own[k, x - 3]
        if x in (0, 7):
            return pick(far[k * 3], near[k]) if x == 0 else pick(near[k], far[k * 3 + 2])
        if x in (1, 2):
            return pick(far[k * 3 + x], mate[k, x - 1])
        return pick(mate[k, x - 5], far[k * 3 + x - 5])

    def shift_at(x):
        if x in (3, 4):
            return own[3, x - 3]
        if x in (1, 2):
            return pick(far[9 + x - 1], mate[3, x - 1])
        return pick(mate[3, x - 5], far[9 + x - 5])

    row = lax.broadcasted_iota(jnp.int32, (16, 256), 0) + (inst * 8 - 3)
    lane = lax.broadcasted_iota(jnp.int32, (16, 256), 1)
    in_row = (row >= 0) & (row < 64)
    first, last = lane == 0, lane == 255

    def inside(x):
        at = cell * 2 - 3 + x
        return in_row & jnp.broadcast_to((at >= 0) & (at < 64), (16, 256))

    def y_up(v):
        return pltpu.roll(v, 15, 0)

    def y_down(v):
        return pltpu.roll(v, 1, 0)

    def z_up(v):
        return jnp.where(last, 0.0, pltpu.roll(v, 255, 1))

    def z_down(v):
        return jnp.where(first, 0.0, pltpu.roll(v, 1, 1))

    def apply(u, lo, hi, keep):
        before = None
        for x in range(lo - 1, hi + 1):
            c = [u(k, x) for k in range(3)]
            u1y, u2z = y_up(c[1]), z_up(c[2])
            dv = (u(0, x + 1) - c[0]) + (u1y - c[1]) + (u2z - c[2])
            mask = inside(x)
            dv = jnp.where(mask, dv, 0.0)
            if x >= lo:
                ups = [(y_up(c[0]), z_up(c[0])), (u1y, z_up(c[1])), (y_up(c[2]), u2z)]
                grads = [before, y_down(dv), z_down(dv)]
                weight = shift_at(x) + 6.0 * MU
                for k in range(3):
                    beside = (u(k, x + 1) + u(k, x - 1)) + (ups[k][0] + y_down(c[k]))
                    beside = beside + (ups[k][1] + z_down(c[k]))
                    image = weight * c[k] - MU * beside + LAME * (grads[k] - dv)
                    keep(k, x, jnp.where(mask, image, 0.0))
            before = dv

    def put(ref):
        def keep(k, x, v):
            ref[k, x] = v

        return keep

    apply(start, 1, 6, put(w1))
    apply(lambda k, x: w1[k, x], 2, 5, put(w2))
    sums = [None] * 6

    def finish(k, x, v):
        w = [own[k, x - 3, 3:11, :], w1[k, x, 3:11, :], w2[k, x, 3:11, :], v[3:11, :]]
        for j in range(4):
            basis[j, k, x - 3] = w[j]
        for n, (i, j) in enumerate(((0, 0), (0, 1), (1, 1), (1, 2), (2, 2), (2, 3))):
            term = w[i] * w[j]
            sums[n] = term if sums[n] is None else sums[n] + term

    apply(lambda k, x: w2[k, x], 3, 4, finish)
    moments[...] = jnp.zeros((8, 128), F32)
    for n in range(6):
        line = jnp.sum(sums[n], axis=0, keepdims=True)
        moments[n : n + 1, :] = line[:, :128] + line[:, 128:]


def two_sum(a, b):
    s = a + b
    t = s - a
    return s, (a - (s - t)) + (b - t)


def two_product(a, b):
    def halves(v):
        t = 4097.0 * v
        high = t - (t - v)
        return high, v - high

    p = a * b
    ah, al = halves(a)
    bh, bl = halves(b)
    return p, ((ah * bh - p) + ah * bl + al * bh) + al * bl


def finish_kernel(pos, parts, basis, mesh_adjoint, residual):
    high = parts[0]
    low = jnp.zeros((8, 128), F32)
    for n in range(1, parts.shape[0]):
        high, error = two_sum(high, parts[n])
        low = low + error
    for step in (64, 32, 16, 8, 4, 2, 1):
        high, error = two_sum(high, pltpu.roll(high, step, 1))
        low = (low + pltpu.roll(low, step, 1)) + error

    def line(v, n):
        return jnp.broadcast_to(v[n : n + 1, :], (8, 128))

    t = line(high, 1) / line(high, 0)
    centred = [line(high, 0) + line(low, 0)]
    for n in range(1, 6):
        product, error = two_product(t, high)
        error = error + t * low
        high, more = two_sum(pltpu.roll(high, 7, 0), -product)
        low = (pltpu.roll(low, 7, 0) - error) + more
        high, low = two_sum(high, low)
        centred.append(line(high, 0) + line(low, 0))

    def dot(u, v):
        total = None
        for i, p in enumerate(u):
            for j, q in enumerate(v):
                term = p * q * centred[i + j]
                total = term if total is None else total + term
        return total

    one = jnp.ones((8, 128), F32)
    r, p, x, now = [one], [one], [], centred[0]
    for sweep in range(ITERS):
        image = [t * p[0]] + [p[n - 1] + t * p[n] for n in range(1, len(p))] + [p[-1]]
        alpha = now / dot(p, image)
        x = [x[n] + alpha * p[n] if n < len(x) else alpha * p[n] for n in range(len(p))]
        r = [r[n] - alpha * image[n] if n < len(r) else -alpha * image[n] for n in range(len(image))]
        if sweep < ITERS - 1:
            new = dot(r, r)
            beta = new / now
            p = [r[n] + beta * p[n] if n < len(p) else r[n] for n in range(len(r))]
            now = new

    def monomials(c):
        out = [c[-1]]
        for term in c[-2::-1]:
            out = [term - t * out[0]] + [out[n - 1] - t * out[n] for n in range(1, len(out))] + [out[-1]]
        return [jnp.broadcast_to(v[0:1, 0:1], (8, 256)) for v in out]

    cx, cr = monomials(x), monomials(r)
    for k in range(3):
        for s in range(2):
            w = [basis[j, k, s] for j in range(4)]
            mesh_adjoint[k, s] = cx[0] * w[0] + cx[1] * w[1] + cx[2] * w[2]
            residual[k, s] = (cr[0] * w[0] + cr[1] * w[1]) + (cr[2] * w[2] + cr[3] * w[3])


def local(adjoint, flux_jac, shift):
    y, zh = lax.axis_index("y"), lax.axis_index("zh")
    inst = lax.axis_index(("y", "zh"))
    cell = lax.axis_index(("x", "zl", "core"))
    core = lax.axis_index("core")
    pos = jnp.stack([y, zh, inst, cell, core]).astype(jnp.int32)

    lo = send_cell(adjoint[:, :, 1:], 1)
    hi = send_cell(adjoint[:, :, :1], -1)
    eight, ten = (18, 8, 256), (20, 8, 256)
    m0, m1, m2, m3 = call(
        sens_kernel,
        [eight, ten, eight, ten],
        (pos, flux_jac, adjoint, lo, hi, shift),
        [pltpu.VMEM((6, 72, 256), F32)],
    )
    r2, r1, r3 = send_y(m2, 2), send_y(m1, 1), send_y(m3, 3)
    own, out = call(sum_y_kernel, [(12, 8, 256), (13, 8, 256)], (pos, m0, r1, r2, r3, shift))
    (block,) = call(block_kernel, [(4, 2, 16, 256)], (pos, own, send_zh(out), shift))

    even = core == 0
    mate = send_core(block)
    near = send_chip(jnp.where(even, block[:3, 0], block[:3, 1]), -1)
    rows = jnp.where(
        even,
        jnp.concatenate([block[:3, 1:2], mate[:3]], axis=1),
        jnp.concatenate([mate[:3], block[:3, 0:1]], axis=1),
    )
    far = send_chip(jnp.concatenate([rows.reshape(9, 16, 256), mate[3]], axis=0), 1)
    scratch = pltpu.VMEM((3, 8, 16, 256), F32)
    basis, moments = call(
        krylov_kernel,
        [(4, 3, 2, 8, 256), (8, 128)],
        (pos, block, mate, far, near),
        [scratch, scratch],
    )
    parts = lax.all_to_all(jnp.broadcast_to(moments, (16, 8, 128)), ("y", "x"), 0, 0)
    moments = jnp.sum(parts, axis=0)
    parts = lax.all_to_all(jnp.broadcast_to(moments, (16, 8, 128)), ("zh", "zl", "core"), 0, 0)
    shape = (3, 2, 8, 256)
    return tuple(call(finish_kernel, [shape, shape], (pos, parts, basis)))


def solution(mesh):
    fine = Mesh(mesh.devices.reshape(SIZES), AXES)
    inst, cell = ("y", "zh"), ("x", "zl", "core")
    out = P(None, cell, inst, None)
    return jax.shard_map(
        local,
        mesh=fine,
        in_specs=(
            P(inst, None, cell, None, None),
            P(inst, None, None, cell, None, None),
            P(cell, inst, None),
        ),
        out_specs=(out, out),
        check_vma=False,
    )
```

time: 599 us -> 89.3 us (0.15)
  blocking collectives: 380 us -> 38.1 us
  waiting for transfers between devices: 140 us -> 14.8 us
  starting transfers between devices: 46.3 us -> 25.1 us
  between operations: 21.1 us -> 0.76 us
  other arithmetic: 7.89 us -> 0.06 us
    psum x5 -> x0, blocking collectives: 380 us -> none  [the longest x3 227 us: squares(): return lax.psum(jnp.sum(residual * residual), ('inst', 'cell'))]
    psum x1 -> x0, waiting for transfers between devices: 111 us -> none  [local(): totals = lax.psum(partial_sum, 'inst')]
    all_to_all x0 -> x2, blocking collectives: none -> 38.1 us  [the longest x1 22.9 us: local(): lax.all_to_all(jnp.broadcast_to(moments, (16, 8, 128)), ('y', 'x'), 0, 0)]
    ppermute x14 -> x9, starting transfers between devices: 46.3 us -> 25.1 us  [send(): return lax.ppermute(v, AXES, pairs)]
    ppermute x14 -> x9, waiting for transfers between devices: 28.5 us -> 14.8 us  [send(): return lax.ppermute(v, AXES, pairs)]
  transfers between devices with their start and end apart: 15 -> 9, of which waited for: 9 -> 6; matrix products, arithmetic and copies ran while one was open for 0% -> 0% of each run, Pallas kernels for 0% -> 0%
where the time goes in v2:
time: 89.3 us; the launch traced here: 88.9 us
  blocking collectives  38.1 us (43%)
  starting transfers between devices  25.1 us (28%)
  waiting for transfers between devices  14.8 us (17%)
  Pallas kernels  5.5 us (6%)
  local copies, waits for them, and re-layouts  4.6 us (5%)
    ppermute x9, starting transfers between devices, send(): return lax.ppermute(v, AXES, pairs)  25.1 us
    all_to_all x1, blocking collectives, local(): lax.all_to_all(jnp.broadcast_to(moments, (16, 8, 128)), ('y', 'x'), 0, 0)  22.9 us
    all_to_all x1, blocking collectives, local(): lax.all_to_all(jnp.broadcast_to(moments, (16, 8, 128)), ('zh', 'zl', 'cor...  15.2 us
    ppermute x9, waiting for transfers between devices, send(): return lax.ppermute(v, AXES, pairs)  14.8 us
    pallas_call x5, Pallas kernels, call(): pl.pallas_call(kernel, out_shape=[jax.ShapeDtypeStruct(s, F32) for s in o...  5.5 us
    unnamed x8, local copies, waits for them, and re-layouts  3.35 us
  transfers between devices with their start and end apart: 9, of which 6 were waited for; matrix products, arithmetic and copies ran while one was open for 0% of the time, Pallas kernels for 0%

profile of v2, /device:TPU:1, one launch (start us, length us, event | category | flops | bytes accessed | tf_op | source)
XLA Modules:
  0.0 88.9 jit_solution(6028695035778686306)
XLA Ops:
  0.6 1.1 %fusion.1 = (bf16[2,5,1,64,256]{4,3,2,1,0:T(8,128)(2,1)S(1)}, bf16[2,5,1,64,256]{4,3,2,1,0:T(8,128)(2,1)S(1)}) fusion(bf16[2,5,2,64,256]{4,3,2,1,0:T(8,128)(2,1)} %a.1), kind=kLoop, calls=%fused_computation.5 | loop fusion | bytes 1310720 | tf_op jit(solution)/shard_map/slice | solution.py:305
  1.8 5.1 %collective-permute-start.1 = (bf16[2,5,1,64,256]{4,3,2,1,0:T(8,128)(2,1)S(1)}, bf16[2,5,1,64,256]{4,3,2,1,0:T(8,128)(2,1)S(1)}, u32[]{:S(2)}, u32[]{:S(2)}) collective-permute-start(bf16[2,5,1,64,256]{4,3,2,1,0:T(8,128)(2,1)S(1)} %get-tuple-element.18), channel_id=1, source_target_pairs={{1,0},{2,1},{3,2},{4,3},{5,4},{6,5},{7,6},{8,7},{9,8},{10,9},{11,1... | collective-permute-start | bytes 983048 | tf_op jit(solution)/shard_map/ppermute | solution.py:30
  6.9 1.9 %collective-permute-start = (bf16[2,5,1,64,256]{4,3,2,1,0:T(8,128)(2,1)S(1)}, bf16[2,5,1,64,256]{4,3,2,1,0:T(8,128)(2,1)S(1)}, u32[]{:S(2)}, u32[]{:S(2)}) collective-permute-start(bf16[2,5,1,64,256]{4,3,2,1,0:T(8,128)(2,1)S(1)} %get-tuple-element.19), channel_id=1, source_target_pairs={{0,1},{1,2},{2,3},{3,4},{4,5},{5,6},{6,7},{7,8},{8,9},{9,10},{10,1... | collective-permute-start | bytes 983048 | tf_op jit(solution)/shard_map/ppermute | solution.py:30
  8.9 0.1 stack.23.pos
  9.0 2.5 %collective-permute-done.1.hi = bf16[2,5,1,64,256]{4,3,2,1,0:T(8,128)(2,1)S(1)} collective-permute-done((bf16[2,5,1,64,256]{4,3,2,1,0:T(8,128)(2,1)S(1)}, bf16[2,5,1,64,256]{4,3,2,1,0:T(8,128)(2,1)S(1)}, u32[]{:S(2)}, u32[]{:S(2)}) %collective-permute-start.1) | collective-permute-done | bytes 327712 | tf_op jit(solution)/shard_map/ppermute | solution.py:30
  11.5 1.4 %collective-permute-done.lo = bf16[2,5,1,64,256]{4,3,2,1,0:T(8,128)(2,1)S(1)} collective-permute-done((bf16[2,5,1,64,256]{4,3,2,1,0:T(8,128)(2,1)S(1)}, bf16[2,5,1,64,256]{4,3,2,1,0:T(8,128)(2,1)S(1)}, u32[]{:S(2)}, u32[]{:S(2)}) %collective-permute-start) | collective-permute-done | bytes 327712 | tf_op jit(solution)/shard_map/ppermute | solution.py:30
  12.9 0.0 copy-start
  12.9 1.1 %copy-done = bf16[2,5,2,64,256]{4,3,2,1,0:T(8,128)(2,1)S(1)} copy-done((bf16[2,5,2,64,256]{4,3,2,1,0:T(8,128)(2,1)S(1)}, bf16[2,5,2,64,256]{4,3,2,1,0:T(8,128)(2,1)}, u32[]{:S(2)}) %copy-start) | copy-done | bytes 655384
  13.9 0.0 copy-start.1
  13.9 1.5 %copy-done.1 = bf16[2,5,3,2,64,256]{5,4,3,2,1,0:T(8,128)(2,1)S(1)} copy-done((bf16[2,5,3,2,64,256]{5,4,3,2,1,0:T(8,128)(2,1)S(1)}, bf16[2,5,3,2,64,256]{5,4,3,2,1,0:T(8,128)(2,1)}, u32[]{:S(2)}) %copy-start.1) | copy-done | bytes 1966104
  15.5 0.0 copy-start.2
  15.5 0.7 copy-done.2
  16.2 0.0 copy-start.3
  16.2 1.1 %shard_map.50 = (f32[18,8,256]{2,1,0:T(8,128)S(1)}, f32[20,8,256]{2,1,0:T(8,128)S(1)}, f32[18,8,256]{2,1,0:T(8,128)S(1)}, f32[20,8,256]{2,1,0:T(8,128)S(1)}) custom-call(s32[5]{0:T(128)S(1)} %stack.23.pos, bf16[2,5,3,2,64,256]{5,4,3,2,1,0:T(8,128)(2,1)S(1)} %copy-done.1, bf16[2,5,2,64,256]{4,3,2,1,0:T(8,128)(2,1)S(1)} %copy-done, ...), custom_call_target="tpu_custom_call" | custom-call | tf_op jit(solution)/shard_map/pallas_call | solution.py:66
  17.3 1.2 %collective-permute-start.2 = (f32[20,8,256]{2,1,0:T(8,128)S(1)}, f32[20,8,256]{2,1,0:T(8,128)S(1)}, u32[]{:S(2)}, u32[]{:S(2)}) collective-permute-start(f32[20,8,256]{2,1,0:T(8,128)S(1)} %get-tuple-element.11), channel_id=1, source_target_pairs={{0,64},{1,65},{2,66},{3,67},{4,68},{5,69},{6,70},{7,71},{8,72},{9,... | collective-permute-start | bytes 491528 | tf_op jit(solution)/shard_map/ppermute | solution.py:30
  18.5 1.6 %collective-permute-start.4 = (f32[20,8,256]{2,1,0:T(8,128)S(1)}, f32[20,8,256]{2,1,0:T(8,128)S(1)}, u32[]{:S(2)}, u32[]{:S(2)}) collective-permute-start(f32[20,8,256]{2,1,0:T(8,128)S(1)} %get-tuple-element.13), channel_id=1, source_target_pairs={{0,192},{1,193},{2,194},{3,195},{4,196},{5,197},{6,198},{7,199},{8... | collective-permute-start | bytes 491528 | tf_op jit(solution)/shard_map/ppermute | solution.py:30
  20.1 1.5 %collective-permute-start.3 = (f32[18,8,256]{2,1,0:T(8,128)S(1)}, f32[18,8,256]{2,1,0:T(8,128)S(1)}, u32[]{:S(2)}, u32[]{:S(2)}) collective-permute-start(f32[18,8,256]{2,1,0:T(8,128)S(1)} %get-tuple-element.12), channel_id=1, source_target_pairs={{0,128},{1,129},{2,130},{3,131},{4,132},{5,133},{6,134},{7,135},{8... | collective-permute-start | bytes 442376 | tf_op jit(solution)/shard_map/ppermute | solution.py:30
  21.5 5.4 %collective-permute-done.3.r2 = f32[18,8,256]{2,1,0:T(8,128)S(1)} collective-permute-done((f32[18,8,256]{2,1,0:T(8,128)S(1)}, f32[18,8,256]{2,1,0:T(8,128)S(1)}, u32[]{:S(2)}, u32[]{:S(2)}) %collective-permute-start.3) | collective-permute-done | bytes 147488 | tf_op jit(solution)/shard_map/ppermute | solution.py:30
  26.9 0.0 collective-permute-done.2.r1
  27.0 0.0 collective-permute-done.4.r3
  27.0 0.6 shard_map.51
  27.6 6.0 %collective-permute-start.5 = (f32[13,8,256]{2,1,0:T(8,128)S(1)}, f32[13,8,256]{2,1,0:T(8,128)S(1)}, u32[]{:S(2)}, u32[]{:S(2)}) collective-permute-start(f32[13,8,256]{2,1,0:T(8,128)S(1)} %get-tuple-element.15), channel_id=1, source_target_pairs={{0,32},{1,33},{2,34},{3,35},{4,36},{5,37},{6,38},{7,39},{8,40},{9,... | collective-permute-start | bytes 319496 | tf_op jit(solution)/shard_map/ppermute | solution.py:30
  33.5 2.9 %collective-permute-done.5.got = f32[13,8,256]{2,1,0:T(8,128)S(1)} collective-permute-done((f32[13,8,256]{2,1,0:T(8,128)S(1)}, f32[13,8,256]{2,1,0:T(8,128)S(1)}, u32[]{:S(2)}, u32[]{:S(2)}) %collective-permute-start.5) | collective-permute-done | bytes 106528 | tf_op jit(solution)/shard_map/ppermute | solution.py:30
  36.4 0.0 copy-done.3
  36.4 0.6 shard_map.52.own
  36.9 0.3 collective-permute-start.6
  37.3 1.1 %collective-permute-done.6.mate = f32[4,2,16,256]{3,2,1,0:T(8,128)S(1)} collective-permute-done((f32[4,2,16,256]{3,2,1,0:T(8,128)S(1)}, f32[4,2,16,256]{3,2,1,0:T(8,128)S(1)}, u32[]{:S(2)}, u32[]{:S(2)}) %collective-permute-start.6) | collective-permute-done | bytes 131104 | tf_op jit(solution)/shard_map/ppermute | solution.py:30
  38.5 1.3 %collective-permute-start.7 = (f32[11,16,256]{2,1,0:T(8,128)S(1)}, f32[11,16,256]{2,1,0:T(8,128)S(1)}, u32[]{:S(2)}, u32[]{:S(2)}) collective-permute-start(f32[11,16,256]{2,1,0:T(8,128)S(1)} %pad_maximum_fusion), channel_id=1, source_target_pairs={{0,2},{2,4},{3,1},{4,6},{5,3},{6,8},{7,5},{8,10},{9,7},{10,12},{11... | collective-permute-start | bytes 540680 | tf_op jit(solution)/shard_map/ppermute | solution.py:30
  39.8 6.1 %collective-permute-start.8 = (f32[3,16,256]{2,1,0:T(8,128)S(1)}, f32[3,16,256]{2,1,0:T(8,128)S(1)}, u32[]{:S(2)}, u32[]{:S(2)}) collective-permute-start(f32[3,16,256]{2,1,0:T(8,128)S(1)} %fusion), channel_id=1, source_target_pairs={{1,3},{2,0},{3,5},{4,2},{5,7},{6,4},{7,9},{8,6},{9,11},{10,8},{11,... | collective-permute-start | bytes 147464 | tf_op jit(solution)/shard_map/ppermute | solution.py:30
  45.9 1.6 %collective-permute-done.8.near = f32[3,16,256]{2,1,0:T(8,128)S(1)} collective-permute-done((f32[3,16,256]{2,1,0:T(8,128)S(1)}, f32[3,16,256]{2,1,0:T(8,128)S(1)}, u32[]{:S(2)}, u32[]{:S(2)}) %collective-permute-start.8) | collective-permute-done | bytes 49184 | tf_op jit(solution)/shard_map/ppermute | solution.py:30
  47.5 0.0 collective-permute-done.7.far
  47.5 1.4 %shard_map.53 = (f32[4,3,2,8,256]{4,3,2,1,0:T(8,128)S(1)}, f32[8,128]{1,0:T(8,128)S(1)}) custom-call(s32[5]{0:T(128)S(1)} %stack.23.pos, f32[4,2,16,256]{3,2,1,0:T(8,128)S(1)} %shard_map.52.own, f32[4,2,16,256]{3,2,1,0:T(8,128)S(1)} %collective-permute-done.6.mate, f32[11,16,256]{2,1,0:T(8,128)S(1)} %collective-permute-done.7.far, ...), custom_call_target="tpu_custom_call" | custom-call | tf_op jit(solution)/shard_map/pallas_call | solution.py:66
  48.9 22.9 %all_to_all.10 = f32[16,8,128]{2,1,0:T(8,128)S(1)} all-to-all(f32[16,8,128]{2,1,0:T(8,128)S(1)} %broadcast_in_dim.6), channel_id=1, replica_groups=mesh['y'=4,'zh'=2,'x'=4,'zl'=4,'core'=2] {'y','x'}, dimensions={0} | all-to-all | bytes 131072 | tf_op jit(solution)/shard_map/all_to_all | solution.py:333
  71.8 15.2 %all_to_all.11.parts = f32[16,8,128]{2,1,0:T(8,128)S(1)} all-to-all(f32[16,8,128]{2,1,0:T(8,128)S(1)} %broadcast_in_dim.7), channel_id=1, replica_groups=mesh['y'=4,'zh'=2,'x'=4,'zl'=4,'core'=2] {'zh','zl','core'}, dimensions={0} | all-to-all | bytes 131072 | tf_op jit(solution)/shard_map/all_to_all | solution.py:335
  87.0 1.9 %shard_map.54 = (f32[3,2,8,256]{3,2,1,0:T(8,128)}, f32[3,2,8,256]{3,2,1,0:T(8,128)}) custom-call(s32[5]{0:T(128)S(1)} %stack.23.pos, f32[16,8,128]{2,1,0:T(8,128)S(1)} %all_to_all.11.parts, f32[4,3,2,8,256]{4,3,2,1,0:T(8,128)S(1)} %get-tuple-element.17.basis), custom_call_target="tpu_custom_call" | custom-call | tf_op jit(solution)/shard_map/pallas_call | solution.py:66
  (9 shorter events, 0.1 us)
Async XLA Ops:
  1.8 9.7 %collective-permute-start.1 = (bf16[2,5,1,64,256]{4,3,2,1,0:T(8,128)(2,1)S(1)}, bf16[2,5,1,64,256]{4,3,2,1,0:T(8,128)(2,1)S(1)}, u32[]{:S(2)}, u32[]{:S(2)}) collective-permute-start(bf16[2,5,1,64,256]{4,3,2,1,0:T(8,128)(2,1)S(1)} %get-tuple-element.18), channel_id=1, source_target_pairs={{1,0},{2,1},{3,2},{4,3},{5,4},{6,5},{7,6},{8,7},{9,8},{10,9},{11,1... | collective-permute-start | bytes 983048 | tf_op jit(solution)/shard_map/ppermute | solution.py:30
  6.9 5.9 %collective-permute-start = (bf16[2,5,1,64,256]{4,3,2,1,0:T(8,128)(2,1)S(1)}, bf16[2,5,1,64,256]{4,3,2,1,0:T(8,128)(2,1)S(1)}, u32[]{:S(2)}, u32[]{:S(2)}) collective-permute-start(bf16[2,5,1,64,256]{4,3,2,1,0:T(8,128)(2,1)S(1)} %get-tuple-element.19), channel_id=1, source_target_pairs={{0,1},{1,2},{2,3},{3,4},{4,5},{5,6},{6,7},{7,8},{8,9},{9,10},{10,1... | collective-permute-start | bytes 983048 | tf_op jit(solution)/shard_map/ppermute | solution.py:30
  12.9 1.1 %copy-start = (bf16[2,5,2,64,256]{4,3,2,1,0:T(8,128)(2,1)S(1)}, bf16[2,5,2,64,256]{4,3,2,1,0:T(8,128)(2,1)}, u32[]{:S(2)}) copy-start(bf16[2,5,2,64,256]{4,3,2,1,0:T(8,128)(2,1)} %a.1) | copy-start | bytes 1966084
  13.9 1.5 %copy-start.1 = (bf16[2,5,3,2,64,256]{5,4,3,2,1,0:T(8,128)(2,1)S(1)}, bf16[2,5,3,2,64,256]{5,4,3,2,1,0:T(8,128)(2,1)}, u32[]{:S(2)}) copy-start(bf16[2,5,3,2,64,256]{5,4,3,2,1,0:T(8,128)(2,1)} %f.1) | copy-start | bytes 5898244
  15.5 0.7 copy-start.2
  16.2 20.2 %copy-start.3 = (f32[2,8,256]{2,1,0:T(8,128)S(1)}, f32[2,8,256]{2,1,0:T(8,128)}, u32[]{:S(2)}) copy-start(f32[2,8,256]{2,1,0:T(8,128)} %shift.5) | copy-start | bytes 49156
  17.3 9.6 %collective-permute-start.2 = (f32[20,8,256]{2,1,0:T(8,128)S(1)}, f32[20,8,256]{2,1,0:T(8,128)S(1)}, u32[]{:S(2)}, u32[]{:S(2)}) collective-permute-start(f32[20,8,256]{2,1,0:T(8,128)S(1)} %get-tuple-element.11), channel_id=1, source_target_pairs={{0,64},{1,65},{2,66},{3,67},{4,68},{5,69},{6,70},{7,71},{8,72},{9,... | collective-permute-start | bytes 491528 | tf_op jit(solution)/shard_map/ppermute | solution.py:30
  18.5 8.5 %collective-permute-start.4 = (f32[20,8,256]{2,1,0:T(8,128)S(1)}, f32[20,8,256]{2,1,0:T(8,128)S(1)}, u32[]{:S(2)}, u32[]{:S(2)}) collective-permute-start(f32[20,8,256]{2,1,0:T(8,128)S(1)} %get-tuple-element.13), channel_id=1, source_target_pairs={{0,192},{1,193},{2,194},{3,195},{4,196},{5,197},{6,198},{7,199},{8... | collective-permute-start | bytes 491528 | tf_op jit(solution)/shard_map/ppermute | solution.py:30
  20.1 6.9 %collective-permute-start.3 = (f32[18,8,256]{2,1,0:T(8,128)S(1)}, f32[18,8,256]{2,1,0:T(8,128)S(1)}, u32[]{:S(2)}, u32[]{:S(2)}) collective-permute-start(f32[18,8,256]{2,1,0:T(8,128)S(1)} %get-tuple-element.12), channel_id=1, source_target_pairs={{0,128},{1,129},{2,130},{3,131},{4,132},{5,133},{6,134},{7,135},{8... | collective-permute-start | bytes 442376 | tf_op jit(solution)/shard_map/ppermute | solution.py:30
  27.6 8.8 %collective-permute-start.5 = (f32[13,8,256]{2,1,0:T(8,128)S(1)}, f32[13,8,256]{2,1,0:T(8,128)S(1)}, u32[]{:S(2)}, u32[]{:S(2)}) collective-permute-start(f32[13,8,256]{2,1,0:T(8,128)S(1)} %get-tuple-element.15), channel_id=1, source_target_pairs={{0,32},{1,33},{2,34},{3,35},{4,36},{5,37},{6,38},{7,39},{8,40},{9,... | collective-permute-start | bytes 319496 | tf_op jit(solution)/shard_map/ppermute | solution.py:30
  36.9 1.4 %collective-permute-start.6 = (f32[4,2,16,256]{3,2,1,0:T(8,128)S(1)}, f32[4,2,16,256]{3,2,1,0:T(8,128)S(1)}, u32[]{:S(2)}, u32[]{:S(2)}) collective-permute-start(f32[4,2,16,256]{3,2,1,0:T(8,128)S(1)} %shard_map.52.own), channel_id=1, source_target_pairs={{0,1},{1,0},{2,3},{3,2},{4,5},{5,4},{6,7},{7,6},{8,9},{9,8},{10,11... | collective-permute-start | bytes 393224 | tf_op jit(solution)/shard_map/ppermute | solution.py:30
  38.5 9.0 %collective-permute-start.7 = (f32[11,16,256]{2,1,0:T(8,128)S(1)}, f32[11,16,256]{2,1,0:T(8,128)S(1)}, u32[]{:S(2)}, u32[]{:S(2)}) collective-permute-start(f32[11,16,256]{2,1,0:T(8,128)S(1)} %pad_maximum_fusion), channel_id=1, source_target_pairs={{0,2},{2,4},{3,1},{4,6},{5,3},{6,8},{7,5},{8,10},{9,7},{10,12},{11... | collective-permute-start | bytes 540680 | tf_op jit(solution)/shard_map/ppermute | solution.py:30
  39.8 7.7 %collective-permute-start.8 = (f32[3,16,256]{2,1,0:T(8,128)S(1)}, f32[3,16,256]{2,1,0:T(8,128)S(1)}, u32[]{:S(2)}, u32[]{:S(2)}) collective-permute-start(f32[3,16,256]{2,1,0:T(8,128)S(1)} %fusion), channel_id=1, source_target_pairs={{1,3},{2,0},{3,5},{4,2},{5,7},{6,4},{7,9},{8,6},{9,11},{10,8},{11,... | collective-permute-start | bytes 147464 | tf_op jit(solution)/shard_map/ppermute | solution.py:30

commit v3 on v2

--- a/solution.py
+++ b/solution.py
@@ -42,116 +42,131 @@
     return send(v, lambda y, zh, x, zl, core: (y, zh, x, zl, 1 - core))
 
 
-def send_cell(v, d):
+def send_pair(v):
     def move(y, zh, x, zl, core):
-        c = x * 8 + zl * 2 + core + d
-        return (y, zh, c // 8, c // 2 % 4, c % 2) if 0 <= c < 32 else None
-
-    return send(v, move)
-
-
-def send_chip(v, low_core):
-    def move(y, zh, x, zl, core):
-        q = x * 4 + zl + (low_core if core == 0 else -low_core)
-        return (y, zh, q // 4, q % 4, core) if 0 <= q < 16 else None
+        q = x * 4 + zl + (1 if core == 1 else -1)
+        return (y, zh, q // 4, q % 4, 1 - core) if 0 <= q < 16 else None
 
     return send(v, move)
 
 
 VMEM = pl.BlockSpec(memory_space=pltpu.VMEM)
 SMEM = pl.BlockSpec(memory_space=pltpu.SMEM)
-
-
-def call(kernel, outs, args, scratch=()):
+HBM = pl.BlockSpec(memory_space=pltpu.HBM)
+
+
+def call(kernel, outs, args, scratch=(), specs=None):
     return pl.pallas_call(
         kernel,
-        out_shape=[jax.ShapeDtypeStruct(s, F32) for s in outs],
-        in_specs=[SMEM] + [VMEM] * (len(args) - 1),
+        out_shape=[s if isinstance(s, jax.ShapeDtypeStruct) else jax.ShapeDtypeStruct(s, F32) for s in outs],
+        in_specs=[SMEM] + (specs or [VMEM] * (len(args) - 1)),
         out_specs=[VMEM] * len(outs),
         scratch_shapes=list(scratch),
         compiler_params=pltpu.CompilerParams(vmem_limit_bytes=24 * 1024 * 1024),
     )(*args)
 
 
-def sens_kernel(pos, f, a, lo, hi, shift, m0, m1, m2, m3, wide):
-    y = pos[0]
+def copy_all(pairs, sems):
+    copies = [pltpu.make_async_copy(src, dst, sems.at[n]) for n, (src, dst) in enumerate(pairs)]
+    for copy in copies:
+        copy.start()
+    for copy in copies:
+        copy.wait()
+
+
+def split_flux_kernel(pos, f, shift, late, early, near_shift, sems):
+    core = pos[4]
+    copy_all(
+        [(f.at[:, :, :, 1 - core], early), (f.at[:, :, :, core], late), (shift, near_shift)], sems
+    )
+
+
+def sens_of_slab(y, sign, f, a, got, outs, wide):
     zero = jnp.zeros((8, 256), F32)
-    for s in range(6):
-        wide[s, 0:8, :] = zero
-        wide[s, 64:72, :] = zero
+    for k in range(3):
+        wide[k, 0:8, :] = zero
+        wide[k, 64:72, :] = zero
     for rows in range(0, 64, 16):
         span = slice(rows, rows + 16)
-        for x in range(2):
-            total = [None] * 3
-            for i in range(2):
-                for v in range(5):
-                    if x == 0:
-                        up, down = a[i, v, 1, span, :], lo[i, v, 0, span, :]
-                    else:
-                        up, down = hi[i, v, 0, span, :], a[i, v, 0, span, :]
-                    step = up.astype(F32) - down.astype(F32)
-                    for k in range(3):
-                        term = f[i, v, k, x, span, :].astype(F32) * step
-                        total[k] = term if total[k] is None else total[k] + term
-            for k in range(3):
-                wide[k * 2 + x, rows + 3 : rows + 19, :] = total[k]
-    for d, out in ((0, m0), (1, m1), (2, m2), (3, m3)):
+        total = [None] * 3
+        for i in range(2):
+            for v in range(5):
+                step = got[i, v, span, :].astype(F32) - a[i, v, span, :].astype(F32)
+                for k in range(3):
+                    term = f[i, v, k, span, :].astype(F32) * step
+                    total[k] = term if total[k] is None else total[k] + term
+        for k in range(3):
+            wide[k, rows + 3 : rows + 19, :] = total[k] * sign
+    for d, out in enumerate(outs):
         first = pl.multiple_of(lax.rem(y + d, 4) * 16, 16)
-        for s in range(6):
-            out[s * 3 : s * 3 + 3] = wide[s, pl.ds(first, 24), :].reshape(3, 8, 256)
+        for k in range(3):
+            out[k * 3 : k * 3 + 3] = wide[k, pl.ds(first, 24), :].reshape(3, 8, 256)
+
+
+def sens_early_kernel(pos, f, a, got, shift, m0, m1, m2, m3, wide):
+    sign = jnp.where(pos[4] == 0, 1.0, -1.0)
+    sens_of_slab(pos[0], sign, f, a, got, (m0, m1, m2, m3), wide)
     for out in (m1, m3):
-        out[18:20] = shift[...]
-
-
-def sum_y_kernel(pos, m0, r1, r2, r3, shift, own, out):
+        out[9:11] = shift[...]
+
+
+def sens_late_kernel(pos, f, a, got, m0, m1, m2, m3, wide):
+    sign = jnp.where(pos[4] == 0, -1.0, 1.0)
+    sens_of_slab(pos[0], sign, f, a, got, (m0, m1, m2, m3), wide)
+
+
+def sum_y_late_kernel(pos, m0, r1, r2, r3, own, out):
     zh = pos[1]
-    for s in range(6):
+    for s in range(3):
         for g in range(2):
             for half, to in ((zh, own), (1 - zh, out)):
                 k = s * 3 + half + g
                 to[s * 2 + g] = (m0[k] + r1[k]) + (r2[k] + r3[k])
-    low = zh == 0
+
+
+def sum_y_early_kernel(pos, m0, r1, r2, r3, shift, after, own, out):
+    sum_y_late_kernel(pos, m0, r1, r2, r3, own, out)
+    low = pos[1] == 0
     for x in range(2):
-        below = jnp.where(low, shift[x, 6:8, :], r1[18 + x, 6:8, :])
-        above = jnp.where(low, r3[18 + x, 0:2, :], shift[x, 0:2, :])
-        out[12, x * 4 : x * 4 + 2, :] = below
-        out[12, x * 4 + 2 : x * 4 + 4, :] = above
-
-
-def block_kernel(pos, own, got, shift, block):
-    for s in range(6):
+        below = jnp.where(low, shift[x, 6:8, :], r1[9 + x, 6:8, :])
+        above = jnp.where(low, r3[9 + x, 0:2, :], shift[x, 0:2, :])
+        out[6, x * 4 : x * 4 + 2, :] = below
+        out[6, x * 4 + 2 : x * 4 + 4, :] = above
+
+
+def block_late_kernel(pos, own, got, block):
+    for s in range(3):
         for g in range(2):
-            block[s // 2, s % 2, g * 8 : g * 8 + 8, :] = own[s * 2 + g] + got[s * 2 + g]
+            block[s, g * 8 : g * 8 + 8, :] = own[s * 2 + g] + got[s * 2 + g]
+
+
+def block_early_kernel(pos, own, got, shift, after, block):
+    block_late_kernel(pos, own, got, block)
     for x in range(2):
-        block[3, x, 0:8, :] = jnp.zeros((8, 256), F32)
-        block[3, x, 8:16, :] = jnp.zeros((8, 256), F32)
-        block[3, x, 3:11, :] = shift[x]
-        block[3, x, 1:3, :] = got[12, x * 4 : x * 4 + 2, :]
-        block[3, x, 11:13, :] = got[12, x * 4 + 2 : x * 4 + 4, :]
-
-
-def krylov_kernel(pos, own, mate, far, near, basis, moments, w1, w2):
+        block[3 + x, 0:8, :] = jnp.zeros((8, 256), F32)
+        block[3 + x, 8:16, :] = jnp.zeros((8, 256), F32)
+        block[3 + x, 3:11, :] = shift[x]
+        block[3 + x, 1:3, :] = got[6, x * 4 : x * 4 + 2, :]
+        block[3 + x, 11:13, :] = got[6, x * 4 + 2 : x * 4 + 4, :]
+
+
+def krylov_kernel(pos, early, late, mate_early, far_early, far_late, mate_late, basis, moments, w0, w1, w2, sh):
     inst, cell, core = pos[2], pos[3], pos[4]
-    even = core == 0
-
-    def pick(p, q):
-        return jnp.where(even, p, q)
-
-    def start(k, x):
-        if x in (3, 4):
-            return own[k, x - 3]
-        if x in (0, 7):
-            return pick(far[k * 3], near[k]) if x == 0 else pick(near[k], far[k * 3 + 2])
-        if x in (1, 2):
-            return pick(far[k * 3 + x], mate[k, x - 1])
-        return pick(mate[k, x - 5], far[k * 3 + x - 5])
-
-    def shift_at(x):
-        if x in (3, 4):
-            return own[3, x - 3]
-        if x in (1, 2):
-            return pick(far[9 + x - 1], mate[3, x - 1])
-        return pick(mate[3, x - 5], far[9 + x - 5])
+
+    def place(x):
+        return x + core * (7 - 2 * x)
+
+    for k in range(3):
+        line = (
+            far_early[3 + k], far_early[k], far_late[k], late[k],
+            early[k], mate_early[k], mate_late[k], mate_late[3 + k],
+        )
+        for x in range(8):
+            w0[k, place(x)] = line[x]
+    for x in range(2):
+        sh[1 + core * 4 + x] = far_early[6 + x]
+        sh[3 + x] = early[3 + x]
+        sh[5 - core * 4 + x] = mate_early[3 + x]
 
     row = lax.broadcasted_iota(jnp.int32, (16, 256), 0) + (inst * 8 - 3)
     lane = lax.broadcasted_iota(jnp.int32, (16, 256), 1)
@@ -185,7 +200,7 @@
             if x >= lo:
                 ups = [(y_up(c[0]), z_up(c[0])), (u1y, z_up(c[1])), (y_up(c[2]), u2z)]
                 grads = [before, y_down(dv), z_down(dv)]
-                weight = shift_at(x) + 6.0 * MU
+                weight = sh[x] + 6.0 * MU
                 for k in range(3):
                     beside = (u(k, x + 1) + u(k, x - 1)) + (ups[k][0] + y_down(c[k]))
                     beside = beside + (ups[k][1] + z_down(c[k]))
@@ -199,12 +214,12 @@
 
         return keep
 
-    apply(start, 1, 6, put(w1))
+    apply(lambda k, x: w0[k, x], 1, 6, put(w1))
     apply(lambda k, x: w1[k, x], 2, 5, put(w2))
     sums = [None] * 6
 
     def finish(k, x, v):
-        w = [own[k, x - 3, 3:11, :], w1[k, x, 3:11, :], w2[k, x, 3:11, :], v[3:11, :]]
+        w = [w0[k, x, 3:11, :], w1[k, x, 3:11, :], w2[k, x, 3:11, :], v[3:11, :]]
         for j in range(4):
             basis[j, k, x - 3] = w[j]
         for n, (i, j) in enumerate(((0, 0), (0, 1), (1, 1), (1, 2), (2, 2), (2, 3))):
@@ -301,34 +316,48 @@
     core = lax.axis_index("core")
     pos = jnp.stack([y, zh, inst, cell, core]).astype(jnp.int32)
 
-    lo = send_cell(adjoint[:, :, 1:], 1)
-    hi = send_cell(adjoint[:, :, :1], -1)
-    eight, ten = (18, 8, 256), (20, 8, 256)
+    slab_flux = jax.ShapeDtypeStruct((2, 5, 3, 64, 256), jnp.bfloat16)
+    outer = lax.dynamic_index_in_dim(adjoint, core, 2, False)
+    inner = lax.dynamic_index_in_dim(adjoint, 1 - core, 2, False)
+    got_outer = send_pair(outer)
+    got_inner = send_core(inner)
+    flux_late, flux_early, shift = call(
+        split_flux_kernel,
+        [slab_flux, slab_flux, (2, 8, 256)],
+        (pos, flux_jac, shift),
+        [pltpu.SemaphoreType.DMA((3,))],
+        [HBM, HBM],
+    )
+
+    nine, eleven = (9, 8, 256), (11, 8, 256)
+    wide = [pltpu.VMEM((3, 72, 256), F32)]
     m0, m1, m2, m3 = call(
-        sens_kernel,
-        [eight, ten, eight, ten],
-        (pos, flux_jac, adjoint, lo, hi, shift),
-        [pltpu.VMEM((6, 72, 256), F32)],
+        sens_early_kernel,
+        [nine, eleven, nine, eleven],
+        (pos, flux_early, outer, got_inner, shift),
+        wide,
     )
     r2, r1, r3 = send_y(m2, 2), send_y(m1, 1), send_y(m3, 3)
-    own, out = call(sum_y_kernel, [(12, 8, 256), (13, 8, 256)], (pos, m0, r1, r2, r3, shift))
-    (block,) = call(block_kernel, [(4, 2, 16, 256)], (pos, own, send_zh(out), shift))
-
-    even = core == 0
-    mate = send_core(block)
-    near = send_chip(jnp.where(even, block[:3, 0], block[:3, 1]), -1)
-    rows = jnp.where(
-        even,
-        jnp.concatenate([block[:3, 1:2], mate[:3]], axis=1),
-        jnp.concatenate([mate[:3], block[:3, 0:1]], axis=1),
-    )
-    far = send_chip(jnp.concatenate([rows.reshape(9, 16, 256), mate[3]], axis=0), 1)
+    n0, n1, n2, n3 = call(sens_late_kernel, [nine] * 4, (pos, flux_late, inner, got_outer), wide)
+    q2, q1, q3 = send_y(n2, 2), send_y(n1, 1), send_y(n3, 3)
+    six, seven = (6, 8, 256), (7, 8, 256)
+    own, out = call(sum_y_early_kernel, [six, seven], (pos, m0, r1, r2, r3, shift, n0))
+    got = send_zh(out)
+    own_late, out_late = call(sum_y_late_kernel, [six, six], (pos, n0, q1, q2, q3))
+    got_late = send_zh(out_late)
+    (early,) = call(block_early_kernel, [(5, 16, 256)], (pos, own, got, shift, own_late))
+    mate_early = send_core(early)
+    far_early = send_pair(jnp.concatenate([early[:3], mate_early[:3], early[3:]], axis=0))
+    (late,) = call(block_late_kernel, [(3, 16, 256)], (pos, own_late, got_late))
+    far_late = send_pair(late)
+    mate_late = send_core(jnp.concatenate([late, far_late], axis=0))
+
     scratch = pltpu.VMEM((3, 8, 16, 256), F32)
     basis, moments = call(
         krylov_kernel,
         [(4, 3, 2, 8, 256), (8, 128)],
-        (pos, block, mate, far, near),
-        [scratch, scratch],
+        (pos, early, late, mate_early, far_early, far_late, mate_late),
+        [scratch, scratch, scratch, pltpu.VMEM((8, 16, 256), F32)],
     )
     parts = lax.all_to_all(jnp.broadcast_to(moments, (16, 8, 128)), ("y", "x"), 0, 0)
     moments = jnp.sum(parts, axis=0)

time: 89.3 us -> 84.8 us (0.950)
  blocking collectives: 38.1 us -> 31.4 us
  starting transfers between devices: 25.1 us -> 30.2 us
  waiting for transfers between devices: 14.8 us -> 10.6 us
  Pallas kernels: 5.5 us -> 7.94 us
  local copies, waits for them, and re-layouts: 4.6 us -> 3.5 us
    all_to_all x1, blocking collectives: 22.9 us -> 14.8 us  [local(): lax.all_to_all(jnp.broadcast_to(moments, (16, 8, 128)), ('y', 'x'), 0, 0)]
    ppermute x9 -> x14, starting transfers between devices: 25.1 us -> 30.2 us  [send(): return lax.ppermute(v, AXES, pairs)]
    ppermute x9 -> x14, waiting for transfers between devices: 14.8 us -> 10.6 us  [send(): return lax.ppermute(v, AXES, pairs)]
    pallas_call x5 -> x9, Pallas kernels: 5.5 us -> 7.94 us  [call(): pl.pallas_call(kernel, out_shape=[s if isinstance(s, jax.ShapeDtypeStruct...]
    all_to_all x1, blocking collectives: 15.2 us -> 16.6 us  [local(): lax.all_to_all(jnp.broadcast_to(moments, (16, 8, 128)), ('zh', 'zl', 'cor...]
    slice x3, local copies, waits for them, and re-layouts: 1.15 us -> 0.01 us  [the longest x1 0.01 us: local(): early[:3]]
    squeeze x1, local copies, waits for them, and re-layouts: 0.01 us -> 1.13 us  [local(): inner = lax.dynamic_index_in_dim(adjoint, 1 - core, 2, False)]
    unnamed x8 -> x4, local copies, waits for them, and re-layouts: 3.35 us -> 2.26 us
  transfers between devices with their start and end apart: 9 -> 14, of which waited for: 6 -> 6; matrix products, arithmetic and copies ran while one was open for 0% -> 0% of each run, Pallas kernels for 0% -> 5%
where the time goes in v3:
time: 84.8 us; the launch traced here: 84.5 us
  blocking collectives  31.4 us (37%)
  starting transfers between devices  30.2 us (36%)
  waiting for transfers between devices  10.6 us (12%)
  Pallas kernels  7.94 us (9%)
  local copies, waits for them, and re-layouts  3.5 us (4%)
    ppermute x14, starting transfers between devices, send(): return lax.ppermute(v, AXES, pairs)  30.2 us
    all_to_all x1, blocking collectives, local(): lax.all_to_all(jnp.broadcast_to(moments, (16, 8, 128)), ('zh', 'zl', 'cor...  16.6 us
    all_to_all x1, blocking collectives, local(): lax.all_to_all(jnp.broadcast_to(moments, (16, 8, 128)), ('y', 'x'), 0, 0)  14.8 us
    ppermute x14, waiting for transfers between devices, send(): return lax.ppermute(v, AXES, pairs)  10.6 us
    pallas_call x9, Pallas kernels, call(): pl.pallas_call(kernel, out_shape=[s if isinstance(s, jax.ShapeDtypeStruct...  7.94 us
    unnamed x4, local copies, waits for them, and re-layouts  2.26 us
  transfers between devices with their start and end apart: 14, of which 6 were waited for; matrix products, arithmetic and copies ran while one was open for 0% of the time, Pallas kernels for 5%

profile of v3, /device:TPU:1, one launch (start us, length us, event | category | flops | bytes accessed | tf_op | source)
XLA Modules:
  0.0 84.5 jit_solution(4762154256233849944)
XLA Ops:
  0.6 1.1 %dynamic-slice_bitcast_fusion = (bf16[2,5,64,256]{3,2,1,0:T(8,128)(2,1)S(1)}, bf16[2,5,64,256]{3,2,1,0:T(8,128)(2,1)S(1)}) fusion(bf16[2,5,2,64,256]{4,3,2,1,0:T(8,128)(2,1)} %param.3, s32[]{:T(128)S(6)} %select_n.8, s32[]{:T(128)S(6)} %select_n.7), kind=kLoop, calls=%fused_computation | loop fusion | bytes 1310728 | tf_op jit(solution)/shard_map/jit(dynamic_index_in_dim)/squeeze | solution.py:321
  1.8 3.3 %collective-permute-start = (bf16[2,5,64,256]{3,2,1,0:T(8,128)(2,1)S(1)}, bf16[2,5,64,256]{3,2,1,0:T(8,128)(2,1)S(1)}, u32[]{:S(2)}, u32[]{:S(2)}) collective-permute-start(bf16[2,5,64,256]{3,2,1,0:T(8,128)(2,1)S(1)} %get-tuple-element.36.a), channel_id=1, source_target_pairs={{0,1},{1,0},{2,3},{3,2},{4,5},{5,4},{6,7},{7,6},{8,9},{9,8},{10,11... | collective-permute-start | bytes 983048 | tf_op jit(solution)/shard_map/ppermute | solution.py:30
  5.1 1.9 %collective-permute-start.4 = (bf16[2,5,64,256]{3,2,1,0:T(8,128)(2,1)S(1)}, bf16[2,5,64,256]{3,2,1,0:T(8,128)(2,1)S(1)}, u32[]{:S(2)}, u32[]{:S(2)}) collective-permute-start(bf16[2,5,64,256]{3,2,1,0:T(8,128)(2,1)S(1)} %get-tuple-element.37.a), channel_id=1, source_target_pairs={{1,2},{2,1},{3,4},{4,3},{5,6},{6,5},{7,8},{8,7},{9,10},{10,9},{11,... | collective-permute-start | bytes 983048 | tf_op jit(solution)/shard_map/ppermute | solution.py:30
  7.0 0.1 stack.23.pos
  7.1 0.0 copy-start
  7.1 1.5 %copy-done = bf16[2,5,3,2,64,256]{5,4,3,2,1,0:T(8,128)(2,1)S(1)} copy-done((bf16[2,5,3,2,64,256]{5,4,3,2,1,0:T(8,128)(2,1)S(1)}, bf16[2,5,3,2,64,256]{5,4,3,2,1,0:T(8,128)(2,1)}, u32[]{:S(2)}) %copy-start) | copy-done | bytes 1966104
  8.7 0.0 copy-start.1
  8.7 0.7 copy-done.1
  9.4 0.8 shard_map.50
  10.1 0.0 collective-permute-done.got
  10.2 0.8 shard_map.51
  11.0 1.2 %collective-permute-start.1 = (f32[11,8,256]{2,1,0:T(8,128)S(1)}, f32[11,8,256]{2,1,0:T(8,128)S(1)}, u32[]{:S(2)}, u32[]{:S(2)}) collective-permute-start(f32[11,8,256]{2,1,0:T(8,128)S(1)} %get-tuple-element.22), channel_id=1, source_target_pairs={{0,64},{1,65},{2,66},{3,67},{4,68},{5,69},{6,70},{7,71},{8,72},{9,... | collective-permute-start | bytes 270344 | tf_op jit(solution)/shard_map/ppermute | solution.py:30
  12.2 1.6 %collective-permute-start.3 = (f32[11,8,256]{2,1,0:T(8,128)S(1)}, f32[11,8,256]{2,1,0:T(8,128)S(1)}, u32[]{:S(2)}, u32[]{:S(2)}) collective-permute-start(f32[11,8,256]{2,1,0:T(8,128)S(1)} %get-tuple-element.24), channel_id=1, source_target_pairs={{0,192},{1,193},{2,194},{3,195},{4,196},{5,197},{6,198},{7,199},{8... | collective-permute-start | bytes 270344 | tf_op jit(solution)/shard_map/ppermute | solution.py:30
  13.7 1.5 %collective-permute-start.2 = (f32[9,8,256]{2,1,0:T(8,128)S(1)}, f32[9,8,256]{2,1,0:T(8,128)S(1)}, u32[]{:S(2)}, u32[]{:S(2)}) collective-permute-start(f32[9,8,256]{2,1,0:T(8,128)S(1)} %get-tuple-element.23), channel_id=1, source_target_pairs={{0,128},{1,129},{2,130},{3,131},{4,132},{5,133},{6,134},{7,135},{8... | collective-permute-start | bytes 221192 | tf_op jit(solution)/shard_map/ppermute | solution.py:30
  15.3 1.5 %collective-permute-done.4.got = bf16[2,5,64,256]{3,2,1,0:T(8,128)(2,1)S(1)} collective-permute-done((bf16[2,5,64,256]{3,2,1,0:T(8,128)(2,1)S(1)}, bf16[2,5,64,256]{3,2,1,0:T(8,128)(2,1)S(1)}, u32[]{:S(2)}, u32[]{:S(2)}) %collective-permute-start.4) | collective-permute-done | bytes 327712 | tf_op jit(solution)/shard_map/ppermute | solution.py:30
  16.7 0.8 shard_map.52
  17.5 0.1 collective-permute-start.6
  17.6 0.5 collective-permute-start.7
  18.1 1.1 %collective-permute-done.2.r2 = f32[9,8,256]{2,1,0:T(8,128)S(1)} collective-permute-done((f32[9,8,256]{2,1,0:T(8,128)S(1)}, f32[9,8,256]{2,1,0:T(8,128)S(1)}, u32[]{:S(2)}, u32[]{:S(2)}) %collective-permute-start.2) | collective-permute-done | bytes 73760 | tf_op jit(solution)/shard_map/ppermute | solution.py:30
  19.2 1.1 %collective-permute-start.8 = (f32[9,8,256]{2,1,0:T(8,128)S(1)}, f32[9,8,256]{2,1,0:T(8,128)S(1)}, u32[]{:S(2)}, u32[]{:S(2)}) collective-permute-start(f32[9,8,256]{2,1,0:T(8,128)S(1)} %get-tuple-element.31), channel_id=1, source_target_pairs={{0,192},{1,193},{2,194},{3,195},{4,196},{5,197},{6,198},{7,199},{8... | collective-permute-start | bytes 221192 | tf_op jit(solution)/shard_map/ppermute | solution.py:30
  20.3 0.0 collective-permute-done.1.r1
  20.3 0.0 collective-permute-done.3.r3
  20.3 0.6 shard_map.53
  20.9 6.1 %collective-permute-start.5 = (f32[7,8,256]{2,1,0:T(8,128)S(1)}, f32[7,8,256]{2,1,0:T(8,128)S(1)}, u32[]{:S(2)}, u32[]{:S(2)}) collective-permute-start(f32[7,8,256]{2,1,0:T(8,128)S(1)} %get-tuple-element.28), channel_id=1, source_target_pairs={{0,32},{1,33},{2,34},{3,35},{4,36},{5,37},{6,38},{7,39},{8,40},{9,... | collective-permute-start | bytes 172040 | tf_op jit(solution)/shard_map/ppermute | solution.py:30
  26.9 0.0 collective-permute-done.6.r1
  26.9 0.0 collective-permute-done.7.r2
  27.0 0.0 collective-permute-done.8.r3
  27.0 0.6 shard_map.54
  27.5 1.8 %collective-permute-done.5.got = f32[7,8,256]{2,1,0:T(8,128)S(1)} collective-permute-done((f32[7,8,256]{2,1,0:T(8,128)S(1)}, f32[7,8,256]{2,1,0:T(8,128)S(1)}, u32[]{:S(2)}, u32[]{:S(2)}) %collective-permute-start.5) | collective-permute-done | bytes 57376 | tf_op jit(solution)/shard_map/ppermute | solution.py:30
  29.3 0.6 shard_map.55.early
  29.9 1.1 %collective-permute-start.10 = (f32[5,16,256]{2,1,0:T(8,128)S(1)}, f32[5,16,256]{2,1,0:T(8,128)S(1)}, u32[]{:S(2)}, u32[]{:S(2)}) collective-permute-start(f32[5,16,256]{2,1,0:T(8,128)S(1)} %shard_map.55.early), channel_id=1, source_target_pairs={{0,1},{1,0},{2,3},{3,2},{4,5},{5,4},{6,7},{7,6},{8,9},{9,8},{10,11... | collective-permute-start | bytes 245768 | tf_op jit(solution)/shard_map/ppermute | solution.py:30
  31.0 6.1 %collective-permute-start.9 = (f32[6,8,256]{2,1,0:T(8,128)S(1)}, f32[6,8,256]{2,1,0:T(8,128)S(1)}, u32[]{:S(2)}, u32[]{:S(2)}) collective-permute-start(f32[6,8,256]{2,1,0:T(8,128)S(1)} %get-tuple-element.33), channel_id=1, source_target_pairs={{0,32},{1,33},{2,34},{3,35},{4,36},{5,37},{6,38},{7,39},{8,40},{9,... | collective-permute-start | bytes 147464 | tf_op jit(solution)/shard_map/ppermute | solution.py:30
  37.1 2.0 %collective-permute-done.9.got = f32[6,8,256]{2,1,0:T(8,128)S(1)} collective-permute-done((f32[6,8,256]{2,1,0:T(8,128)S(1)}, f32[6,8,256]{2,1,0:T(8,128)S(1)}, u32[]{:S(2)}, u32[]{:S(2)}) %collective-permute-start.9) | collective-permute-done | bytes 49184 | tf_op jit(solution)/shard_map/ppermute | solution.py:30
  39.1 0.5 shard_map.56.late
  39.6 3.8 %collective-permute-start.12 = (f32[3,16,256]{2,1,0:T(8,128)S(1)}, f32[3,16,256]{2,1,0:T(8,128)S(1)}, u32[]{:S(2)}, u32[]{:S(2)}) collective-permute-start(f32[3,16,256]{2,1,0:T(8,128)S(1)} %shard_map.56.late), channel_id=1, source_target_pairs={{1,2},{2,1},{3,4},{4,3},{5,6},{6,5},{7,8},{8,7},{9,10},{10,9},{11,... | collective-permute-start | bytes 147464 | tf_op jit(solution)/shard_map/ppermute | solution.py:30
  43.5 0.0 collective-permute-done.10.mate_early
  43.5 1.9 %collective-permute-start.11 = (f32[8,16,256]{2,1,0:T(8,128)S(1)}, f32[8,16,256]{2,1,0:T(8,128)S(1)}, u32[]{:S(2)}, u32[]{:S(2)}) collective-permute-start(f32[8,16,256]{2,1,0:T(8,128)S(1)} %pad_maximum_fusion), channel_id=1, source_target_pairs={{1,2},{2,1},{3,4},{4,3},{5,6},{6,5},{7,8},{8,7},{9,10},{10,9},{11,... | collective-permute-start | bytes 393224 | tf_op jit(solution)/shard_map/ppermute | solution.py:30
  45.4 0.0 collective-permute-done.12.far_late
  45.5 0.1 collective-permute-start.13
  45.6 1.3 %collective-permute-done.13.mate_late = f32[6,16,256]{2,1,0:T(8,128)S(1)} collective-permute-done((f32[6,16,256]{2,1,0:T(8,128)S(1)}, f32[6,16,256]{2,1,0:T(8,128)S(1)}, u32[]{:S(2)}, u32[]{:S(2)}) %collective-permute-start.13) | collective-permute-done | bytes 98336 | tf_op jit(solution)/shard_map/ppermute | solution.py:30
  46.9 2.9 %collective-permute-done.11.far_early = f32[8,16,256]{2,1,0:T(8,128)S(1)} collective-permute-done((f32[8,16,256]{2,1,0:T(8,128)S(1)}, f32[8,16,256]{2,1,0:T(8,128)S(1)}, u32[]{:S(2)}, u32[]{:S(2)}) %collective-permute-start.11) | collective-permute-done | bytes 131104 | tf_op jit(solution)/shard_map/ppermute | solution.py:30
  49.8 1.4 %shard_map.57 = (f32[4,3,2,8,256]{4,3,2,1,0:T(8,128)S(1)}, f32[8,128]{1,0:T(8,128)S(1)}) custom-call(s32[5]{0:T(128)S(1)} %stack.23.pos, f32[5,16,256]{2,1,0:T(8,128)S(1)} %shard_map.55.early, f32[3,16,256]{2,1,0:T(8,128)S(1)} %shard_map.56.late, f32[5,16,256]{2,1,0:T(8,128)S(1)} %collective-permute-done.10.mate_early, ...), custom_call_target="tpu_custom_call" | custom-call | tf_op jit(solution)/shard_map/pallas_call | solution.py:59
  51.2 14.8 %all_to_all.10 = f32[16,8,128]{2,1,0:T(8,128)S(1)} all-to-all(f32[16,8,128]{2,1,0:T(8,128)S(1)} %broadcast_in_dim.6), channel_id=1, replica_groups=mesh['y'=4,'zh'=2,'x'=4,'zl'=4,'core'=2] {'y','x'}, dimensions={0} | all-to-all | bytes 131072 | tf_op jit(solution)/shard_map/all_to_all | solution.py:362
  66.0 16.6 %all_to_all.11.parts = f32[16,8,128]{2,1,0:T(8,128)S(1)} all-to-all(f32[16,8,128]{2,1,0:T(8,128)S(1)} %broadcast_in_dim.7), channel_id=1, replica_groups=mesh['y'=4,'zh'=2,'x'=4,'zl'=4,'core'=2] {'zh','zl','core'}, dimensions={0} | all-to-all | bytes 131072 | tf_op jit(solution)/shard_map/all_to_all | solution.py:364
  82.6 1.9 %shard_map.58 = (f32[3,2,8,256]{3,2,1,0:T(8,128)}, f32[3,2,8,256]{3,2,1,0:T(8,128)}) custom-call(s32[5]{0:T(128)S(1)} %stack.23.pos, f32[16,8,128]{2,1,0:T(8,128)S(1)} %all_to_all.11.parts, f32[4,3,2,8,256]{4,3,2,1,0:T(8,128)S(1)} %get-tuple-element.35.basis), custom_call_target="tpu_custom_call" | custom-call | tf_op jit(solution)/shard_map/pallas_call | solution.py:59
  (8 shorter events, 0.1 us)
Async XLA Ops:
  1.8 8.4 %collective-permute-start = (bf16[2,5,64,256]{3,2,1,0:T(8,128)(2,1)S(1)}, bf16[2,5,64,256]{3,2,1,0:T(8,128)(2,1)S(1)}, u32[]{:S(2)}, u32[]{:S(2)}) collective-permute-start(bf16[2,5,64,256]{3,2,1,0:T(8,128)(2,1)S(1)} %get-tuple-element.36.a), channel_id=1, source_target_pairs={{0,1},{1,0},{2,3},{3,2},{4,5},{5,4},{6,7},{7,6},{8,9},{9,8},{10,11... | collective-permute-start | bytes 983048 | tf_op jit(solution)/shard_map/ppermute | solution.py:30
  5.1 11.6 %collective-permute-start.4 = (bf16[2,5,64,256]{3,2,1,0:T(8,128)(2,1)S(1)}, bf16[2,5,64,256]{3,2,1,0:T(8,128)(2,1)S(1)}, u32[]{:S(2)}, u32[]{:S(2)}) collective-permute-start(bf16[2,5,64,256]{3,2,1,0:T(8,128)(2,1)S(1)} %get-tuple-element.37.a), channel_id=1, source_target_pairs={{1,2},{2,1},{3,4},{4,3},{5,6},{6,5},{7,8},{8,7},{9,10},{10,9},{11,... | collective-permute-start | bytes 983048 | tf_op jit(solution)/shard_map/ppermute | solution.py:30
  7.1 1.5 %copy-start = (bf16[2,5,3,2,64,256]{5,4,3,2,1,0:T(8,128)(2,1)S(1)}, bf16[2,5,3,2,64,256]{5,4,3,2,1,0:T(8,128)(2,1)}, u32[]{:S(2)}) copy-start(bf16[2,5,3,2,64,256]{5,4,3,2,1,0:T(8,128)(2,1)} %f.1) | copy-start | bytes 5898244
  8.7 0.7 copy-start.1
  11.0 9.3 %collective-permute-start.1 = (f32[11,8,256]{2,1,0:T(8,128)S(1)}, f32[11,8,256]{2,1,0:T(8,128)S(1)}, u32[]{:S(2)}, u32[]{:S(2)}) collective-permute-start(f32[11,8,256]{2,1,0:T(8,128)S(1)} %get-tuple-element.22), channel_id=1, source_target_pairs={{0,64},{1,65},{2,66},{3,67},{4,68},{5,69},{6,70},{7,71},{8,72},{9,... | collective-permute-start | bytes 270344 | tf_op jit(solution)/shard_map/ppermute | solution.py:30
  12.2 8.1 %collective-permute-start.3 = (f32[11,8,256]{2,1,0:T(8,128)S(1)}, f32[11,8,256]{2,1,0:T(8,128)S(1)}, u32[]{:S(2)}, u32[]{:S(2)}) collective-permute-start(f32[11,8,256]{2,1,0:T(8,128)S(1)} %get-tuple-element.24), channel_id=1, source_target_pairs={{0,192},{1,193},{2,194},{3,195},{4,196},{5,197},{6,198},{7,199},{8... | collective-permute-start | bytes 270344 | tf_op jit(solution)/shard_map/ppermute | solution.py:30
  13.7 5.5 %collective-permute-start.2 = (f32[9,8,256]{2,1,0:T(8,128)S(1)}, f32[9,8,256]{2,1,0:T(8,128)S(1)}, u32[]{:S(2)}, u32[]{:S(2)}) collective-permute-start(f32[9,8,256]{2,1,0:T(8,128)S(1)} %get-tuple-element.23), channel_id=1, source_target_pairs={{0,128},{1,129},{2,130},{3,131},{4,132},{5,133},{6,134},{7,135},{8... | collective-permute-start | bytes 221192 | tf_op jit(solution)/shard_map/ppermute | solution.py:30
  17.5 9.4 %collective-permute-start.6 = (f32[9,8,256]{2,1,0:T(8,128)S(1)}, f32[9,8,256]{2,1,0:T(8,128)S(1)}, u32[]{:S(2)}, u32[]{:S(2)}) collective-permute-start(f32[9,8,256]{2,1,0:T(8,128)S(1)} %get-tuple-element.29), channel_id=1, source_target_pairs={{0,64},{1,65},{2,66},{3,67},{4,68},{5,69},{6,70},{7,71},{8,72},{9,... | collective-permute-start | bytes 221192 | tf_op jit(solution)/shard_map/ppermute | solution.py:30
  17.6 9.3 %collective-permute-start.7 = (f32[9,8,256]{2,1,0:T(8,128)S(1)}, f32[9,8,256]{2,1,0:T(8,128)S(1)}, u32[]{:S(2)}, u32[]{:S(2)}) collective-permute-start(f32[9,8,256]{2,1,0:T(8,128)S(1)} %get-tuple-element.30), channel_id=1, source_target_pairs={{0,128},{1,129},{2,130},{3,131},{4,132},{5,133},{6,134},{7,135},{8... | collective-permute-start | bytes 221192 | tf_op jit(solution)/shard_map/ppermute | solution.py:30
  19.2 7.7 %collective-permute-start.8 = (f32[9,8,256]{2,1,0:T(8,128)S(1)}, f32[9,8,256]{2,1,0:T(8,128)S(1)}, u32[]{:S(2)}, u32[]{:S(2)}) collective-permute-start(f32[9,8,256]{2,1,0:T(8,128)S(1)} %get-tuple-element.31), channel_id=1, source_target_pairs={{0,192},{1,193},{2,194},{3,195},{4,196},{5,197},{6,198},{7,199},{8... | collective-permute-start | bytes 221192 | tf_op jit(solution)/shard_map/ppermute | solution.py:30
  20.9 8.4 %collective-permute-start.5 = (f32[7,8,256]{2,1,0:T(8,128)S(1)}, f32[7,8,256]{2,1,0:T(8,128)S(1)}, u32[]{:S(2)}, u32[]{:S(2)}) collective-permute-start(f32[7,8,256]{2,1,0:T(8,128)S(1)} %get-tuple-element.28), channel_id=1, source_target_pairs={{0,32},{1,33},{2,34},{3,35},{4,36},{5,37},{6,38},{7,39},{8,40},{9,... | collective-permute-start | bytes 172040 | tf_op jit(solution)/shard_map/ppermute | solution.py:30
  29.9 13.6 %collective-permute-start.10 = (f32[5,16,256]{2,1,0:T(8,128)S(1)}, f32[5,16,256]{2,1,0:T(8,128)S(1)}, u32[]{:S(2)}, u32[]{:S(2)}) collective-permute-start(f32[5,16,256]{2,1,0:T(8,128)S(1)} %shard_map.55.early), channel_id=1, source_target_pairs={{0,1},{1,0},{2,3},{3,2},{4,5},{5,4},{6,7},{7,6},{8,9},{9,8},{10,11... | collective-permute-start | bytes 245768 | tf_op jit(solution)/shard_map/ppermute | solution.py:30
  31.0 8.1 %collective-permute-start.9 = (f32[6,8,256]{2,1,0:T(8,128)S(1)}, f32[6,8,256]{2,1,0:T(8,128)S(1)}, u32[]{:S(2)}, u32[]{:S(2)}) collective-permute-start(f32[6,8,256]{2,1,0:T(8,128)S(1)} %get-tuple-element.33), channel_id=1, source_target_pairs={{0,32},{1,33},{2,34},{3,35},{4,36},{5,37},{6,38},{7,39},{8,40},{9,... | collective-permute-start | bytes 147464 | tf_op jit(solution)/shard_map/ppermute | solution.py:30
  39.6 5.8 %collective-permute-start.12 = (f32[3,16,256]{2,1,0:T(8,128)S(1)}, f32[3,16,256]{2,1,0:T(8,128)S(1)}, u32[]{:S(2)}, u32[]{:S(2)}) collective-permute-start(f32[3,16,256]{2,1,0:T(8,128)S(1)} %shard_map.56.late), channel_id=1, source_target_pairs={{1,2},{2,1},{3,4},{4,3},{5,6},{6,5},{7,8},{8,7},{9,10},{10,9},{11,... | collective-permute-start | bytes 147464 | tf_op jit(solution)/shard_map/ppermute | solution.py:30
  43.5 6.3 %collective-permute-start.11 = (f32[8,16,256]{2,1,0:T(8,128)S(1)}, f32[8,16,256]{2,1,0:T(8,128)S(1)}, u32[]{:S(2)}, u32[]{:S(2)}) collective-permute-start(f32[8,16,256]{2,1,0:T(8,128)S(1)} %pad_maximum_fusion), channel_id=1, source_target_pairs={{1,2},{2,1},{3,4},{4,3},{5,6},{6,5},{7,8},{8,7},{9,10},{10,9},{11,... | collective-permute-start | bytes 393224 | tf_op jit(solution)/shard_map/ppermute | solution.py:30
  45.5 1.4 %collective-permute-start.13 = (f32[6,16,256]{2,1,0:T(8,128)S(1)}, f32[6,16,256]{2,1,0:T(8,128)S(1)}, u32[]{:S(2)}, u32[]{:S(2)}) collective-permute-start(f32[6,16,256]{2,1,0:T(8,128)S(1)} %pad_maximum_fusion.1), channel_id=1, source_target_pairs={{0,1},{1,0},{2,3},{3,2},{4,5},{5,4},{6,7},{7,6},{8,9},{9,8},{10,11... | collective-permute-start | bytes 294920 | tf_op jit(solution)/shard_map/ppermute | solution.py:30

commit v4 on v3

--- a/solution.py
+++ b/solution.py
@@ -52,36 +52,20 @@
 
 VMEM = pl.BlockSpec(memory_space=pltpu.VMEM)
 SMEM = pl.BlockSpec(memory_space=pltpu.SMEM)
-HBM = pl.BlockSpec(memory_space=pltpu.HBM)
-
-
-def call(kernel, outs, args, scratch=(), specs=None):
+
+
+def call(kernel, outs, args, scratch=()):
     return pl.pallas_call(
         kernel,
-        out_shape=[s if isinstance(s, jax.ShapeDtypeStruct) else jax.ShapeDtypeStruct(s, F32) for s in outs],
-        in_specs=[SMEM] + (specs or [VMEM] * (len(args) - 1)),
+        out_shape=[jax.ShapeDtypeStruct(s, F32) for s in outs],
+        in_specs=[SMEM] + [VMEM] * (len(args) - 1),
         out_specs=[VMEM] * len(outs),
         scratch_shapes=list(scratch),
         compiler_params=pltpu.CompilerParams(vmem_limit_bytes=24 * 1024 * 1024),
     )(*args)
 
 
-def copy_all(pairs, sems):
-    copies = [pltpu.make_async_copy(src, dst, sems.at[n]) for n, (src, dst) in enumerate(pairs)]
-    for copy in copies:
-        copy.start()
-    for copy in copies:
-        copy.wait()
-
-
-def split_flux_kernel(pos, f, shift, late, early, near_shift, sems):
-    core = pos[4]
-    copy_all(
-        [(f.at[:, :, :, 1 - core], early), (f.at[:, :, :, core], late), (shift, near_shift)], sems
-    )
-
-
-def sens_of_slab(y, sign, f, a, got, outs, wide):
+def sens_of_slab(y, slab, sign, f, a, got, outs, wide):
     zero = jnp.zeros((8, 256), F32)
     for k in range(3):
         wide[k, 0:8, :] = zero
@@ -93,7 +77,7 @@
             for v in range(5):
                 step = got[i, v, span, :].astype(F32) - a[i, v, span, :].astype(F32)
                 for k in range(3):
-                    term = f[i, v, k, span, :].astype(F32) * step
+                    term = f[i, v, k, slab, span, :].astype(F32) * step
                     total[k] = term if total[k] is None else total[k] + term
         for k in range(3):
             wide[k, rows + 3 : rows + 19, :] = total[k] * sign
@@ -105,52 +89,45 @@
 
 def sens_early_kernel(pos, f, a, got, shift, m0, m1, m2, m3, wide):
     sign = jnp.where(pos[4] == 0, 1.0, -1.0)
-    sens_of_slab(pos[0], sign, f, a, got, (m0, m1, m2, m3), wide)
+    sens_of_slab(pos[0], 1 - pos[4], sign, f, a, got, (m0, m1, m2, m3), wide)
     for out in (m1, m3):
         out[9:11] = shift[...]
 
 
-def sens_late_kernel(pos, f, a, got, m0, m1, m2, m3, wide):
+def sens_late_kernel(pos, f, a, got, after, m0, m1, m2, m3, wide):
     sign = jnp.where(pos[4] == 0, -1.0, 1.0)
-    sens_of_slab(pos[0], sign, f, a, got, (m0, m1, m2, m3), wide)
-
-
-def sum_y_late_kernel(pos, m0, r1, r2, r3, own, out):
+    sens_of_slab(pos[0], pos[4], sign, f, a, got, (m0, m1, m2, m3), wide)
+
+
+def sum_y_kernel(pos, m0, r1, r2, r3, n0, q1, q2, q3, shift, own, out):
     zh = pos[1]
-    for s in range(3):
-        for g in range(2):
-            for half, to in ((zh, own), (1 - zh, out)):
-                k = s * 3 + half + g
-                to[s * 2 + g] = (m0[k] + r1[k]) + (r2[k] + r3[k])
-
-
-def sum_y_early_kernel(pos, m0, r1, r2, r3, shift, after, own, out):
-    sum_y_late_kernel(pos, m0, r1, r2, r3, own, out)
-    low = pos[1] == 0
+    for first, (p0, p1, p2, p3) in ((0, (m0, r1, r2, r3)), (6, (n0, q1, q2, q3))):
+        for s in range(3):
+            for g in range(2):
+                for half, to in ((zh, own), (1 - zh, out)):
+                    k = s * 3 + half + g
+                    to[first + s * 2 + g] = (p0[k] + p1[k]) + (p2[k] + p3[k])
+    low = zh == 0
     for x in range(2):
         below = jnp.where(low, shift[x, 6:8, :], r1[9 + x, 6:8, :])
         above = jnp.where(low, r3[9 + x, 0:2, :], shift[x, 0:2, :])
-        out[6, x * 4 : x * 4 + 2, :] = below
-        out[6, x * 4 + 2 : x * 4 + 4, :] = above
-
-
-def block_late_kernel(pos, own, got, block):
-    for s in range(3):
+        out[12, x * 4 : x * 4 + 2, :] = below
+        out[12, x * 4 + 2 : x * 4 + 4, :] = above
+
+
+def block_kernel(pos, own, got, shift, block):
+    for s in range(6):
         for g in range(2):
             block[s, g * 8 : g * 8 + 8, :] = own[s * 2 + g] + got[s * 2 + g]
-
-
-def block_early_kernel(pos, own, got, shift, after, block):
-    block_late_kernel(pos, own, got, block)
     for x in range(2):
-        block[3 + x, 0:8, :] = jnp.zeros((8, 256), F32)
-        block[3 + x, 8:16, :] = jnp.zeros((8, 256), F32)
-        block[3 + x, 3:11, :] = shift[x]
-        block[3 + x, 1:3, :] = got[6, x * 4 : x * 4 + 2, :]
-        block[3 + x, 11:13, :] = got[6, x * 4 + 2 : x * 4 + 4, :]
-
-
-def krylov_kernel(pos, early, late, mate_early, far_early, far_late, mate_late, basis, moments, w0, w1, w2, sh):
+        block[6 + x, 0:8, :] = jnp.zeros((8, 256), F32)
+        block[6 + x, 8:16, :] = jnp.zeros((8, 256), F32)
+        block[6 + x, 3:11, :] = shift[x]
+        block[6 + x, 1:3, :] = got[12, x * 4 : x * 4 + 2, :]
+        block[6 + x, 11:13, :] = got[12, x * 4 + 2 : x * 4 + 4, :]
+
+
+def krylov_kernel(pos, block, mate, far, beyond, basis, moments, w0, w1, w2, sh):
     inst, cell, core = pos[2], pos[3], pos[4]
 
     def place(x):
@@ -158,15 +135,15 @@
 
     for k in range(3):
         line = (
-            far_early[3 + k], far_early[k], far_late[k], late[k],
-            early[k], mate_early[k], mate_late[k], mate_late[3 + k],
+            far[8 + k], far[k], far[3 + k], block[3 + k],
+            block[k], mate[k], mate[3 + k], beyond[k],
         )
         for x in range(8):
             w0[k, place(x)] = line[x]
     for x in range(2):
-        sh[1 + core * 4 + x] = far_early[6 + x]
-        sh[3 + x] = early[3 + x]
-        sh[5 - core * 4 + x] = mate_early[3 + x]
+        sh[1 + core * 4 + x] = far[6 + x]
+        sh[3 + x] = block[6 + x]
+        sh[5 - core * 4 + x] = mate[6 + x]
 
     row = lax.broadcasted_iota(jnp.int32, (16, 256), 0) + (inst * 8 - 3)
     lane = lax.broadcasted_iota(jnp.int32, (16, 256), 1)
@@ -252,11 +229,14 @@
 
 
 def finish_kernel(pos, parts, basis, mesh_adjoint, residual):
-    high = parts[0]
-    low = jnp.zeros((8, 128), F32)
-    for n in range(1, parts.shape[0]):
-        high, error = two_sum(high, parts[n])
-        low = low + error
+    sums = [(parts[n], None) for n in range(parts.shape[0])]
+    while len(sums) > 1:
+        pairs = []
+        for (p, rest), (q, more_rest) in zip(sums[::2], sums[1::2]):
+            high, low = two_sum(p, q)
+            pairs.append((high, low if rest is None else low + (rest + more_rest)))
+        sums = pairs
+    high, low = sums[0]
     for step in (64, 32, 16, 8, 4, 2, 1):
         high, error = two_sum(high, pltpu.roll(high, step, 1))
         low = (low + pltpu.roll(low, step, 1)) + error
@@ -316,47 +296,35 @@
     core = lax.axis_index("core")
     pos = jnp.stack([y, zh, inst, cell, core]).astype(jnp.int32)
 
-    slab_flux = jax.ShapeDtypeStruct((2, 5, 3, 64, 256), jnp.bfloat16)
     outer = lax.dynamic_index_in_dim(adjoint, core, 2, False)
     inner = lax.dynamic_index_in_dim(adjoint, 1 - core, 2, False)
     got_outer = send_pair(outer)
     got_inner = send_core(inner)
-    flux_late, flux_early, shift = call(
-        split_flux_kernel,
-        [slab_flux, slab_flux, (2, 8, 256)],
-        (pos, flux_jac, shift),
-        [pltpu.SemaphoreType.DMA((3,))],
-        [HBM, HBM],
-    )
 
     nine, eleven = (9, 8, 256), (11, 8, 256)
     wide = [pltpu.VMEM((3, 72, 256), F32)]
     m0, m1, m2, m3 = call(
         sens_early_kernel,
         [nine, eleven, nine, eleven],
-        (pos, flux_early, outer, got_inner, shift),
+        (pos, flux_jac, outer, got_inner, shift),
         wide,
     )
     r2, r1, r3 = send_y(m2, 2), send_y(m1, 1), send_y(m3, 3)
-    n0, n1, n2, n3 = call(sens_late_kernel, [nine] * 4, (pos, flux_late, inner, got_outer), wide)
+    n0, n1, n2, n3 = call(sens_late_kernel, [nine] * 4, (pos, flux_jac, inner, got_outer, m0), wide)
     q2, q1, q3 = send_y(n2, 2), send_y(n1, 1), send_y(n3, 3)
-    six, seven = (6, 8, 256), (7, 8, 256)
-    own, out = call(sum_y_early_kernel, [six, seven], (pos, m0, r1, r2, r3, shift, n0))
-    got = send_zh(out)
-    own_late, out_late = call(sum_y_late_kernel, [six, six], (pos, n0, q1, q2, q3))
-    got_late = send_zh(out_late)
-    (early,) = call(block_early_kernel, [(5, 16, 256)], (pos, own, got, shift, own_late))
-    mate_early = send_core(early)
-    far_early = send_pair(jnp.concatenate([early[:3], mate_early[:3], early[3:]], axis=0))
-    (late,) = call(block_late_kernel, [(3, 16, 256)], (pos, own_late, got_late))
-    far_late = send_pair(late)
-    mate_late = send_core(jnp.concatenate([late, far_late], axis=0))
+    own, out = call(
+        sum_y_kernel, [(12, 8, 256), (13, 8, 256)], (pos, m0, r1, r2, r3, n0, q1, q2, q3, shift)
+    )
+    (block,) = call(block_kernel, [(8, 16, 256)], (pos, own, send_zh(out), shift))
+    mate = send_core(block)
+    far = send_pair(jnp.concatenate([block, mate[:3]], axis=0))
+    beyond = send_core(far[3:6])
 
     scratch = pltpu.VMEM((3, 8, 16, 256), F32)
     basis, moments = call(
         krylov_kernel,
         [(4, 3, 2, 8, 256), (8, 128)],
-        (pos, early, late, mate_early, far_early, far_late, mate_late),
+        (pos, block, mate, far, beyond),
         [scratch, scratch, scratch, pltpu.VMEM((8, 16, 256), F32)],
     )
     parts = lax.all_to_all(jnp.broadcast_to(moments, (16, 8, 128)), ("y", "x"), 0, 0)

time: 84.8 us -> 82.2 us (0.969)
  starting transfers between devices: 30.2 us -> 24.8 us
  waiting for transfers between devices: 10.6 us -> 14 us
  Pallas kernels: 7.94 us -> 6.08 us
  blocking collectives: 31.4 us -> 32.8 us
    ppermute x14 -> x12, starting transfers between devices: 30.2 us -> 24.8 us  [send(): return lax.ppermute(v, AXES, pairs)]
    ppermute x14 -> x12, waiting for transfers between devices: 10.6 us -> 14 us  [send(): return lax.ppermute(v, AXES, pairs)]
    all_to_all x1, blocking collectives: 14.8 us -> 17.2 us  [local(): lax.all_to_all(jnp.broadcast_to(moments, (16, 8, 128)), ('y', 'x'), 0, 0)]
    pallas_call x9 -> x6, Pallas kernels: 7.94 us -> 6.08 us  [call(): pl.pallas_call(kernel, out_shape=[jax.ShapeDtypeStruct(s, F32) for s in o...]
    all_to_all x1, blocking collectives: 16.6 us -> 15.6 us  [local(): lax.all_to_all(jnp.broadcast_to(moments, (16, 8, 128)), ('zh', 'zl', 'cor...]
  transfers between devices with their start and end apart: 14 -> 12, of which waited for: 6 -> 7; matrix products, arithmetic and copies ran while one was open for 0% -> 0% of each run, Pallas kernels for 5% -> 2%
where the time goes in v4:
time: 82.2 us; the launch traced here: 81.9 us
  blocking collectives  32.8 us (40%)
  starting transfers between devices  24.8 us (30%)
  waiting for transfers between devices  14 us (17%)
  Pallas kernels  6.08 us (7%)
  local copies, waits for them, and re-layouts  3.5 us (4%)
    ppermute x12, starting transfers between devices, send(): return lax.ppermute(v, AXES, pairs)  24.8 us
    all_to_all x1, blocking collectives, local(): lax.all_to_all(jnp.broadcast_to(moments, (16, 8, 128)), ('y', 'x'), 0, 0)  17.2 us
    all_to_all x1, blocking collectives, local(): lax.all_to_all(jnp.broadcast_to(moments, (16, 8, 128)), ('zh', 'zl', 'cor...  15.6 us
    ppermute x12, waiting for transfers between devices, send(): return lax.ppermute(v, AXES, pairs)  14 us
    pallas_call x6, Pallas kernels, call(): pl.pallas_call(kernel, out_shape=[jax.ShapeDtypeStruct(s, F32) for s in o...  6.08 us
    unnamed x4, local copies, waits for them, and re-layouts  2.26 us
  transfers between devices with their start and end apart: 12, of which 7 were waited for; matrix products, arithmetic and copies ran while one was open for 0% of the time, Pallas kernels for 2%

profile of v4, /device:TPU:1, one launch (start us, length us, event | category | flops | bytes accessed | tf_op | source)
XLA Modules:
  0.0 81.9 jit_solution(11479387288033105448)
XLA Ops:
  0.6 1.1 %dynamic-slice_bitcast_fusion = (bf16[2,5,64,256]{3,2,1,0:T(8,128)(2,1)S(1)}, bf16[2,5,64,256]{3,2,1,0:T(8,128)(2,1)S(1)}) fusion(bf16[2,5,2,64,256]{4,3,2,1,0:T(8,128)(2,1)} %param.3, s32[]{:T(128)S(6)} %select_n.8, s32[]{:T(128)S(6)} %select_n.7), kind=kLoop, calls=%fused_computation | loop fusion | bytes 1310728 | tf_op jit(solution)/shard_map/jit(dynamic_index_in_dim)/squeeze | solution.py:300
  1.8 3.3 %collective-permute-start = (bf16[2,5,64,256]{3,2,1,0:T(8,128)(2,1)S(1)}, bf16[2,5,64,256]{3,2,1,0:T(8,128)(2,1)S(1)}, u32[]{:S(2)}, u32[]{:S(2)}) collective-permute-start(bf16[2,5,64,256]{3,2,1,0:T(8,128)(2,1)S(1)} %get-tuple-element.26.a), channel_id=1, source_target_pairs={{0,1},{1,0},{2,3},{3,2},{4,5},{5,4},{6,7},{7,6},{8,9},{9,8},{10,11... | collective-permute-start | bytes 983048 | tf_op jit(solution)/shard_map/ppermute | solution.py:30
  5.1 1.9 %collective-permute-start.4 = (bf16[2,5,64,256]{3,2,1,0:T(8,128)(2,1)S(1)}, bf16[2,5,64,256]{3,2,1,0:T(8,128)(2,1)S(1)}, u32[]{:S(2)}, u32[]{:S(2)}) collective-permute-start(bf16[2,5,64,256]{3,2,1,0:T(8,128)(2,1)S(1)} %get-tuple-element.27.a), channel_id=1, source_target_pairs={{1,2},{2,1},{3,4},{4,3},{5,6},{6,5},{7,8},{8,7},{9,10},{10,9},{11,... | collective-permute-start | bytes 983048 | tf_op jit(solution)/shard_map/ppermute | solution.py:30
  7.0 0.1 stack.23.pos
  7.1 0.0 collective-permute-done.got
  7.1 0.0 copy-start
  7.1 1.5 %copy-done = bf16[2,5,3,2,64,256]{5,4,3,2,1,0:T(8,128)(2,1)S(1)} copy-done((bf16[2,5,3,2,64,256]{5,4,3,2,1,0:T(8,128)(2,1)S(1)}, bf16[2,5,3,2,64,256]{5,4,3,2,1,0:T(8,128)(2,1)}, u32[]{:S(2)}) %copy-start) | copy-done | bytes 1966104
  8.7 0.0 copy-start.1
  8.7 0.7 copy-done.1
  9.4 0.8 %shard_map.50 = (f32[9,8,256]{2,1,0:T(8,128)S(1)}, f32[11,8,256]{2,1,0:T(8,128)S(1)}, f32[9,8,256]{2,1,0:T(8,128)S(1)}, f32[11,8,256]{2,1,0:T(8,128)S(1)}) custom-call(s32[5]{0:T(128)S(1)} %stack.23.pos, bf16[2,5,3,2,64,256]{5,4,3,2,1,0:T(8,128)(2,1)S(1)} %copy-done, bf16[2,5,64,256]{3,2,1,0:T(8,128)(2,1)S(1)} %get-tuple-element.27.a, ...), custom_call_target="tpu_custom_call" | custom-call | tf_op jit(solution)/shard_map/pallas_call | solution.py:58
  10.2 2.8 %collective-permute-start.2 = (f32[9,8,256]{2,1,0:T(8,128)S(1)}, f32[9,8,256]{2,1,0:T(8,128)S(1)}, u32[]{:S(2)}, u32[]{:S(2)}) collective-permute-start(f32[9,8,256]{2,1,0:T(8,128)S(1)} %get-tuple-element.16), channel_id=1, source_target_pairs={{0,128},{1,129},{2,130},{3,131},{4,132},{5,133},{6,134},{7,135},{8... | collective-permute-start | bytes 221192 | tf_op jit(solution)/shard_map/ppermute | solution.py:30
  13.0 0.4 collective-permute-start.1
  13.4 2.3 %collective-permute-start.3 = (f32[11,8,256]{2,1,0:T(8,128)S(1)}, f32[11,8,256]{2,1,0:T(8,128)S(1)}, u32[]{:S(2)}, u32[]{:S(2)}) collective-permute-start(f32[11,8,256]{2,1,0:T(8,128)S(1)} %get-tuple-element.17), channel_id=1, source_target_pairs={{0,192},{1,193},{2,194},{3,195},{4,196},{5,197},{6,198},{7,199},{8... | collective-permute-start | bytes 270344 | tf_op jit(solution)/shard_map/ppermute | solution.py:30
  15.7 1.3 %collective-permute-done.4.got = bf16[2,5,64,256]{3,2,1,0:T(8,128)(2,1)S(1)} collective-permute-done((bf16[2,5,64,256]{3,2,1,0:T(8,128)(2,1)S(1)}, bf16[2,5,64,256]{3,2,1,0:T(8,128)(2,1)S(1)}, u32[]{:S(2)}, u32[]{:S(2)}) %collective-permute-start.4) | collective-permute-done | bytes 327712 | tf_op jit(solution)/shard_map/ppermute | solution.py:30
  17.0 0.8 %shard_map.51 = (f32[9,8,256]{2,1,0:T(8,128)S(1)}, f32[9,8,256]{2,1,0:T(8,128)S(1)}, f32[9,8,256]{2,1,0:T(8,128)S(1)}, f32[9,8,256]{2,1,0:T(8,128)S(1)}) custom-call(s32[5]{0:T(128)S(1)} %stack.23.pos, bf16[2,5,3,2,64,256]{5,4,3,2,1,0:T(8,128)(2,1)S(1)} %copy-done, bf16[2,5,64,256]{3,2,1,0:T(8,128)(2,1)S(1)} %get-tuple-element.26.a, ...), custom_call_target="tpu_custom_call" | custom-call | tf_op jit(solution)/shard_map/pallas_call | solution.py:58
  17.8 0.1 collective-permute-start.5
  17.9 0.4 collective-permute-start.6
  18.4 0.0 collective-permute-done.2.r2
  18.4 2.2 %collective-permute-start.7 = (f32[9,8,256]{2,1,0:T(8,128)S(1)}, f32[9,8,256]{2,1,0:T(8,128)S(1)}, u32[]{:S(2)}, u32[]{:S(2)}) collective-permute-start(f32[9,8,256]{2,1,0:T(8,128)S(1)} %get-tuple-element.21), channel_id=1, source_target_pairs={{0,192},{1,193},{2,194},{3,195},{4,196},{5,197},{6,198},{7,199},{8... | collective-permute-start | bytes 221192 | tf_op jit(solution)/shard_map/ppermute | solution.py:30
  20.6 2.5 %collective-permute-done.5.q1 = f32[9,8,256]{2,1,0:T(8,128)S(1)} collective-permute-done((f32[9,8,256]{2,1,0:T(8,128)S(1)}, f32[9,8,256]{2,1,0:T(8,128)S(1)}, u32[]{:S(2)}, u32[]{:S(2)}) %collective-permute-start.5) | collective-permute-done | bytes 73760 | tf_op jit(solution)/shard_map/ppermute | solution.py:30
  23.1 0.0 collective-permute-done.6.q2
  23.1 0.6 collective-permute-done.7.q3
  23.7 0.0 collective-permute-done.1.r1
  23.7 0.0 collective-permute-done.3.r3
  23.7 0.6 shard_map.52
  24.3 6.2 %collective-permute-start.8 = (f32[13,8,256]{2,1,0:T(8,128)S(1)}, f32[13,8,256]{2,1,0:T(8,128)S(1)}, u32[]{:S(2)}, u32[]{:S(2)}) collective-permute-start(f32[13,8,256]{2,1,0:T(8,128)S(1)} %get-tuple-element.23), channel_id=1, source_target_pairs={{0,32},{1,33},{2,34},{3,35},{4,36},{5,37},{6,38},{7,39},{8,40},{9,... | collective-permute-start | bytes 319496 | tf_op jit(solution)/shard_map/ppermute | solution.py:30
  30.5 2.5 %collective-permute-done.8.got = f32[13,8,256]{2,1,0:T(8,128)S(1)} collective-permute-done((f32[13,8,256]{2,1,0:T(8,128)S(1)}, f32[13,8,256]{2,1,0:T(8,128)S(1)}, u32[]{:S(2)}, u32[]{:S(2)}) %collective-permute-start.8) | collective-permute-done | bytes 106528 | tf_op jit(solution)/shard_map/ppermute | solution.py:30
  33.0 0.6 shard_map.53.block
  33.6 3.2 %collective-permute-start.9 = (f32[8,16,256]{2,1,0:T(8,128)S(1)}, f32[8,16,256]{2,1,0:T(8,128)S(1)}, u32[]{:S(2)}, u32[]{:S(2)}) collective-permute-start(f32[8,16,256]{2,1,0:T(8,128)S(1)} %shard_map.53.block), channel_id=1, source_target_pairs={{0,1},{1,0},{2,3},{3,2},{4,5},{5,4},{6,7},{7,6},{8,9},{9,8},{10,11... | collective-permute-start | bytes 393224 | tf_op jit(solution)/shard_map/ppermute | solution.py:30
  36.8 1.0 %collective-permute-done.9.mate = f32[8,16,256]{2,1,0:T(8,128)S(1)} collective-permute-done((f32[8,16,256]{2,1,0:T(8,128)S(1)}, f32[8,16,256]{2,1,0:T(8,128)S(1)}, u32[]{:S(2)}, u32[]{:S(2)}) %collective-permute-start.9) | collective-permute-done | bytes 131104 | tf_op jit(solution)/shard_map/ppermute | solution.py:30
  37.8 1.9 %collective-permute-start.10 = (f32[11,16,256]{2,1,0:T(8,128)S(1)}, f32[11,16,256]{2,1,0:T(8,128)S(1)}, u32[]{:S(2)}, u32[]{:S(2)}) collective-permute-start(f32[11,16,256]{2,1,0:T(8,128)S(1)} %pad_maximum_fusion), channel_id=1, source_target_pairs={{1,2},{2,1},{3,4},{4,3},{5,6},{6,5},{7,8},{8,7},{9,10},{10,9},{11,... | collective-permute-start | bytes 540680 | tf_op jit(solution)/shard_map/ppermute | solution.py:30
  39.7 4.9 %collective-permute-done.10.far = f32[11,16,256]{2,1,0:T(8,128)S(1)} collective-permute-done((f32[11,16,256]{2,1,0:T(8,128)S(1)}, f32[11,16,256]{2,1,0:T(8,128)S(1)}, u32[]{:S(2)}, u32[]{:S(2)}) %collective-permute-start.10) | collective-permute-done | bytes 180256 | tf_op jit(solution)/shard_map/ppermute | solution.py:30
  44.6 0.0 collective-permute-start.11
  44.6 1.2 %collective-permute-done.11.beyond = f32[3,16,256]{2,1,0:T(8,128)S(1)} collective-permute-done((f32[3,16,256]{2,1,0:T(8,128)S(1)}, f32[3,16,256]{2,1,0:T(8,128)S(1)}, u32[]{:S(2)}, u32[]{:S(2)}) %collective-permute-start.11) | collective-permute-done | bytes 49184 | tf_op jit(solution)/shard_map/ppermute | solution.py:30
  45.8 1.4 %shard_map.54 = (f32[4,3,2,8,256]{4,3,2,1,0:T(8,128)S(1)}, f32[8,128]{1,0:T(8,128)S(1)}) custom-call(s32[5]{0:T(128)S(1)} %stack.23.pos, f32[8,16,256]{2,1,0:T(8,128)S(1)} %shard_map.53.block, f32[8,16,256]{2,1,0:T(8,128)S(1)} %collective-permute-done.9.mate, f32[11,16,256]{2,1,0:T(8,128)S(1)} %collective-permute-done.10.far, ...), custom_call_target="tpu_custom_call" | custom-call | tf_op jit(solution)/shard_map/pallas_call | solution.py:58
  47.2 17.2 %all_to_all.10 = f32[16,8,128]{2,1,0:T(8,128)S(1)} all-to-all(f32[16,8,128]{2,1,0:T(8,128)S(1)} %broadcast_in_dim.6), channel_id=1, replica_groups=mesh['y'=4,'zh'=2,'x'=4,'zl'=4,'core'=2] {'y','x'}, dimensions={0} | all-to-all | bytes 131072 | tf_op jit(solution)/shard_map/all_to_all | solution.py:330
  64.4 15.6 %all_to_all.11.parts = f32[16,8,128]{2,1,0:T(8,128)S(1)} all-to-all(f32[16,8,128]{2,1,0:T(8,128)S(1)} %broadcast_in_dim.7), channel_id=1, replica_groups=mesh['y'=4,'zh'=2,'x'=4,'zl'=4,'core'=2] {'zh','zl','core'}, dimensions={0} | all-to-all | bytes 131072 | tf_op jit(solution)/shard_map/all_to_all | solution.py:332
  80.1 1.9 %shard_map.55 = (f32[3,2,8,256]{3,2,1,0:T(8,128)}, f32[3,2,8,256]{3,2,1,0:T(8,128)}) custom-call(s32[5]{0:T(128)S(1)} %stack.23.pos, f32[16,8,128]{2,1,0:T(8,128)S(1)} %all_to_all.11.parts, f32[4,3,2,8,256]{4,3,2,1,0:T(8,128)S(1)} %get-tuple-element.25.basis), custom_call_target="tpu_custom_call" | custom-call | tf_op jit(solution)/shard_map/pallas_call | solution.py:58
  (6 shorter events, 0.1 us)
Async XLA Ops:
  1.8 5.3 %collective-permute-start = (bf16[2,5,64,256]{3,2,1,0:T(8,128)(2,1)S(1)}, bf16[2,5,64,256]{3,2,1,0:T(8,128)(2,1)S(1)}, u32[]{:S(2)}, u32[]{:S(2)}) collective-permute-start(bf16[2,5,64,256]{3,2,1,0:T(8,128)(2,1)S(1)} %get-tuple-element.26.a), channel_id=1, source_target_pairs={{0,1},{1,0},{2,3},{3,2},{4,5},{5,4},{6,7},{7,6},{8,9},{9,8},{10,11... | collective-permute-start | bytes 983048 | tf_op jit(solution)/shard_map/ppermute | solution.py:30
  5.1 11.9 %collective-permute-start.4 = (bf16[2,5,64,256]{3,2,1,0:T(8,128)(2,1)S(1)}, bf16[2,5,64,256]{3,2,1,0:T(8,128)(2,1)S(1)}, u32[]{:S(2)}, u32[]{:S(2)}) collective-permute-start(bf16[2,5,64,256]{3,2,1,0:T(8,128)(2,1)S(1)} %get-tuple-element.27.a), channel_id=1, source_target_pairs={{1,2},{2,1},{3,4},{4,3},{5,6},{6,5},{7,8},{8,7},{9,10},{10,9},{11,... | collective-permute-start | bytes 983048 | tf_op jit(solution)/shard_map/ppermute | solution.py:30
  7.1 1.5 %copy-start = (bf16[2,5,3,2,64,256]{5,4,3,2,1,0:T(8,128)(2,1)S(1)}, bf16[2,5,3,2,64,256]{5,4,3,2,1,0:T(8,128)(2,1)}, u32[]{:S(2)}) copy-start(bf16[2,5,3,2,64,256]{5,4,3,2,1,0:T(8,128)(2,1)} %f.3) | copy-start | bytes 5898244
  8.7 0.7 copy-start.1
  10.2 8.1 %collective-permute-start.2 = (f32[9,8,256]{2,1,0:T(8,128)S(1)}, f32[9,8,256]{2,1,0:T(8,128)S(1)}, u32[]{:S(2)}, u32[]{:S(2)}) collective-permute-start(f32[9,8,256]{2,1,0:T(8,128)S(1)} %get-tuple-element.16), channel_id=1, source_target_pairs={{0,128},{1,129},{2,130},{3,131},{4,132},{5,133},{6,134},{7,135},{8... | collective-permute-start | bytes 221192 | tf_op jit(solution)/shard_map/ppermute | solution.py:30
  13.0 10.7 %collective-permute-start.1 = (f32[11,8,256]{2,1,0:T(8,128)S(1)}, f32[11,8,256]{2,1,0:T(8,128)S(1)}, u32[]{:S(2)}, u32[]{:S(2)}) collective-permute-start(f32[11,8,256]{2,1,0:T(8,128)S(1)} %get-tuple-element.15), channel_id=1, source_target_pairs={{0,64},{1,65},{2,66},{3,67},{4,68},{5,69},{6,70},{7,71},{8,72},{9,... | collective-permute-start | bytes 270344 | tf_op jit(solution)/shard_map/ppermute | solution.py:30
  13.4 10.3 %collective-permute-start.3 = (f32[11,8,256]{2,1,0:T(8,128)S(1)}, f32[11,8,256]{2,1,0:T(8,128)S(1)}, u32[]{:S(2)}, u32[]{:S(2)}) collective-permute-start(f32[11,8,256]{2,1,0:T(8,128)S(1)} %get-tuple-element.17), channel_id=1, source_target_pairs={{0,192},{1,193},{2,194},{3,195},{4,196},{5,197},{6,198},{7,199},{8... | collective-permute-start | bytes 270344 | tf_op jit(solution)/shard_map/ppermute | solution.py:30
  17.8 5.3 %collective-permute-start.5 = (f32[9,8,256]{2,1,0:T(8,128)S(1)}, f32[9,8,256]{2,1,0:T(8,128)S(1)}, u32[]{:S(2)}, u32[]{:S(2)}) collective-permute-start(f32[9,8,256]{2,1,0:T(8,128)S(1)} %get-tuple-element.19), channel_id=1, source_target_pairs={{0,64},{1,65},{2,66},{3,67},{4,68},{5,69},{6,70},{7,71},{8,72},{9,... | collective-permute-start | bytes 221192 | tf_op jit(solution)/shard_map/ppermute | solution.py:30
  17.9 5.2 %collective-permute-start.6 = (f32[9,8,256]{2,1,0:T(8,128)S(1)}, f32[9,8,256]{2,1,0:T(8,128)S(1)}, u32[]{:S(2)}, u32[]{:S(2)}) collective-permute-start(f32[9,8,256]{2,1,0:T(8,128)S(1)} %get-tuple-element.20), channel_id=1, source_target_pairs={{0,128},{1,129},{2,130},{3,131},{4,132},{5,133},{6,134},{7,135},{8... | collective-permute-start | bytes 221192 | tf_op jit(solution)/shard_map/ppermute | solution.py:30
  18.4 5.3 %collective-permute-start.7 = (f32[9,8,256]{2,1,0:T(8,128)S(1)}, f32[9,8,256]{2,1,0:T(8,128)S(1)}, u32[]{:S(2)}, u32[]{:S(2)}) collective-permute-start(f32[9,8,256]{2,1,0:T(8,128)S(1)} %get-tuple-element.21), channel_id=1, source_target_pairs={{0,192},{1,193},{2,194},{3,195},{4,196},{5,197},{6,198},{7,199},{8... | collective-permute-start | bytes 221192 | tf_op jit(solution)/shard_map/ppermute | solution.py:30
  24.3 8.7 %collective-permute-start.8 = (f32[13,8,256]{2,1,0:T(8,128)S(1)}, f32[13,8,256]{2,1,0:T(8,128)S(1)}, u32[]{:S(2)}, u32[]{:S(2)}) collective-permute-start(f32[13,8,256]{2,1,0:T(8,128)S(1)} %get-tuple-element.23), channel_id=1, source_target_pairs={{0,32},{1,33},{2,34},{3,35},{4,36},{5,37},{6,38},{7,39},{8,40},{9,... | collective-permute-start | bytes 319496 | tf_op jit(solution)/shard_map/ppermute | solution.py:30
  33.6 4.2 %collective-permute-start.9 = (f32[8,16,256]{2,1,0:T(8,128)S(1)}, f32[8,16,256]{2,1,0:T(8,128)S(1)}, u32[]{:S(2)}, u32[]{:S(2)}) collective-permute-start(f32[8,16,256]{2,1,0:T(8,128)S(1)} %shard_map.53.block), channel_id=1, source_target_pairs={{0,1},{1,0},{2,3},{3,2},{4,5},{5,4},{6,7},{7,6},{8,9},{9,8},{10,11... | collective-permute-start | bytes 393224 | tf_op jit(solution)/shard_map/ppermute | solution.py:30
  37.8 6.8 %collective-permute-start.10 = (f32[11,16,256]{2,1,0:T(8,128)S(1)}, f32[11,16,256]{2,1,0:T(8,128)S(1)}, u32[]{:S(2)}, u32[]{:S(2)}) collective-permute-start(f32[11,16,256]{2,1,0:T(8,128)S(1)} %pad_maximum_fusion), channel_id=1, source_target_pairs={{1,2},{2,1},{3,4},{4,3},{5,6},{6,5},{7,8},{8,7},{9,10},{10,9},{11,... | collective-permute-start | bytes 540680 | tf_op jit(solution)/shard_map/ppermute | solution.py:30
  44.6 1.2 %collective-permute-start.11 = (f32[3,16,256]{2,1,0:T(8,128)S(1)}, f32[3,16,256]{2,1,0:T(8,128)S(1)}, u32[]{:S(2)}, u32[]{:S(2)}) collective-permute-start(f32[3,16,256]{2,1,0:T(8,128)S(1)} %slice.9), channel_id=1, source_target_pairs={{0,1},{1,0},{2,3},{3,2},{4,5},{5,4},{6,7},{7,6},{8,9},{9,8},{10,11... | collective-permute-start | bytes 147464 | tf_op jit(solution)/shard_map/ppermute | solution.py:30

commit v5 on v4

--- a/solution.py
+++ b/solution.py
@@ -51,21 +51,20 @@
 
 
 VMEM = pl.BlockSpec(memory_space=pltpu.VMEM)
-SMEM = pl.BlockSpec(memory_space=pltpu.SMEM)
 
 
 def call(kernel, outs, args, scratch=()):
     return pl.pallas_call(
         kernel,
         out_shape=[jax.ShapeDtypeStruct(s, F32) for s in outs],
-        in_specs=[SMEM] + [VMEM] * (len(args) - 1),
+        in_specs=[VMEM] * len(args),
         out_specs=[VMEM] * len(outs),
         scratch_shapes=list(scratch),
         compiler_params=pltpu.CompilerParams(vmem_limit_bytes=24 * 1024 * 1024),
     )(*args)
 
 
-def sens_of_slab(y, slab, sign, f, a, got, outs, wide):
+def sens_of_slab(slab, sign, f, a, got, wide):
     zero = jnp.zeros((8, 256), F32)
     for k in range(3):
         wide[k, 0:8, :] = zero
@@ -81,54 +80,44 @@
                     total[k] = term if total[k] is None else total[k] + term
         for k in range(3):
             wide[k, rows + 3 : rows + 19, :] = total[k] * sign
-    for d, out in enumerate(outs):
+
+
+def sens_early_kernel(f, a, got, wide):
+    core = lax.axis_index("core")
+    sens_of_slab(1 - core, jnp.where(core == 0, 1.0, -1.0), f, a, got, wide)
+
+
+def sens_late_kernel(f, a, got, early, shift, m0, m1, m2, m3, wide):
+    y, core = lax.axis_index("y"), lax.axis_index("core")
+    sens_of_slab(core, jnp.where(core == 0, -1.0, 1.0), f, a, got, wide)
+    for d, out in enumerate((m0, m1, m2, m3)):
         first = pl.multiple_of(lax.rem(y + d, 4) * 16, 16)
         for k in range(3):
-            out[k * 3 : k * 3 + 3] = wide[k, pl.ds(first, 24), :].reshape(3, 8, 256)
-
-
-def sens_early_kernel(pos, f, a, got, shift, m0, m1, m2, m3, wide):
-    sign = jnp.where(pos[4] == 0, 1.0, -1.0)
-    sens_of_slab(pos[0], 1 - pos[4], sign, f, a, got, (m0, m1, m2, m3), wide)
+            out[k * 3 : k * 3 + 3] = early[k, pl.ds(first, 24), :].reshape(3, 8, 256)
+            out[9 + k * 3 : 12 + k * 3] = wide[k, pl.ds(first, 24), :].reshape(3, 8, 256)
     for out in (m1, m3):
-        out[9:11] = shift[...]
-
-
-def sens_late_kernel(pos, f, a, got, after, m0, m1, m2, m3, wide):
-    sign = jnp.where(pos[4] == 0, -1.0, 1.0)
-    sens_of_slab(pos[0], pos[4], sign, f, a, got, (m0, m1, m2, m3), wide)
-
-
-def sum_y_kernel(pos, m0, r1, r2, r3, n0, q1, q2, q3, shift, own, out):
-    zh = pos[1]
-    for first, (p0, p1, p2, p3) in ((0, (m0, r1, r2, r3)), (6, (n0, q1, q2, q3))):
-        for s in range(3):
-            for g in range(2):
-                for half, to in ((zh, own), (1 - zh, out)):
-                    k = s * 3 + half + g
-                    to[first + s * 2 + g] = (p0[k] + p1[k]) + (p2[k] + p3[k])
+        out[18:20] = shift[...]
+
+
+def sum_y_kernel(m0, r1, r2, r3, shift, own, out):
+    zh = lax.axis_index("zh")
+    for s in range(6):
+        for g in range(2):
+            for half, to in ((zh, own), (1 - zh, out)):
+                k = s * 3 + half + g
+                to[s * 2 + g] = (m0[k] + r1[k]) + (r2[k] + r3[k])
     low = zh == 0
     for x in range(2):
-        below = jnp.where(low, shift[x, 6:8, :], r1[9 + x, 6:8, :])
-        above = jnp.where(low, r3[9 + x, 0:2, :], shift[x, 0:2, :])
+        below = jnp.where(low, shift[x, 6:8, :], r1[18 + x, 6:8, :])
+        above = jnp.where(low, r3[18 + x, 0:2, :], shift[x, 0:2, :])
         out[12, x * 4 : x * 4 + 2, :] = below
         out[12, x * 4 + 2 : x * 4 + 4, :] = above
 
 
-def block_kernel(pos, own, got, shift, block):
-    for s in range(6):
-        for g in range(2):
-            block[s, g * 8 : g * 8 + 8, :] = own[s * 2 + g] + got[s * 2 + g]
-    for x in range(2):
-        block[6 + x, 0:8, :] = jnp.zeros((8, 256), F32)
-        block[6 + x, 8:16, :] = jnp.zeros((8, 256), F32)
-        block[6 + x, 3:11, :] = shift[x]
-        block[6 + x, 1:3, :] = got[12, x * 4 : x * 4 + 2, :]
-        block[6 + x, 11:13, :] = got[12, x * 4 + 2 : x * 4 + 4, :]
-
-
-def krylov_kernel(pos, block, mate, far, beyond, basis, moments, w0, w1, w2, sh):
-    inst, cell, core = pos[2], pos[3], pos[4]
+def krylov_kernel(block, mate, far, beyond, basis, moments, w0, w1, w2, sh):
+    core = lax.axis_index("core")
+    inst = lax.axis_index("y") * 2 + lax.axis_index("zh")
+    cell = lax.axis_index("x") * 8 + lax.axis_index("zl") * 2 + core
 
     def place(x):
         return x + core * (7 - 2 * x)
@@ -228,7 +217,7 @@
     return p, ((ah * bh - p) + ah * bl + al * bh) + al * bl
 
 
-def finish_kernel(pos, parts, basis, mesh_adjoint, residual):
+def finish_kernel(parts, basis, mesh_adjoint, residual):
     sums = [(parts[n], None) for n in range(parts.shape[0])]
     while len(sums) > 1:
         pairs = []
@@ -290,32 +279,28 @@
 
 
 def local(adjoint, flux_jac, shift):
-    y, zh = lax.axis_index("y"), lax.axis_index("zh")
-    inst = lax.axis_index(("y", "zh"))
-    cell = lax.axis_index(("x", "zl", "core"))
     core = lax.axis_index("core")
-    pos = jnp.stack([y, zh, inst, cell, core]).astype(jnp.int32)
-
     outer = lax.dynamic_index_in_dim(adjoint, core, 2, False)
     inner = lax.dynamic_index_in_dim(adjoint, 1 - core, 2, False)
     got_outer = send_pair(outer)
     got_inner = send_core(inner)
 
-    nine, eleven = (9, 8, 256), (11, 8, 256)
-    wide = [pltpu.VMEM((3, 72, 256), F32)]
+    rows = (3, 72, 256)
+    (early,) = call(sens_early_kernel, [rows], (flux_jac, outer, got_inner))
+    eight, ten = (18, 8, 256), (20, 8, 256)
     m0, m1, m2, m3 = call(
-        sens_early_kernel,
-        [nine, eleven, nine, eleven],
-        (pos, flux_jac, outer, got_inner, shift),
-        wide,
+        sens_late_kernel,
+        [eight, ten, eight, ten],
+        (flux_jac, inner, got_outer, early, shift),
+        [pltpu.VMEM(rows, F32)],
     )
     r2, r1, r3 = send_y(m2, 2), send_y(m1, 1), send_y(m3, 3)
-    n0, n1, n2, n3 = call(sens_late_kernel, [nine] * 4, (pos, flux_jac, inner, got_outer, m0), wide)
-    q2, q1, q3 = send_y(n2, 2), send_y(n1, 1), send_y(n3, 3)
-    own, out = call(
-        sum_y_kernel, [(12, 8, 256), (13, 8, 256)], (pos, m0, r1, r2, r3, n0, q1, q2, q3, shift)
-    )
-    (block,) = call(block_kernel, [(8, 16, 256)], (pos, own, send_zh(out), shift))
+    own, out = call(sum_y_kernel, [(12, 8, 256), (13, 8, 256)], (m0, r1, r2, r3, shift))
+    got = send_zh(out)
+    sides = got[12].reshape(2, 4, 256)
+    ends = [jnp.zeros((2, n, 256), F32) for n in (1, 3)]
+    wider = jnp.concatenate([ends[0], sides[:, :2], shift, sides[:, 2:], ends[1]], axis=1)
+    block = jnp.concatenate([(own + got[:12]).reshape(6, 16, 256), wider], axis=0)
     mate = send_core(block)
     far = send_pair(jnp.concatenate([block, mate[:3]], axis=0))
     beyond = send_core(far[3:6])
@@ -324,14 +309,14 @@
     basis, moments = call(
         krylov_kernel,
         [(4, 3, 2, 8, 256), (8, 128)],
-        (pos, block, mate, far, beyond),
+        (block, mate, far, beyond),
         [scratch, scratch, scratch, pltpu.VMEM((8, 16, 256), F32)],
     )
     parts = lax.all_to_all(jnp.broadcast_to(moments, (16, 8, 128)), ("y", "x"), 0, 0)
     moments = jnp.sum(parts, axis=0)
     parts = lax.all_to_all(jnp.broadcast_to(moments, (16, 8, 128)), ("zh", "zl", "core"), 0, 0)
     shape = (3, 2, 8, 256)
-    return tuple(call(finish_kernel, [shape, shape], (pos, parts, basis)))
+    return tuple(call(finish_kernel, [shape, shape], (parts, basis)))
 
 
 def solution(mesh):

time: 82.2 us -> 81.2 us (0.988)
  waiting for transfers between devices: 14 us -> 23.4 us
  starting transfers between devices: 24.8 us -> 16.7 us
  Pallas kernels: 6.08 us -> 2.81 us
  blocking collectives: 32.8 us -> 34.3 us
    ppermute x12 -> x9, waiting for transfers between devices: 14 us -> 23.4 us  [send(): return lax.ppermute(v, AXES, pairs)]
    ppermute x12 -> x9, starting transfers between devices: 24.8 us -> 16.7 us  [send(): return lax.ppermute(v, AXES, pairs)]
    pallas_call x6 -> x5, Pallas kernels: 6.08 us -> 2.81 us  [call(): pl.pallas_call(kernel, out_shape=[jax.ShapeDtypeStruct(s, F32) for s in o...]
    all_to_all x1, blocking collectives: 17.2 us -> 18.8 us  [local(): lax.all_to_all(jnp.broadcast_to(moments, (16, 8, 128)), ('y', 'x'), 0, 0)]
  transfers between devices with their start and end apart: 12 -> 9, of which waited for: 7 -> 6; matrix products, arithmetic and copies ran while one was open for 0% -> 0% of each run, Pallas kernels for 2% -> 0%
where the time goes in v5:
time: 81.2 us; the launch traced here: 80.9 us
  blocking collectives  34.3 us (42%)
  waiting for transfers between devices  23.4 us (29%)
  starting transfers between devices  16.7 us (21%)
  local copies, waits for them, and re-layouts  2.86 us (4%)
  Pallas kernels  2.81 us (3%)
    ppermute x9, waiting for transfers between devices, send(): return lax.ppermute(v, AXES, pairs)  23.4 us
    all_to_all x1, blocking collectives, local(): lax.all_to_all(jnp.broadcast_to(moments, (16, 8, 128)), ('y', 'x'), 0, 0)  18.8 us
    ppermute x9, starting transfers between devices, send(): return lax.ppermute(v, AXES, pairs)  16.7 us
    all_to_all x1, blocking collectives, local(): lax.all_to_all(jnp.broadcast_to(moments, (16, 8, 128)), ('zh', 'zl', 'cor...  15.5 us
    pallas_call x5, Pallas kernels, call(): pl.pallas_call(kernel, out_shape=[jax.ShapeDtypeStruct(s, F32) for s in o...  2.81 us
  transfers between devices with their start and end apart: 9, of which 6 were waited for; matrix products, arithmetic and copies ran while one was open for 0% of the time, Pallas kernels for 0%

profile of v5, /device:TPU:1, one launch (start us, length us, event | category | flops | bytes accessed | tf_op | source)
XLA Modules:
  0.0 80.9 jit_solution(4962433850790324620)
XLA Ops:
  0.6 0.0 copy-start.1
  0.6 1.1 %dynamic-slice_bitcast_fusion = (bf16[2,5,64,256]{3,2,1,0:T(8,128)(2,1)S(1)}, bf16[2,5,64,256]{3,2,1,0:T(8,128)(2,1)S(1)}) fusion(bf16[2,5,2,64,256]{4,3,2,1,0:T(8,128)(2,1)} %param.3, s32[]{:T(128)S(6)} %select_n.8, s32[]{:T(128)S(6)} %select_n.7), kind=kLoop, calls=%fused_computation | loop fusion | bytes 1310728 | tf_op jit(solution)/shard_map/jit(dynamic_index_in_dim)/squeeze | solution.py:283
  1.8 3.3 %collective-permute-start.1 = (bf16[2,5,64,256]{3,2,1,0:T(8,128)(2,1)S(1)}, bf16[2,5,64,256]{3,2,1,0:T(8,128)(2,1)S(1)}, u32[]{:S(2)}, u32[]{:S(2)}) collective-permute-start(bf16[2,5,64,256]{3,2,1,0:T(8,128)(2,1)S(1)} %get-tuple-element.19.a), channel_id=1, source_target_pairs={{0,1},{1,0},{2,3},{3,2},{4,5},{5,4},{6,7},{7,6},{8,9},{9,8},{10,11... | collective-permute-start | bytes 983048 | tf_op jit(solution)/shard_map/ppermute | solution.py:30
  5.1 1.9 %collective-permute-start = (bf16[2,5,64,256]{3,2,1,0:T(8,128)(2,1)S(1)}, bf16[2,5,64,256]{3,2,1,0:T(8,128)(2,1)S(1)}, u32[]{:S(2)}, u32[]{:S(2)}) collective-permute-start(bf16[2,5,64,256]{3,2,1,0:T(8,128)(2,1)S(1)} %get-tuple-element.18.a), channel_id=1, source_target_pairs={{1,2},{2,1},{3,4},{4,3},{5,6},{6,5},{7,8},{8,7},{9,10},{10,9},{11,... | collective-permute-start | bytes 983048 | tf_op jit(solution)/shard_map/ppermute | solution.py:30
  7.0 0.0 collective-permute-done.1.got
  7.0 0.0 copy-start
  7.0 1.5 %copy-done = bf16[2,5,3,2,64,256]{5,4,3,2,1,0:T(8,128)(2,1)S(1)} copy-done((bf16[2,5,3,2,64,256]{5,4,3,2,1,0:T(8,128)(2,1)S(1)}, bf16[2,5,3,2,64,256]{5,4,3,2,1,0:T(8,128)(2,1)}, u32[]{:S(2)}) %copy-start) | copy-done | bytes 1966104
  8.6 0.3 shard_map.50.early
  8.9 8.2 %collective-permute-done.got = bf16[2,5,64,256]{3,2,1,0:T(8,128)(2,1)S(1)} collective-permute-done((bf16[2,5,64,256]{3,2,1,0:T(8,128)(2,1)S(1)}, bf16[2,5,64,256]{3,2,1,0:T(8,128)(2,1)S(1)}, u32[]{:S(2)}, u32[]{:S(2)}) %collective-permute-start) | collective-permute-done | bytes 327712 | tf_op jit(solution)/shard_map/ppermute | solution.py:30
  17.0 0.0 copy-done.1
  17.0 0.3 shard_map.51
  17.3 0.1 collective-permute-start.2
  17.4 2.7 %collective-permute-start.4 = (f32[20,8,256]{2,1,0:T(8,128)S(1)}, f32[20,8,256]{2,1,0:T(8,128)S(1)}, u32[]{:S(2)}, u32[]{:S(2)}) collective-permute-start(f32[20,8,256]{2,1,0:T(8,128)S(1)} %get-tuple-element.13), channel_id=1, source_target_pairs={{0,192},{1,193},{2,194},{3,195},{4,196},{5,197},{6,198},{7,199},{8... | collective-permute-start | bytes 491528 | tf_op jit(solution)/shard_map/ppermute | solution.py:30
  20.1 0.0 collective-permute-start.3
  20.1 5.5 %collective-permute-done.3.r2 = f32[18,8,256]{2,1,0:T(8,128)S(1)} collective-permute-done((f32[18,8,256]{2,1,0:T(8,128)S(1)}, f32[18,8,256]{2,1,0:T(8,128)S(1)}, u32[]{:S(2)}, u32[]{:S(2)}) %collective-permute-start.3) | collective-permute-done | bytes 147488 | tf_op jit(solution)/shard_map/ppermute | solution.py:30
  25.6 0.0 collective-permute-done.2.r1
  25.6 0.0 collective-permute-done.4.r3
  25.6 0.1 shard_map.52
  25.6 3.6 %collective-permute-start.5 = (f32[13,8,256]{2,1,0:T(8,128)S(1)}, f32[13,8,256]{2,1,0:T(8,128)S(1)}, u32[]{:S(2)}, u32[]{:S(2)}) collective-permute-start(f32[13,8,256]{2,1,0:T(8,128)S(1)} %get-tuple-element.15), channel_id=1, source_target_pairs={{0,32},{1,33},{2,34},{3,35},{4,36},{5,37},{6,38},{7,39},{8,40},{9,... | collective-permute-start | bytes 319496 | tf_op jit(solution)/shard_map/ppermute | solution.py:30
  29.2 4.0 %collective-permute-done.5 = f32[13,8,256]{2,1,0:T(8,128)S(1)} collective-permute-done((f32[13,8,256]{2,1,0:T(8,128)S(1)}, f32[13,8,256]{2,1,0:T(8,128)S(1)}, u32[]{:S(2)}, u32[]{:S(2)}) %collective-permute-start.5) | collective-permute-done | bytes 106528 | tf_op jit(solution)/shard_map/ppermute | solution.py:30
  33.3 0.1 concatenate.10
  33.5 0.1 collective-permute-start.6
  33.6 1.3 %collective-permute-done.6.mate = f32[8,16,256]{2,1,0:T(8,128)S(1)} collective-permute-done((f32[8,16,256]{2,1,0:T(8,128)S(1)}, f32[8,16,256]{2,1,0:T(8,128)S(1)}, u32[]{:S(2)}, u32[]{:S(2)}) %collective-permute-start.6) | collective-permute-done | bytes 131104 | tf_op jit(solution)/shard_map/ppermute | solution.py:30
  34.9 5.0 %collective-permute-start.7 = (f32[11,16,256]{2,1,0:T(8,128)S(1)}, f32[11,16,256]{2,1,0:T(8,128)S(1)}, u32[]{:S(2)}, u32[]{:S(2)}) collective-permute-start(f32[11,16,256]{2,1,0:T(8,128)S(1)} %pad_maximum_fusion), channel_id=1, source_target_pairs={{1,2},{2,1},{3,4},{4,3},{5,6},{6,5},{7,8},{8,7},{9,10},{10,9},{11,... | collective-permute-start | bytes 540680 | tf_op jit(solution)/shard_map/ppermute | solution.py:30
  39.9 3.2 %collective-permute-done.7.far = f32[11,16,256]{2,1,0:T(8,128)S(1)} collective-permute-done((f32[11,16,256]{2,1,0:T(8,128)S(1)}, f32[11,16,256]{2,1,0:T(8,128)S(1)}, u32[]{:S(2)}, u32[]{:S(2)}) %collective-permute-start.7) | collective-permute-done | bytes 180256 | tf_op jit(solution)/shard_map/ppermute | solution.py:30
  43.1 0.0 collective-permute-start.8
  43.1 1.2 %collective-permute-done.8.beyond = f32[3,16,256]{2,1,0:T(8,128)S(1)} collective-permute-done((f32[3,16,256]{2,1,0:T(8,128)S(1)}, f32[3,16,256]{2,1,0:T(8,128)S(1)}, u32[]{:S(2)}, u32[]{:S(2)}) %collective-permute-start.8) | collective-permute-done | bytes 49184 | tf_op jit(solution)/shard_map/ppermute | solution.py:30
  44.3 0.9 %shard_map.53 = (f32[4,3,2,8,256]{4,3,2,1,0:T(8,128)S(1)}, f32[8,128]{1,0:T(8,128)S(1)}) custom-call(f32[8,16,256]{2,1,0:T(8,128)S(1)} %pad_maximum_fusion.1.block, f32[8,16,256]{2,1,0:T(8,128)S(1)} %collective-permute-done.6.mate, f32[11,16,256]{2,1,0:T(8,128)S(1)} %collective-permute-done.7.far, f32[3,16,256]{2,1,0:T(8,128)S(1)} %collective-permute-done.8.beyond), custom_call_target="tpu_custom_call" | custom-call | tf_op jit(solution)/shard_map/pallas_call | solution.py:57
  45.2 18.8 %all_to_all.10 = f32[16,8,128]{2,1,0:T(8,128)S(1)} all-to-all(f32[16,8,128]{2,1,0:T(8,128)S(1)} %broadcast_in_dim.14), channel_id=1, replica_groups=mesh['y'=4,'zh'=2,'x'=4,'zl'=4,'core'=2] {'y','x'}, dimensions={0} | all-to-all | bytes 131072 | tf_op jit(solution)/shard_map/all_to_all | solution.py:315
  64.1 15.5 %all_to_all.11.parts = f32[16,8,128]{2,1,0:T(8,128)S(1)} all-to-all(f32[16,8,128]{2,1,0:T(8,128)S(1)} %broadcast_in_dim.15), channel_id=1, replica_groups=mesh['y'=4,'zh'=2,'x'=4,'zl'=4,'core'=2] {'zh','zl','core'}, dimensions={0} | all-to-all | bytes 131072 | tf_op jit(solution)/shard_map/all_to_all | solution.py:317
  79.6 1.3 %shard_map.54 = (f32[3,2,8,256]{3,2,1,0:T(8,128)}, f32[3,2,8,256]{3,2,1,0:T(8,128)}) custom-call(f32[16,8,128]{2,1,0:T(8,128)S(1)} %all_to_all.11.parts, f32[4,3,2,8,256]{4,3,2,1,0:T(8,128)S(1)} %get-tuple-element.17.basis), custom_call_target="tpu_custom_call" | custom-call | tf_op jit(solution)/shard_map/pallas_call | solution.py:57
  (13 shorter events, 0.1 us)
Async XLA Ops:
  0.6 16.4 %copy-start.1 = (f32[2,8,256]{2,1,0:T(8,128)S(1)}, f32[2,8,256]{2,1,0:T(8,128)}, u32[]{:S(2)}) copy-start(f32[2,8,256]{2,1,0:T(8,128)} %shift.3) | copy-start | bytes 49156
  1.8 5.2 %collective-permute-start.1 = (bf16[2,5,64,256]{3,2,1,0:T(8,128)(2,1)S(1)}, bf16[2,5,64,256]{3,2,1,0:T(8,128)(2,1)S(1)}, u32[]{:S(2)}, u32[]{:S(2)}) collective-permute-start(bf16[2,5,64,256]{3,2,1,0:T(8,128)(2,1)S(1)} %get-tuple-element.19.a), channel_id=1, source_target_pairs={{0,1},{1,0},{2,3},{3,2},{4,5},{5,4},{6,7},{7,6},{8,9},{9,8},{10,11... | collective-permute-start | bytes 983048 | tf_op jit(solution)/shard_map/ppermute | solution.py:30
  5.1 11.9 %collective-permute-start = (bf16[2,5,64,256]{3,2,1,0:T(8,128)(2,1)S(1)}, bf16[2,5,64,256]{3,2,1,0:T(8,128)(2,1)S(1)}, u32[]{:S(2)}, u32[]{:S(2)}) collective-permute-start(bf16[2,5,64,256]{3,2,1,0:T(8,128)(2,1)S(1)} %get-tuple-element.18.a), channel_id=1, source_target_pairs={{1,2},{2,1},{3,4},{4,3},{5,6},{6,5},{7,8},{8,7},{9,10},{10,9},{11,... | collective-permute-start | bytes 983048 | tf_op jit(solution)/shard_map/ppermute | solution.py:30
  7.0 1.5 %copy-start = (bf16[2,5,3,2,64,256]{5,4,3,2,1,0:T(8,128)(2,1)S(1)}, bf16[2,5,3,2,64,256]{5,4,3,2,1,0:T(8,128)(2,1)}, u32[]{:S(2)}) copy-start(bf16[2,5,3,2,64,256]{5,4,3,2,1,0:T(8,128)(2,1)} %f.3) | copy-start | bytes 5898244
  17.3 8.3 %collective-permute-start.2 = (f32[20,8,256]{2,1,0:T(8,128)S(1)}, f32[20,8,256]{2,1,0:T(8,128)S(1)}, u32[]{:S(2)}, u32[]{:S(2)}) collective-permute-start(f32[20,8,256]{2,1,0:T(8,128)S(1)} %get-tuple-element.11), channel_id=1, source_target_pairs={{0,64},{1,65},{2,66},{3,67},{4,68},{5,69},{6,70},{7,71},{8,72},{9,... | collective-permute-start | bytes 491528 | tf_op jit(solution)/shard_map/ppermute | solution.py:30
  17.4 8.2 %collective-permute-start.4 = (f32[20,8,256]{2,1,0:T(8,128)S(1)}, f32[20,8,256]{2,1,0:T(8,128)S(1)}, u32[]{:S(2)}, u32[]{:S(2)}) collective-permute-start(f32[20,8,256]{2,1,0:T(8,128)S(1)} %get-tuple-element.13), channel_id=1, source_target_pairs={{0,192},{1,193},{2,194},{3,195},{4,196},{5,197},{6,198},{7,199},{8... | collective-permute-start | bytes 491528 | tf_op jit(solution)/shard_map/ppermute | solution.py:30
  20.1 5.5 %collective-permute-start.3 = (f32[18,8,256]{2,1,0:T(8,128)S(1)}, f32[18,8,256]{2,1,0:T(8,128)S(1)}, u32[]{:S(2)}, u32[]{:S(2)}) collective-permute-start(f32[18,8,256]{2,1,0:T(8,128)S(1)} %get-tuple-element.12), channel_id=1, source_target_pairs={{0,128},{1,129},{2,130},{3,131},{4,132},{5,133},{6,134},{7,135},{8... | collective-permute-start | bytes 442376 | tf_op jit(solution)/shard_map/ppermute | solution.py:30
  25.6 7.6 %collective-permute-start.5 = (f32[13,8,256]{2,1,0:T(8,128)S(1)}, f32[13,8,256]{2,1,0:T(8,128)S(1)}, u32[]{:S(2)}, u32[]{:S(2)}) collective-permute-start(f32[13,8,256]{2,1,0:T(8,128)S(1)} %get-tuple-element.15), channel_id=1, source_target_pairs={{0,32},{1,33},{2,34},{3,35},{4,36},{5,37},{6,38},{7,39},{8,40},{9,... | collective-permute-start | bytes 319496 | tf_op jit(solution)/shard_map/ppermute | solution.py:30
  33.5 1.4 %collective-permute-start.6 = (f32[8,16,256]{2,1,0:T(8,128)S(1)}, f32[8,16,256]{2,1,0:T(8,128)S(1)}, u32[]{:S(2)}, u32[]{:S(2)}) collective-permute-start(f32[8,16,256]{2,1,0:T(8,128)S(1)} %pad_maximum_fusion.1.block), channel_id=1, source_target_pairs={{0,1},{1,0},{2,3},{3,2},{4,5},{5,4},{6,7},{7,6},{8,9},{9,8},{10,11... | collective-permute-start | bytes 393224 | tf_op jit(solution)/shard_map/ppermute | solution.py:30
  34.9 8.2 %collective-permute-start.7 = (f32[11,16,256]{2,1,0:T(8,128)S(1)}, f32[11,16,256]{2,1,0:T(8,128)S(1)}, u32[]{:S(2)}, u32[]{:S(2)}) collective-permute-start(f32[11,16,256]{2,1,0:T(8,128)S(1)} %pad_maximum_fusion), channel_id=1, source_target_pairs={{1,2},{2,1},{3,4},{4,3},{5,6},{6,5},{7,8},{8,7},{9,10},{10,9},{11,... | collective-permute-start | bytes 540680 | tf_op jit(solution)/shard_map/ppermute | solution.py:30
  43.1 1.2 %collective-permute-start.8 = (f32[3,16,256]{2,1,0:T(8,128)S(1)}, f32[3,16,256]{2,1,0:T(8,128)S(1)}, u32[]{:S(2)}, u32[]{:S(2)}) collective-permute-start(f32[3,16,256]{2,1,0:T(8,128)S(1)} %slice.29), channel_id=1, source_target_pairs={{0,1},{1,0},{2,3},{3,2},{4,5},{5,4},{6,7},{7,6},{8,9},{9,8},{10,11... | collective-permute-start | bytes 147464 | tf_op jit(solution)/shard_map/ppermute | solution.py:30

commit v6 on v5

--- a/solution.py
+++ b/solution.py
@@ -95,11 +95,13 @@
         for k in range(3):
             out[k * 3 : k * 3 + 3] = early[k, pl.ds(first, 24), :].reshape(3, 8, 256)
             out[9 + k * 3 : 12 + k * 3] = wide[k, pl.ds(first, 24), :].reshape(3, 8, 256)
-    for out in (m1, m3):
-        out[18:20] = shift[...]
-
-
-def sum_y_kernel(m0, r1, r2, r3, shift, own, out):
+    for out, span in ((m1, slice(6, 8)), (m2, slice(6, 8)), (m3, slice(0, 2))):
+        for x in range(2):
+            out[18, x * 2 : x * 2 + 2, :] = shift[x, span, :]
+        out[18, 4:8, :] = jnp.zeros((4, 256), F32)
+
+
+def sum_y_kernel(m0, r2, r1, r3, shift, own, out):
     zh = lax.axis_index("zh")
     for s in range(6):
         for g in range(2):
@@ -108,8 +110,8 @@
                 to[s * 2 + g] = (m0[k] + r1[k]) + (r2[k] + r3[k])
     low = zh == 0
     for x in range(2):
-        below = jnp.where(low, shift[x, 6:8, :], r1[18 + x, 6:8, :])
-        above = jnp.where(low, r3[18 + x, 0:2, :], shift[x, 0:2, :])
+        below = jnp.where(low, shift[x, 6:8, :], r1[18, x * 2 : x * 2 + 2, :])
+        above = jnp.where(low, r3[18, x * 2 : x * 2 + 2, :], shift[x, 0:2, :])
         out[12, x * 4 : x * 4 + 2, :] = below
         out[12, x * 4 + 2 : x * 4 + 4, :] = above
 
@@ -287,15 +289,15 @@
 
     rows = (3, 72, 256)
     (early,) = call(sens_early_kernel, [rows], (flux_jac, outer, got_inner))
-    eight, ten = (18, 8, 256), (20, 8, 256)
+    nineteen = (19, 8, 256)
     m0, m1, m2, m3 = call(
         sens_late_kernel,
-        [eight, ten, eight, ten],
+        [(18, 8, 256)] + [nineteen] * 3,
         (flux_jac, inner, got_outer, early, shift),
         [pltpu.VMEM(rows, F32)],
     )
     r2, r1, r3 = send_y(m2, 2), send_y(m1, 1), send_y(m3, 3)
-    own, out = call(sum_y_kernel, [(12, 8, 256), (13, 8, 256)], (m0, r1, r2, r3, shift))
+    own, out = call(sum_y_kernel, [(12, 8, 256), (13, 8, 256)], (m0, r2, r1, r3, shift))
     got = send_zh(out)
     sides = got[12].reshape(2, 4, 256)
     ends = [jnp.zeros((2, n, 256), F32) for n in (1, 3)]

time: 81.2 us -> 81.4 us (level)
  starting transfers between devices: 16.7 us -> 21.7 us
  blocking collectives: 34.3 us -> 31.9 us
  waiting for transfers between devices: 23.4 us -> 21 us
    ppermute x9, starting transfers between devices: 16.7 us -> 21.7 us  [send(): return lax.ppermute(v, AXES, pairs)]
    ppermute x9, waiting for transfers between devices: 23.4 us -> 21 us  [send(): return lax.ppermute(v, AXES, pairs)]
    all_to_all x1, blocking collectives: 18.8 us -> 16.9 us  [local(): lax.all_to_all(jnp.broadcast_to(moments, (16, 8, 128)), ('y', 'x'), 0, 0)]
  transfers between devices with their start and end apart: 9 -> 9, of which waited for: 6 -> 7; matrix products, arithmetic and copies ran while one was open for 0% -> 0% of each run, Pallas kernels for 0% -> 0%
where the time goes in v6:
time: 81.4 us; the launch traced here: 81.1 us
  blocking collectives  31.9 us (39%)
  starting transfers between devices  21.7 us (27%)
  waiting for transfers between devices  21 us (26%)
  local copies, waits for them, and re-layouts  2.86 us (4%)
  Pallas kernels  2.81 us (3%)
    ppermute x9, starting transfers between devices, send(): return lax.ppermute(v, AXES, pairs)  21.7 us
    ppermute x9, waiting for transfers between devices, send(): return lax.ppermute(v, AXES, pairs)  21 us
    all_to_all x1, blocking collectives, local(): lax.all_to_all(jnp.broadcast_to(moments, (16, 8, 128)), ('y', 'x'), 0, 0)  16.9 us
    all_to_all x1, blocking collectives, local(): lax.all_to_all(jnp.broadcast_to(moments, (16, 8, 128)), ('zh', 'zl', 'cor...  15 us
    pallas_call x5, Pallas kernels, call(): pl.pallas_call(kernel, out_shape=[jax.ShapeDtypeStruct(s, F32) for s in o...  2.81 us
  transfers between devices with their start and end apart: 9, of which 7 were waited for; matrix products, arithmetic and copies ran while one was open for 0% of the time, Pallas kernels for 0%

profile of v6, /device:TPU:1, one launch (start us, length us, event | category | flops | bytes accessed | tf_op | source)
XLA Modules:
  0.0 81.1 jit_solution(8031363732868074128)
XLA Ops:
  0.6 0.0 copy-start.1
  0.6 1.1 %dynamic-slice_bitcast_fusion = (bf16[2,5,64,256]{3,2,1,0:T(8,128)(2,1)S(1)}, bf16[2,5,64,256]{3,2,1,0:T(8,128)(2,1)S(1)}) fusion(bf16[2,5,2,64,256]{4,3,2,1,0:T(8,128)(2,1)} %param.3, s32[]{:T(128)S(6)} %select_n.8, s32[]{:T(128)S(6)} %select_n.7), kind=kLoop, calls=%fused_computation | loop fusion | bytes 1310728 | tf_op jit(solution)/shard_map/jit(dynamic_index_in_dim)/squeeze | solution.py:285
  1.8 3.3 %collective-permute-start.1 = (bf16[2,5,64,256]{3,2,1,0:T(8,128)(2,1)S(1)}, bf16[2,5,64,256]{3,2,1,0:T(8,128)(2,1)S(1)}, u32[]{:S(2)}, u32[]{:S(2)}) collective-permute-start(bf16[2,5,64,256]{3,2,1,0:T(8,128)(2,1)S(1)} %get-tuple-element.19.a), channel_id=1, source_target_pairs={{0,1},{1,0},{2,3},{3,2},{4,5},{5,4},{6,7},{7,6},{8,9},{9,8},{10,11... | collective-permute-start | bytes 983048 | tf_op jit(solution)/shard_map/ppermute | solution.py:30
  5.1 1.9 %collective-permute-start = (bf16[2,5,64,256]{3,2,1,0:T(8,128)(2,1)S(1)}, bf16[2,5,64,256]{3,2,1,0:T(8,128)(2,1)S(1)}, u32[]{:S(2)}, u32[]{:S(2)}) collective-permute-start(bf16[2,5,64,256]{3,2,1,0:T(8,128)(2,1)S(1)} %get-tuple-element.18.a), channel_id=1, source_target_pairs={{1,2},{2,1},{3,4},{4,3},{5,6},{6,5},{7,8},{8,7},{9,10},{10,9},{11,... | collective-permute-start | bytes 983048 | tf_op jit(solution)/shard_map/ppermute | solution.py:30
  7.0 0.0 collective-permute-done.1.got
  7.0 0.0 copy-start
  7.0 1.5 %copy-done = bf16[2,5,3,2,64,256]{5,4,3,2,1,0:T(8,128)(2,1)S(1)} copy-done((bf16[2,5,3,2,64,256]{5,4,3,2,1,0:T(8,128)(2,1)S(1)}, bf16[2,5,3,2,64,256]{5,4,3,2,1,0:T(8,128)(2,1)}, u32[]{:S(2)}) %copy-start) | copy-done | bytes 1966104
  8.6 0.3 shard_map.50.early
  8.9 8.1 %collective-permute-done.got = bf16[2,5,64,256]{3,2,1,0:T(8,128)(2,1)S(1)} collective-permute-done((bf16[2,5,64,256]{3,2,1,0:T(8,128)(2,1)S(1)}, bf16[2,5,64,256]{3,2,1,0:T(8,128)(2,1)S(1)}, u32[]{:S(2)}, u32[]{:S(2)}) %collective-permute-start) | collective-permute-done | bytes 327712 | tf_op jit(solution)/shard_map/ppermute | solution.py:30
  17.0 0.0 copy-done.1
  17.0 0.3 shard_map.51
  17.3 0.1 collective-permute-start.2
  17.4 0.1 collective-permute-start.3
  17.5 2.7 %collective-permute-start.4 = (f32[19,8,256]{2,1,0:T(8,128)S(1)}, f32[19,8,256]{2,1,0:T(8,128)S(1)}, u32[]{:S(2)}, u32[]{:S(2)}) collective-permute-start(f32[19,8,256]{2,1,0:T(8,128)S(1)} %get-tuple-element.13), channel_id=1, source_target_pairs={{0,192},{1,193},{2,194},{3,195},{4,196},{5,197},{6,198},{7,199},{8... | collective-permute-start | bytes 466952 | tf_op jit(solution)/shard_map/ppermute | solution.py:30
  20.1 2.9 %collective-permute-done.2.r2 = f32[19,8,256]{2,1,0:T(8,128)S(1)} collective-permute-done((f32[19,8,256]{2,1,0:T(8,128)S(1)}, f32[19,8,256]{2,1,0:T(8,128)S(1)}, u32[]{:S(2)}, u32[]{:S(2)}) %collective-permute-start.2) | collective-permute-done | bytes 155680 | tf_op jit(solution)/shard_map/ppermute | solution.py:30
  23.1 1.4 %collective-permute-done.3.r1 = f32[19,8,256]{2,1,0:T(8,128)S(1)} collective-permute-done((f32[19,8,256]{2,1,0:T(8,128)S(1)}, f32[19,8,256]{2,1,0:T(8,128)S(1)}, u32[]{:S(2)}, u32[]{:S(2)}) %collective-permute-start.3) | collective-permute-done | bytes 155680 | tf_op jit(solution)/shard_map/ppermute | solution.py:30
  24.4 0.0 collective-permute-done.4.r3
  24.4 0.1 shard_map.52
  24.5 4.6 %collective-permute-start.5 = (f32[13,8,256]{2,1,0:T(8,128)S(1)}, f32[13,8,256]{2,1,0:T(8,128)S(1)}, u32[]{:S(2)}, u32[]{:S(2)}) collective-permute-start(f32[13,8,256]{2,1,0:T(8,128)S(1)} %get-tuple-element.15), channel_id=1, source_target_pairs={{0,32},{1,33},{2,34},{3,35},{4,36},{5,37},{6,38},{7,39},{8,40},{9,... | collective-permute-start | bytes 319496 | tf_op jit(solution)/shard_map/ppermute | solution.py:30
  29.1 2.9 %collective-permute-done.5 = f32[13,8,256]{2,1,0:T(8,128)S(1)} collective-permute-done((f32[13,8,256]{2,1,0:T(8,128)S(1)}, f32[13,8,256]{2,1,0:T(8,128)S(1)}, u32[]{:S(2)}, u32[]{:S(2)}) %collective-permute-start.5) | collective-permute-done | bytes 106528 | tf_op jit(solution)/shard_map/ppermute | solution.py:30
  32.1 0.1 concatenate.10
  32.2 0.1 collective-permute-start.6
  32.3 1.3 %collective-permute-done.6.mate = f32[8,16,256]{2,1,0:T(8,128)S(1)} collective-permute-done((f32[8,16,256]{2,1,0:T(8,128)S(1)}, f32[8,16,256]{2,1,0:T(8,128)S(1)}, u32[]{:S(2)}, u32[]{:S(2)}) %collective-permute-start.6) | collective-permute-done | bytes 131104 | tf_op jit(solution)/shard_map/ppermute | solution.py:30
  33.7 8.9 %collective-permute-start.7 = (f32[11,16,256]{2,1,0:T(8,128)S(1)}, f32[11,16,256]{2,1,0:T(8,128)S(1)}, u32[]{:S(2)}, u32[]{:S(2)}) collective-permute-start(f32[11,16,256]{2,1,0:T(8,128)S(1)} %pad_maximum_fusion), channel_id=1, source_target_pairs={{1,2},{2,1},{3,4},{4,3},{5,6},{6,5},{7,8},{8,7},{9,10},{10,9},{11,... | collective-permute-start | bytes 540680 | tf_op jit(solution)/shard_map/ppermute | solution.py:30
  42.6 3.2 %collective-permute-done.7.far = f32[11,16,256]{2,1,0:T(8,128)S(1)} collective-permute-done((f32[11,16,256]{2,1,0:T(8,128)S(1)}, f32[11,16,256]{2,1,0:T(8,128)S(1)}, u32[]{:S(2)}, u32[]{:S(2)}) %collective-permute-start.7) | collective-permute-done | bytes 180256 | tf_op jit(solution)/shard_map/ppermute | solution.py:30
  45.8 0.0 collective-permute-start.8
  45.8 1.2 %collective-permute-done.8.beyond = f32[3,16,256]{2,1,0:T(8,128)S(1)} collective-permute-done((f32[3,16,256]{2,1,0:T(8,128)S(1)}, f32[3,16,256]{2,1,0:T(8,128)S(1)}, u32[]{:S(2)}, u32[]{:S(2)}) %collective-permute-start.8) | collective-permute-done | bytes 49184 | tf_op jit(solution)/shard_map/ppermute | solution.py:30
  47.0 0.9 %shard_map.53 = (f32[4,3,2,8,256]{4,3,2,1,0:T(8,128)S(1)}, f32[8,128]{1,0:T(8,128)S(1)}) custom-call(f32[8,16,256]{2,1,0:T(8,128)S(1)} %pad_maximum_fusion.1.block, f32[8,16,256]{2,1,0:T(8,128)S(1)} %collective-permute-done.6.mate, f32[11,16,256]{2,1,0:T(8,128)S(1)} %collective-permute-done.7.far, f32[3,16,256]{2,1,0:T(8,128)S(1)} %collective-permute-done.8.beyond), custom_call_target="tpu_custom_call" | custom-call | tf_op jit(solution)/shard_map/pallas_call | solution.py:57
  47.9 16.9 %all_to_all.10 = f32[16,8,128]{2,1,0:T(8,128)S(1)} all-to-all(f32[16,8,128]{2,1,0:T(8,128)S(1)} %broadcast_in_dim.14), channel_id=1, replica_groups=mesh['y'=4,'zh'=2,'x'=4,'zl'=4,'core'=2] {'y','x'}, dimensions={0} | all-to-all | bytes 131072 | tf_op jit(solution)/shard_map/all_to_all | solution.py:317
  64.8 15.0 %all_to_all.11.parts = f32[16,8,128]{2,1,0:T(8,128)S(1)} all-to-all(f32[16,8,128]{2,1,0:T(8,128)S(1)} %broadcast_in_dim.15), channel_id=1, replica_groups=mesh['y'=4,'zh'=2,'x'=4,'zl'=4,'core'=2] {'zh','zl','core'}, dimensions={0} | all-to-all | bytes 131072 | tf_op jit(solution)/shard_map/all_to_all | solution.py:319
  79.8 1.3 %shard_map.54 = (f32[3,2,8,256]{3,2,1,0:T(8,128)}, f32[3,2,8,256]{3,2,1,0:T(8,128)}) custom-call(f32[16,8,128]{2,1,0:T(8,128)S(1)} %all_to_all.11.parts, f32[4,3,2,8,256]{4,3,2,1,0:T(8,128)S(1)} %get-tuple-element.17.basis), custom_call_target="tpu_custom_call" | custom-call | tf_op jit(solution)/shard_map/pallas_call | solution.py:57
  (13 shorter events, 0.1 us)
Async XLA Ops:
  0.6 16.3 %copy-start.1 = (f32[2,8,256]{2,1,0:T(8,128)S(1)}, f32[2,8,256]{2,1,0:T(8,128)}, u32[]{:S(2)}) copy-start(f32[2,8,256]{2,1,0:T(8,128)} %shift.3) | copy-start | bytes 49156
  1.8 5.2 %collective-permute-start.1 = (bf16[2,5,64,256]{3,2,1,0:T(8,128)(2,1)S(1)}, bf16[2,5,64,256]{3,2,1,0:T(8,128)(2,1)S(1)}, u32[]{:S(2)}, u32[]{:S(2)}) collective-permute-start(bf16[2,5,64,256]{3,2,1,0:T(8,128)(2,1)S(1)} %get-tuple-element.19.a), channel_id=1, source_target_pairs={{0,1},{1,0},{2,3},{3,2},{4,5},{5,4},{6,7},{7,6},{8,9},{9,8},{10,11... | collective-permute-start | bytes 983048 | tf_op jit(solution)/shard_map/ppermute | solution.py:30
  5.1 11.9 %collective-permute-start = (bf16[2,5,64,256]{3,2,1,0:T(8,128)(2,1)S(1)}, bf16[2,5,64,256]{3,2,1,0:T(8,128)(2,1)S(1)}, u32[]{:S(2)}, u32[]{:S(2)}) collective-permute-start(bf16[2,5,64,256]{3,2,1,0:T(8,128)(2,1)S(1)} %get-tuple-element.18.a), channel_id=1, source_target_pairs={{1,2},{2,1},{3,4},{4,3},{5,6},{6,5},{7,8},{8,7},{9,10},{10,9},{11,... | collective-permute-start | bytes 983048 | tf_op jit(solution)/shard_map/ppermute | solution.py:30
  7.0 1.5 %copy-start = (bf16[2,5,3,2,64,256]{5,4,3,2,1,0:T(8,128)(2,1)S(1)}, bf16[2,5,3,2,64,256]{5,4,3,2,1,0:T(8,128)(2,1)}, u32[]{:S(2)}) copy-start(bf16[2,5,3,2,64,256]{5,4,3,2,1,0:T(8,128)(2,1)} %f.3) | copy-start | bytes 5898244
  17.3 5.8 %collective-permute-start.2 = (f32[19,8,256]{2,1,0:T(8,128)S(1)}, f32[19,8,256]{2,1,0:T(8,128)S(1)}, u32[]{:S(2)}, u32[]{:S(2)}) collective-permute-start(f32[19,8,256]{2,1,0:T(8,128)S(1)} %get-tuple-element.11), channel_id=1, source_target_pairs={{0,128},{1,129},{2,130},{3,131},{4,132},{5,133},{6,134},{7,135},{8... | collective-permute-start | bytes 466952 | tf_op jit(solution)/shard_map/ppermute | solution.py:30
  17.4 7.0 %collective-permute-start.3 = (f32[19,8,256]{2,1,0:T(8,128)S(1)}, f32[19,8,256]{2,1,0:T(8,128)S(1)}, u32[]{:S(2)}, u32[]{:S(2)}) collective-permute-start(f32[19,8,256]{2,1,0:T(8,128)S(1)} %get-tuple-element.12), channel_id=1, source_target_pairs={{0,64},{1,65},{2,66},{3,67},{4,68},{5,69},{6,70},{7,71},{8,72},{9,... | collective-permute-start | bytes 466952 | tf_op jit(solution)/shard_map/ppermute | solution.py:30
  17.5 6.9 %collective-permute-start.4 = (f32[19,8,256]{2,1,0:T(8,128)S(1)}, f32[19,8,256]{2,1,0:T(8,128)S(1)}, u32[]{:S(2)}, u32[]{:S(2)}) collective-permute-start(f32[19,8,256]{2,1,0:T(8,128)S(1)} %get-tuple-element.13), channel_id=1, source_target_pairs={{0,192},{1,193},{2,194},{3,195},{4,196},{5,197},{6,198},{7,199},{8... | collective-permute-start | bytes 466952 | tf_op jit(solution)/shard_map/ppermute | solution.py:30
  24.5 7.5 %collective-permute-start.5 = (f32[13,8,256]{2,1,0:T(8,128)S(1)}, f32[13,8,256]{2,1,0:T(8,128)S(1)}, u32[]{:S(2)}, u32[]{:S(2)}) collective-permute-start(f32[13,8,256]{2,1,0:T(8,128)S(1)} %get-tuple-element.15), channel_id=1, source_target_pairs={{0,32},{1,33},{2,34},{3,35},{4,36},{5,37},{6,38},{7,39},{8,40},{9,... | collective-permute-start | bytes 319496 | tf_op jit(solution)/shard_map/ppermute | solution.py:30
  32.2 1.4 %collective-permute-start.6 = (f32[8,16,256]{2,1,0:T(8,128)S(1)}, f32[8,16,256]{2,1,0:T(8,128)S(1)}, u32[]{:S(2)}, u32[]{:S(2)}) collective-permute-start(f32[8,16,256]{2,1,0:T(8,128)S(1)} %pad_maximum_fusion.1.block), channel_id=1, source_target_pairs={{0,1},{1,0},{2,3},{3,2},{4,5},{5,4},{6,7},{7,6},{8,9},{9,8},{10,11... | collective-permute-start | bytes 393224 | tf_op jit(solution)/shard_map/ppermute | solution.py:30
  33.7 12.0 %collective-permute-start.7 = (f32[11,16,256]{2,1,0:T(8,128)S(1)}, f32[11,16,256]{2,1,0:T(8,128)S(1)}, u32[]{:S(2)}, u32[]{:S(2)}) collective-permute-start(f32[11,16,256]{2,1,0:T(8,128)S(1)} %pad_maximum_fusion), channel_id=1, source_target_pairs={{1,2},{2,1},{3,4},{4,3},{5,6},{6,5},{7,8},{8,7},{9,10},{10,9},{11,... | collective-permute-start | bytes 540680 | tf_op jit(solution)/shard_map/ppermute | solution.py:30
  45.8 1.2 %collective-permute-start.8 = (f32[3,16,256]{2,1,0:T(8,128)S(1)}, f32[3,16,256]{2,1,0:T(8,128)S(1)}, u32[]{:S(2)}, u32[]{:S(2)}) collective-permute-start(f32[3,16,256]{2,1,0:T(8,128)S(1)} %slice.29), channel_id=1, source_target_pairs={{0,1},{1,0},{2,3},{3,2},{4,5},{5,4},{6,7},{7,6},{8,9},{9,8},{10,11... | collective-permute-start | bytes 147464 | tf_op jit(solution)/shard_map/ppermute | solution.py:30

commit v7 on v6

--- a/solution.py
+++ b/solution.py
@@ -46,6 +46,14 @@
     def move(y, zh, x, zl, core):
         q = x * 4 + zl + (1 if core == 1 else -1)
         return (y, zh, q // 4, q % 4, 1 - core) if 0 <= q < 16 else None
+
+    return send(v, move)
+
+
+def send_chip(v):
+    def move(y, zh, x, zl, core):
+        q = x * 4 + zl + (1 if core == 0 else -1)
+        return (y, zh, q // 4, q % 4, core) if 0 <= q < 16 else None
 
     return send(v, move)
 
@@ -116,7 +124,7 @@
         out[12, x * 4 + 2 : x * 4 + 4, :] = above
 
 
-def krylov_kernel(block, mate, far, beyond, basis, moments, w0, w1, w2, sh):
+def krylov_kernel(block, mate, far, farther, beyond, basis, moments, w0, w1, w2, sh):
     core = lax.axis_index("core")
     inst = lax.axis_index("y") * 2 + lax.axis_index("zh")
     cell = lax.axis_index("x") * 8 + lax.axis_index("zl") * 2 + core
@@ -126,7 +134,7 @@
 
     for k in range(3):
         line = (
-            far[8 + k], far[k], far[3 + k], block[3 + k],
+            farther[k], far[k], far[3 + k], block[3 + k],
             block[k], mate[k], mate[3 + k], beyond[k],
         )
         for x in range(8):
@@ -303,15 +311,16 @@
     ends = [jnp.zeros((2, n, 256), F32) for n in (1, 3)]
     wider = jnp.concatenate([ends[0], sides[:, :2], shift, sides[:, 2:], ends[1]], axis=1)
     block = jnp.concatenate([(own + got[:12]).reshape(6, 16, 256), wider], axis=0)
+    far = send_pair(block)
+    farther = send_chip(block[:3])
     mate = send_core(block)
-    far = send_pair(jnp.concatenate([block, mate[:3]], axis=0))
     beyond = send_core(far[3:6])
 
     scratch = pltpu.VMEM((3, 8, 16, 256), F32)
     basis, moments = call(
         krylov_kernel,
         [(4, 3, 2, 8, 256), (8, 128)],
-        (block, mate, far, beyond),
+        (block, mate, far, farther, beyond),
         [scratch, scratch, scratch, pltpu.VMEM((8, 16, 256), F32)],
     )
     parts = lax.all_to_all(jnp.broadcast_to(moments, (16, 8, 128)), ("y", "x"), 0, 0)

time: 81.4 us -> 81.8 us (level)
  waiting for transfers between devices: 21 us -> 19.4 us
  starting transfers between devices: 21.7 us -> 23 us
    all_to_all x1, blocking collectives: 15 us -> 17.6 us  [local(): lax.all_to_all(jnp.broadcast_to(moments, (16, 8, 128)), ('zh', 'zl', 'cor...]
    all_to_all x1, blocking collectives: 16.9 us -> 15.1 us  [local(): lax.all_to_all(jnp.broadcast_to(moments, (16, 8, 128)), ('y', 'x'), 0, 0)]
    ppermute x9 -> x10, waiting for transfers between devices: 21 us -> 19.4 us  [send(): return lax.ppermute(v, AXES, pairs)]
    ppermute x9 -> x10, starting transfers between devices: 21.7 us -> 23 us  [send(): return lax.ppermute(v, AXES, pairs)]
  transfers between devices with their start and end apart: 9 -> 10, of which waited for: 7 -> 6; matrix products, arithmetic and copies ran while one was open for 0% -> 0% of each run, Pallas kernels for 0% -> 0%
where the time goes in v7:
time: 81.8 us; the launch traced here: 81.5 us
  blocking collectives  32.7 us (40%)
  starting transfers between devices  23 us (28%)
  waiting for transfers between devices  19.4 us (24%)
  local copies, waits for them, and re-layouts  2.86 us (3%)
  Pallas kernels  2.81 us (3%)
    ppermute x10, starting transfers between devices, send(): return lax.ppermute(v, AXES, pairs)  23 us
    ppermute x10, waiting for transfers between devices, send(): return lax.ppermute(v, AXES, pairs)  19.4 us
    all_to_all x1, blocking collectives, local(): lax.all_to_all(jnp.broadcast_to(moments, (16, 8, 128)), ('zh', 'zl', 'cor...  17.6 us
    all_to_all x1, blocking collectives, local(): lax.all_to_all(jnp.broadcast_to(moments, (16, 8, 128)), ('y', 'x'), 0, 0)  15.1 us
    pallas_call x5, Pallas kernels, call(): pl.pallas_call(kernel, out_shape=[jax.ShapeDtypeStruct(s, F32) for s in o...  2.81 us
  transfers between devices with their start and end apart: 10, of which 6 were waited for; matrix products, arithmetic and copies ran while one was open for 0% of the time, Pallas kernels for 0%

profile of v7, /device:TPU:1, one launch (start us, length us, event | category | flops | bytes accessed | tf_op | source)
XLA Modules:
  0.0 81.5 jit_solution(15158027669619436172)
XLA Ops:
  0.6 0.0 copy-start.1
  0.6 1.1 %dynamic-slice_bitcast_fusion = (bf16[2,5,64,256]{3,2,1,0:T(8,128)(2,1)S(1)}, bf16[2,5,64,256]{3,2,1,0:T(8,128)(2,1)S(1)}) fusion(bf16[2,5,2,64,256]{4,3,2,1,0:T(8,128)(2,1)} %param.3, s32[]{:T(128)S(6)} %select_n.8, s32[]{:T(128)S(6)} %select_n.7), kind=kLoop, calls=%fused_computation | loop fusion | bytes 1310728 | tf_op jit(solution)/shard_map/jit(dynamic_index_in_dim)/squeeze | solution.py:293
  1.8 3.3 %collective-permute-start.1 = (bf16[2,5,64,256]{3,2,1,0:T(8,128)(2,1)S(1)}, bf16[2,5,64,256]{3,2,1,0:T(8,128)(2,1)S(1)}, u32[]{:S(2)}, u32[]{:S(2)}) collective-permute-start(bf16[2,5,64,256]{3,2,1,0:T(8,128)(2,1)S(1)} %get-tuple-element.19.a), channel_id=1, source_target_pairs={{0,1},{1,0},{2,3},{3,2},{4,5},{5,4},{6,7},{7,6},{8,9},{9,8},{10,11... | collective-permute-start | bytes 983048 | tf_op jit(solution)/shard_map/ppermute | solution.py:30
  5.1 1.9 %collective-permute-start = (bf16[2,5,64,256]{3,2,1,0:T(8,128)(2,1)S(1)}, bf16[2,5,64,256]{3,2,1,0:T(8,128)(2,1)S(1)}, u32[]{:S(2)}, u32[]{:S(2)}) collective-permute-start(bf16[2,5,64,256]{3,2,1,0:T(8,128)(2,1)S(1)} %get-tuple-element.18.a), channel_id=1, source_target_pairs={{1,2},{2,1},{3,4},{4,3},{5,6},{6,5},{7,8},{8,7},{9,10},{10,9},{11,... | collective-permute-start | bytes 983048 | tf_op jit(solution)/shard_map/ppermute | solution.py:30
  7.0 0.0 collective-permute-done.1.got
  7.0 0.0 copy-start
  7.0 1.5 %copy-done = bf16[2,5,3,2,64,256]{5,4,3,2,1,0:T(8,128)(2,1)S(1)} copy-done((bf16[2,5,3,2,64,256]{5,4,3,2,1,0:T(8,128)(2,1)S(1)}, bf16[2,5,3,2,64,256]{5,4,3,2,1,0:T(8,128)(2,1)}, u32[]{:S(2)}) %copy-start) | copy-done | bytes 1966104
  8.6 0.3 shard_map.50.early
  8.9 8.1 %collective-permute-done.got = bf16[2,5,64,256]{3,2,1,0:T(8,128)(2,1)S(1)} collective-permute-done((bf16[2,5,64,256]{3,2,1,0:T(8,128)(2,1)S(1)}, bf16[2,5,64,256]{3,2,1,0:T(8,128)(2,1)S(1)}, u32[]{:S(2)}, u32[]{:S(2)}) %collective-permute-start) | collective-permute-done | bytes 327712 | tf_op jit(solution)/shard_map/ppermute | solution.py:30
  17.0 0.0 copy-done.1
  17.0 0.3 shard_map.51
  17.3 0.1 collective-permute-start.2
  17.4 0.1 collective-permute-start.3
  17.5 2.7 %collective-permute-start.4 = (f32[19,8,256]{2,1,0:T(8,128)S(1)}, f32[19,8,256]{2,1,0:T(8,128)S(1)}, u32[]{:S(2)}, u32[]{:S(2)}) collective-permute-start(f32[19,8,256]{2,1,0:T(8,128)S(1)} %get-tuple-element.13), channel_id=1, source_target_pairs={{0,192},{1,193},{2,194},{3,195},{4,196},{5,197},{6,198},{7,199},{8... | collective-permute-start | bytes 466952 | tf_op jit(solution)/shard_map/ppermute | solution.py:30
  20.1 2.9 %collective-permute-done.2.r2 = f32[19,8,256]{2,1,0:T(8,128)S(1)} collective-permute-done((f32[19,8,256]{2,1,0:T(8,128)S(1)}, f32[19,8,256]{2,1,0:T(8,128)S(1)}, u32[]{:S(2)}, u32[]{:S(2)}) %collective-permute-start.2) | collective-permute-done | bytes 155680 | tf_op jit(solution)/shard_map/ppermute | solution.py:30
  23.1 1.4 %collective-permute-done.3.r1 = f32[19,8,256]{2,1,0:T(8,128)S(1)} collective-permute-done((f32[19,8,256]{2,1,0:T(8,128)S(1)}, f32[19,8,256]{2,1,0:T(8,128)S(1)}, u32[]{:S(2)}, u32[]{:S(2)}) %collective-permute-start.3) | collective-permute-done | bytes 155680 | tf_op jit(solution)/shard_map/ppermute | solution.py:30
  24.4 0.0 collective-permute-done.4.r3
  24.4 0.1 shard_map.52
  24.5 4.6 %collective-permute-start.5 = (f32[13,8,256]{2,1,0:T(8,128)S(1)}, f32[13,8,256]{2,1,0:T(8,128)S(1)}, u32[]{:S(2)}, u32[]{:S(2)}) collective-permute-start(f32[13,8,256]{2,1,0:T(8,128)S(1)} %get-tuple-element.15), channel_id=1, source_target_pairs={{0,32},{1,33},{2,34},{3,35},{4,36},{5,37},{6,38},{7,39},{8,40},{9,... | collective-permute-start | bytes 319496 | tf_op jit(solution)/shard_map/ppermute | solution.py:30
  29.1 2.9 %collective-permute-done.5 = f32[13,8,256]{2,1,0:T(8,128)S(1)} collective-permute-done((f32[13,8,256]{2,1,0:T(8,128)S(1)}, f32[13,8,256]{2,1,0:T(8,128)S(1)}, u32[]{:S(2)}, u32[]{:S(2)}) %collective-permute-start.5) | collective-permute-done | bytes 106528 | tf_op jit(solution)/shard_map/ppermute | solution.py:30
  32.1 0.1 concatenate.6
  32.2 8.9 %collective-permute-start.7 = (f32[8,16,256]{2,1,0:T(8,128)S(1)}, f32[8,16,256]{2,1,0:T(8,128)S(1)}, u32[]{:S(2)}, u32[]{:S(2)}) collective-permute-start(f32[8,16,256]{2,1,0:T(8,128)S(1)} %pad_maximum_fusion.block), channel_id=1, source_target_pairs={{1,2},{2,1},{3,4},{4,3},{5,6},{6,5},{7,8},{8,7},{9,10},{10,9},{11,... | collective-permute-start | bytes 393224 | tf_op jit(solution)/shard_map/ppermute | solution.py:30
  41.1 0.1 collective-permute-start.6
  41.2 1.3 %collective-permute-start.8 = (f32[3,16,256]{2,1,0:T(8,128)S(1)}, f32[3,16,256]{2,1,0:T(8,128)S(1)}, u32[]{:S(2)}, u32[]{:S(2)}) collective-permute-start(f32[3,16,256]{2,1,0:T(8,128)S(1)} %bitcast.7), channel_id=1, source_target_pairs={{0,2},{2,4},{3,1},{4,6},{5,3},{6,8},{7,5},{8,10},{9,7},{10,12},{11... | collective-permute-start | bytes 147464 | tf_op jit(solution)/shard_map/ppermute | solution.py:30
  42.5 1.2 %collective-permute-done.7.far = f32[8,16,256]{2,1,0:T(8,128)S(1)} collective-permute-done((f32[8,16,256]{2,1,0:T(8,128)S(1)}, f32[8,16,256]{2,1,0:T(8,128)S(1)}, u32[]{:S(2)}, u32[]{:S(2)}) %collective-permute-start.7) | collective-permute-done | bytes 131104 | tf_op jit(solution)/shard_map/ppermute | solution.py:30
  43.8 0.0 collective-permute-start.9
  43.8 2.8 %collective-permute-done.8.farther = f32[3,16,256]{2,1,0:T(8,128)S(1)} collective-permute-done((f32[3,16,256]{2,1,0:T(8,128)S(1)}, f32[3,16,256]{2,1,0:T(8,128)S(1)}, u32[]{:S(2)}, u32[]{:S(2)}) %collective-permute-start.8) | collective-permute-done | bytes 49184 | tf_op jit(solution)/shard_map/ppermute | solution.py:30
  46.6 0.0 collective-permute-done.6.mate
  46.6 0.0 collective-permute-done.9.beyond
  46.6 0.9 %shard_map.53 = (f32[4,3,2,8,256]{4,3,2,1,0:T(8,128)S(1)}, f32[8,128]{1,0:T(8,128)S(1)}) custom-call(f32[8,16,256]{2,1,0:T(8,128)S(1)} %pad_maximum_fusion.block, f32[8,16,256]{2,1,0:T(8,128)S(1)} %collective-permute-done.6.mate, f32[8,16,256]{2,1,0:T(8,128)S(1)} %collective-permute-done.7.far, f32[3,16,256]{2,1,0:T(8,128)S(1)} %collective-permute-done.8.farther, ...), custom_call_target="tpu_custom_call" | custom-call | tf_op jit(solution)/shard_map/pallas_call | solution.py:65
  47.5 15.1 %all_to_all.10 = f32[16,8,128]{2,1,0:T(8,128)S(1)} all-to-all(f32[16,8,128]{2,1,0:T(8,128)S(1)} %broadcast_in_dim.14), channel_id=1, replica_groups=mesh['y'=4,'zh'=2,'x'=4,'zl'=4,'core'=2] {'y','x'}, dimensions={0} | all-to-all | bytes 131072 | tf_op jit(solution)/shard_map/all_to_all | solution.py:326
  62.7 17.6 %all_to_all.11.parts = f32[16,8,128]{2,1,0:T(8,128)S(1)} all-to-all(f32[16,8,128]{2,1,0:T(8,128)S(1)} %broadcast_in_dim.15), channel_id=1, replica_groups=mesh['y'=4,'zh'=2,'x'=4,'zl'=4,'core'=2] {'zh','zl','core'}, dimensions={0} | all-to-all | bytes 131072 | tf_op jit(solution)/shard_map/all_to_all | solution.py:328
  80.2 1.3 %shard_map.54 = (f32[3,2,8,256]{3,2,1,0:T(8,128)}, f32[3,2,8,256]{3,2,1,0:T(8,128)}) custom-call(f32[16,8,128]{2,1,0:T(8,128)S(1)} %all_to_all.11.parts, f32[4,3,2,8,256]{4,3,2,1,0:T(8,128)S(1)} %get-tuple-element.17.basis), custom_call_target="tpu_custom_call" | custom-call | tf_op jit(solution)/shard_map/pallas_call | solution.py:65
  (12 shorter events, 0.1 us)
Async XLA Ops:
  0.6 16.3 %copy-start.1 = (f32[2,8,256]{2,1,0:T(8,128)S(1)}, f32[2,8,256]{2,1,0:T(8,128)}, u32[]{:S(2)}) copy-start(f32[2,8,256]{2,1,0:T(8,128)} %shift.3) | copy-start | bytes 49156
  1.8 5.2 %collective-permute-start.1 = (bf16[2,5,64,256]{3,2,1,0:T(8,128)(2,1)S(1)}, bf16[2,5,64,256]{3,2,1,0:T(8,128)(2,1)S(1)}, u32[]{:S(2)}, u32[]{:S(2)}) collective-permute-start(bf16[2,5,64,256]{3,2,1,0:T(8,128)(2,1)S(1)} %get-tuple-element.19.a), channel_id=1, source_target_pairs={{0,1},{1,0},{2,3},{3,2},{4,5},{5,4},{6,7},{7,6},{8,9},{9,8},{10,11... | collective-permute-start | bytes 983048 | tf_op jit(solution)/shard_map/ppermute | solution.py:30
  5.1 11.9 %collective-permute-start = (bf16[2,5,64,256]{3,2,1,0:T(8,128)(2,1)S(1)}, bf16[2,5,64,256]{3,2,1,0:T(8,128)(2,1)S(1)}, u32[]{:S(2)}, u32[]{:S(2)}) collective-permute-start(bf16[2,5,64,256]{3,2,1,0:T(8,128)(2,1)S(1)} %get-tuple-element.18.a), channel_id=1, source_target_pairs={{1,2},{2,1},{3,4},{4,3},{5,6},{6,5},{7,8},{8,7},{9,10},{10,9},{11,... | collective-permute-start | bytes 983048 | tf_op jit(solution)/shard_map/ppermute | solution.py:30
  7.0 1.5 %copy-start = (bf16[2,5,3,2,64,256]{5,4,3,2,1,0:T(8,128)(2,1)S(1)}, bf16[2,5,3,2,64,256]{5,4,3,2,1,0:T(8,128)(2,1)}, u32[]{:S(2)}) copy-start(bf16[2,5,3,2,64,256]{5,4,3,2,1,0:T(8,128)(2,1)} %f.3) | copy-start | bytes 5898244
  17.3 5.8 %collective-permute-start.2 = (f32[19,8,256]{2,1,0:T(8,128)S(1)}, f32[19,8,256]{2,1,0:T(8,128)S(1)}, u32[]{:S(2)}, u32[]{:S(2)}) collective-permute-start(f32[19,8,256]{2,1,0:T(8,128)S(1)} %get-tuple-element.11), channel_id=1, source_target_pairs={{0,128},{1,129},{2,130},{3,131},{4,132},{5,133},{6,134},{7,135},{8... | collective-permute-start | bytes 466952 | tf_op jit(solution)/shard_map/ppermute | solution.py:30
  17.4 7.0 %collective-permute-start.3 = (f32[19,8,256]{2,1,0:T(8,128)S(1)}, f32[19,8,256]{2,1,0:T(8,128)S(1)}, u32[]{:S(2)}, u32[]{:S(2)}) collective-permute-start(f32[19,8,256]{2,1,0:T(8,128)S(1)} %get-tuple-element.12), channel_id=1, source_target_pairs={{0,64},{1,65},{2,66},{3,67},{4,68},{5,69},{6,70},{7,71},{8,72},{9,... | collective-permute-start | bytes 466952 | tf_op jit(solution)/shard_map/ppermute | solution.py:30
  17.5 6.9 %collective-permute-start.4 = (f32[19,8,256]{2,1,0:T(8,128)S(1)}, f32[19,8,256]{2,1,0:T(8,128)S(1)}, u32[]{:S(2)}, u32[]{:S(2)}) collective-permute-start(f32[19,8,256]{2,1,0:T(8,128)S(1)} %get-tuple-element.13), channel_id=1, source_target_pairs={{0,192},{1,193},{2,194},{3,195},{4,196},{5,197},{6,198},{7,199},{8... | collective-permute-start | bytes 466952 | tf_op jit(solution)/shard_map/ppermute | solution.py:30
  24.5 7.5 %collective-permute-start.5 = (f32[13,8,256]{2,1,0:T(8,128)S(1)}, f32[13,8,256]{2,1,0:T(8,128)S(1)}, u32[]{:S(2)}, u32[]{:S(2)}) collective-permute-start(f32[13,8,256]{2,1,0:T(8,128)S(1)} %get-tuple-element.15), channel_id=1, source_target_pairs={{0,32},{1,33},{2,34},{3,35},{4,36},{5,37},{6,38},{7,39},{8,40},{9,... | collective-permute-start | bytes 319496 | tf_op jit(solution)/shard_map/ppermute | solution.py:30
  32.2 11.5 %collective-permute-start.7 = (f32[8,16,256]{2,1,0:T(8,128)S(1)}, f32[8,16,256]{2,1,0:T(8,128)S(1)}, u32[]{:S(2)}, u32[]{:S(2)}) collective-permute-start(f32[8,16,256]{2,1,0:T(8,128)S(1)} %pad_maximum_fusion.block), channel_id=1, source_target_pairs={{1,2},{2,1},{3,4},{4,3},{5,6},{6,5},{7,8},{8,7},{9,10},{10,9},{11,... | collective-permute-start | bytes 393224 | tf_op jit(solution)/shard_map/ppermute | solution.py:30
  41.1 5.5 %collective-permute-start.6 = (f32[8,16,256]{2,1,0:T(8,128)S(1)}, f32[8,16,256]{2,1,0:T(8,128)S(1)}, u32[]{:S(2)}, u32[]{:S(2)}) collective-permute-start(f32[8,16,256]{2,1,0:T(8,128)S(1)} %pad_maximum_fusion.block), channel_id=1, source_target_pairs={{0,1},{1,0},{2,3},{3,2},{4,5},{5,4},{6,7},{7,6},{8,9},{9,8},{10,11... | collective-permute-start | bytes 393224 | tf_op jit(solution)/shard_map/ppermute | solution.py:30
  41.2 5.4 %collective-permute-start.8 = (f32[3,16,256]{2,1,0:T(8,128)S(1)}, f32[3,16,256]{2,1,0:T(8,128)S(1)}, u32[]{:S(2)}, u32[]{:S(2)}) collective-permute-start(f32[3,16,256]{2,1,0:T(8,128)S(1)} %bitcast.7), channel_id=1, source_target_pairs={{0,2},{2,4},{3,1},{4,6},{5,3},{6,8},{7,5},{8,10},{9,7},{10,12},{11... | collective-permute-start | bytes 147464 | tf_op jit(solution)/shard_map/ppermute | solution.py:30
  43.8 2.8 %collective-permute-start.9 = (f32[3,16,256]{2,1,0:T(8,128)S(1)}, f32[3,16,256]{2,1,0:T(8,128)S(1)}, u32[]{:S(2)}, u32[]{:S(2)}) collective-permute-start(f32[3,16,256]{2,1,0:T(8,128)S(1)} %slice.33), channel_id=1, source_target_pairs={{0,1},{1,0},{2,3},{3,2},{4,5},{5,4},{6,7},{7,6},{8,9},{9,8},{10,11... | collective-permute-start | bytes 147464 | tf_op jit(solution)/shard_map/ppermute | solution.py:30

commit v8 on v5

--- a/solution.py
+++ b/solution.py
@@ -82,36 +82,52 @@
             wide[k, rows + 3 : rows + 19, :] = total[k] * sign
 
 
-def sens_early_kernel(f, a, got, wide):
+def cut(y, wide, outs):
+    for d, out in enumerate(outs):
+        first = pl.multiple_of(lax.rem(y + d, 4) * 16, 16)
+        for k in range(3):
+            out[k * 3 : k * 3 + 3] = wide[k, pl.ds(first, 24), :].reshape(3, 8, 256)
+
+
+def sens_early_kernel(f, a, got, shift, m0, m1, m2, m3, wide):
     core = lax.axis_index("core")
     sens_of_slab(1 - core, jnp.where(core == 0, 1.0, -1.0), f, a, got, wide)
-
-
-def sens_late_kernel(f, a, got, early, shift, m0, m1, m2, m3, wide):
-    y, core = lax.axis_index("y"), lax.axis_index("core")
+    cut(lax.axis_index("y"), wide, (m0, m1, m2, m3))
+    for out, span in ((m1, slice(6, 8)), (m2, slice(6, 8)), (m3, slice(0, 2))):
+        for x in range(2):
+            out[9, x * 2 : x * 2 + 2, :] = shift[x, span, :]
+        out[9, 4:8, :] = jnp.zeros((4, 256), F32)
+
+
+def sens_late_kernel(f, a, got, after, m0, m1, m2, m3, wide):
+    core = lax.axis_index("core")
     sens_of_slab(core, jnp.where(core == 0, -1.0, 1.0), f, a, got, wide)
-    for d, out in enumerate((m0, m1, m2, m3)):
-        first = pl.multiple_of(lax.rem(y + d, 4) * 16, 16)
-        for k in range(3):
-            out[k * 3 : k * 3 + 3] = early[k, pl.ds(first, 24), :].reshape(3, 8, 256)
-            out[9 + k * 3 : 12 + k * 3] = wide[k, pl.ds(first, 24), :].reshape(3, 8, 256)
-    for out in (m1, m3):
-        out[18:20] = shift[...]
-
-
-def sum_y_kernel(m0, r1, r2, r3, shift, own, out):
+    cut(lax.axis_index("y"), wide, (m0, m1, m2, m3))
+
+
+def sum_y(m0, r2, r1, r3, own, out):
     zh = lax.axis_index("zh")
-    for s in range(6):
+    for s in range(3):
         for g in range(2):
             for half, to in ((zh, own), (1 - zh, out)):
                 k = s * 3 + half + g
                 to[s * 2 + g] = (m0[k] + r1[k]) + (r2[k] + r3[k])
-    low = zh == 0
+
+
+def sum_y_early_kernel(m0, r2, r1, r3, shift, after, own, out):
+    sum_y(m0, r2, r1, r3, own, out)
+    low = lax.axis_index("zh") == 0
     for x in range(2):
-        below = jnp.where(low, shift[x, 6:8, :], r1[18 + x, 6:8, :])
-        above = jnp.where(low, r3[18 + x, 0:2, :], shift[x, 0:2, :])
-        out[12, x * 4 : x * 4 + 2, :] = below
-        out[12, x * 4 + 2 : x * 4 + 4, :] = above
+        below = jnp.where(low, shift[x, 6:8, :], r1[9, x * 2 : x * 2 + 2, :])
+        above = jnp.where(low, r3[9, x * 2 : x * 2 + 2, :], shift[x, 0:2, :])
+        out[6, x * 4 : x * 4 + 2, :] = below
+        out[6, x * 4 + 2 : x * 4 + 4, :] = above
+
+
+def sum_y_late_kernel(m0, r2, r1, r3, own_early, out_early, own, out):
+    sum_y(m0, r2, r1, r3, own, out)
+    own[6:12] = own_early[...]
+    out[6:13] = out_early[...]
 
 
 def krylov_kernel(block, mate, far, beyond, basis, moments, w0, w1, w2, sh):
@@ -124,8 +140,8 @@
 
     for k in range(3):
         line = (
-            far[8 + k], far[k], far[3 + k], block[3 + k],
-            block[k], mate[k], mate[3 + k], beyond[k],
+            far[8 + k], far[3 + k], far[k], block[k],
+            block[3 + k], mate[3 + k], mate[k], beyond[k],
         )
         for x in range(8):
             w0[k, place(x)] = line[x]
@@ -285,25 +301,24 @@
     got_outer = send_pair(outer)
     got_inner = send_core(inner)
 
-    rows = (3, 72, 256)
-    (early,) = call(sens_early_kernel, [rows], (flux_jac, outer, got_inner))
-    eight, ten = (18, 8, 256), (20, 8, 256)
+    six, nine, ten = (6, 8, 256), (9, 8, 256), (10, 8, 256)
+    wide = [pltpu.VMEM((3, 72, 256), F32)]
     m0, m1, m2, m3 = call(
-        sens_late_kernel,
-        [eight, ten, eight, ten],
-        (flux_jac, inner, got_outer, early, shift),
-        [pltpu.VMEM(rows, F32)],
+        sens_early_kernel, [nine, ten, ten, ten], (flux_jac, outer, got_inner, shift), wide
     )
     r2, r1, r3 = send_y(m2, 2), send_y(m1, 1), send_y(m3, 3)
-    own, out = call(sum_y_kernel, [(12, 8, 256), (13, 8, 256)], (m0, r1, r2, r3, shift))
+    n0, n1, n2, n3 = call(sens_late_kernel, [nine] * 4, (flux_jac, inner, got_outer, m0), wide)
+    q2, q1, q3 = send_y(n2, 2), send_y(n1, 1), send_y(n3, 3)
+    own, out = call(sum_y_early_kernel, [six, (7, 8, 256)], (m0, r2, r1, r3, shift, n0))
+    own, out = call(sum_y_late_kernel, [(12, 8, 256), (13, 8, 256)], (n0, q2, q1, q3, own, out))
     got = send_zh(out)
     sides = got[12].reshape(2, 4, 256)
     ends = [jnp.zeros((2, n, 256), F32) for n in (1, 3)]
     wider = jnp.concatenate([ends[0], sides[:, :2], shift, sides[:, 2:], ends[1]], axis=1)
     block = jnp.concatenate([(own + got[:12]).reshape(6, 16, 256), wider], axis=0)
     mate = send_core(block)
-    far = send_pair(jnp.concatenate([block, mate[:3]], axis=0))
-    beyond = send_core(far[3:6])
+    far = send_pair(jnp.concatenate([block, mate[3:6]], axis=0))
+    beyond = send_core(far[:3])
 
     scratch = pltpu.VMEM((3, 8, 16, 256), F32)
     basis, moments = call(
@@ -312,9 +327,9 @@
         (block, mate, far, beyond),
         [scratch, scratch, scratch, pltpu.VMEM((8, 16, 256), F32)],
     )
+    parts = lax.all_to_all(jnp.broadcast_to(moments, (16, 8, 128)), ("zh", "zl", "core"), 0, 0)
+    moments = jnp.sum(parts, axis=0)
     parts = lax.all_to_all(jnp.broadcast_to(moments, (16, 8, 128)), ("y", "x"), 0, 0)
-    moments = jnp.sum(parts, axis=0)
-    parts = lax.all_to_all(jnp.broadcast_to(moments, (16, 8, 128)), ("zh", "zl", "core"), 0, 0)
     shape = (3, 2, 8, 256)
     return tuple(call(finish_kernel, [shape, shape], (parts, basis)))
 

time: 81.2 us -> 78.9 us (0.972)
  waiting for transfers between devices: 23.4 us -> 12.6 us
  starting transfers between devices: 16.7 us -> 24.4 us
    ppermute x9 -> x12, waiting for transfers between devices: 23.4 us -> 12.6 us  [send(): return lax.ppermute(v, AXES, pairs)]
    ppermute x9 -> x12, starting transfers between devices: 16.7 us -> 24.4 us  [send(): return lax.ppermute(v, AXES, pairs)]
    all_to_all x1, blocking collectives: 18.8 us -> 14.7 us  [local(): lax.all_to_all(jnp.broadcast_to(moments, (16, 8, 128)), ('y', 'x'), 0, 0)]
    all_to_all x1, blocking collectives: 15.5 us -> 19.6 us  [local(): lax.all_to_all(jnp.broadcast_to(moments, (16, 8, 128)), ('zh', 'zl', 'cor...]
    unnamed x4 -> x6, local copies, waits for them, and re-layouts: 1.54 us -> 2.26 us
    pallas_call x5 -> x6, Pallas kernels: 2.81 us -> 2.83 us  [call(): pl.pallas_call(kernel, out_shape=[jax.ShapeDtypeStruct(s, F32) for s in o...]
  transfers between devices with their start and end apart: 9 -> 12, of which waited for: 6 -> 7; matrix products, arithmetic and copies ran while one was open for 0% -> 0% of each run, Pallas kernels for 0% -> 1%
where the time goes in v8:
time: 78.9 us; the launch traced here: 78.6 us
  blocking collectives  34.3 us (43%)
  starting transfers between devices  24.4 us (31%)
  waiting for transfers between devices  12.6 us (16%)
  local copies, waits for them, and re-layouts  3.58 us (5%)
  Pallas kernels  2.83 us (4%)
    ppermute x12, starting transfers between devices, send(): return lax.ppermute(v, AXES, pairs)  24.4 us
    all_to_all x1, blocking collectives, local(): lax.all_to_all(jnp.broadcast_to(moments, (16, 8, 128)), ('zh', 'zl', 'cor...  19.6 us
    all_to_all x1, blocking collectives, local(): lax.all_to_all(jnp.broadcast_to(moments, (16, 8, 128)), ('y', 'x'), 0, 0)  14.7 us
    ppermute x12, waiting for transfers between devices, send(): return lax.ppermute(v, AXES, pairs)  12.6 us
    pallas_call x6, Pallas kernels, call(): pl.pallas_call(kernel, out_shape=[jax.ShapeDtypeStruct(s, F32) for s in o...  2.83 us
    unnamed x6, local copies, waits for them, and re-layouts  2.26 us
  transfers between devices with their start and end apart: 12, of which 7 were waited for; matrix products, arithmetic and copies ran while one was open for 0% of the time, Pallas kernels for 1%

profile of v8, /device:TPU:1, one launch (start us, length us, event | category | flops | bytes accessed | tf_op | source)
XLA Modules:
  0.0 78.6 jit_solution(16443796335249042388)
XLA Ops:
  0.6 1.1 %dynamic-slice_bitcast_fusion = (bf16[2,5,64,256]{3,2,1,0:T(8,128)(2,1)S(1)}, bf16[2,5,64,256]{3,2,1,0:T(8,128)(2,1)S(1)}) fusion(bf16[2,5,2,64,256]{4,3,2,1,0:T(8,128)(2,1)} %param.3, s32[]{:T(128)S(6)} %select_n.8, s32[]{:T(128)S(6)} %select_n.7), kind=kLoop, calls=%fused_computation | loop fusion | bytes 1310728 | tf_op jit(solution)/shard_map/jit(dynamic_index_in_dim)/squeeze | solution.py:299
  1.8 3.3 %collective-permute-start.1 = (bf16[2,5,64,256]{3,2,1,0:T(8,128)(2,1)S(1)}, bf16[2,5,64,256]{3,2,1,0:T(8,128)(2,1)S(1)}, u32[]{:S(2)}, u32[]{:S(2)}) collective-permute-start(bf16[2,5,64,256]{3,2,1,0:T(8,128)(2,1)S(1)} %get-tuple-element.31.a), channel_id=1, source_target_pairs={{0,1},{1,0},{2,3},{3,2},{4,5},{5,4},{6,7},{7,6},{8,9},{9,8},{10,11... | collective-permute-start | bytes 983048 | tf_op jit(solution)/shard_map/ppermute | solution.py:30
  5.1 1.9 %collective-permute-start = (bf16[2,5,64,256]{3,2,1,0:T(8,128)(2,1)S(1)}, bf16[2,5,64,256]{3,2,1,0:T(8,128)(2,1)S(1)}, u32[]{:S(2)}, u32[]{:S(2)}) collective-permute-start(bf16[2,5,64,256]{3,2,1,0:T(8,128)(2,1)S(1)} %get-tuple-element.30.a), channel_id=1, source_target_pairs={{1,2},{2,1},{3,4},{4,3},{5,6},{6,5},{7,8},{8,7},{9,10},{10,9},{11,... | collective-permute-start | bytes 983048 | tf_op jit(solution)/shard_map/ppermute | solution.py:30
  7.0 0.0 collective-permute-done.1.got
  7.0 0.0 copy-start
  7.0 1.5 %copy-done = bf16[2,5,3,2,64,256]{5,4,3,2,1,0:T(8,128)(2,1)S(1)} copy-done((bf16[2,5,3,2,64,256]{5,4,3,2,1,0:T(8,128)(2,1)S(1)}, bf16[2,5,3,2,64,256]{5,4,3,2,1,0:T(8,128)(2,1)}, u32[]{:S(2)}) %copy-start) | copy-done | bytes 1966104
  8.6 0.0 copy-start.1
  8.6 0.7 copy-done.1
  9.3 0.3 shard_map.50
  9.6 0.0 copy-start.2
  9.6 2.8 %collective-permute-start.5 = (f32[10,8,256]{2,1,0:T(8,128)S(1)}, f32[10,8,256]{2,1,0:T(8,128)S(1)}, u32[]{:S(2)}, u32[]{:S(2)}) collective-permute-start(f32[10,8,256]{2,1,0:T(8,128)S(1)} %get-tuple-element.21), channel_id=1, source_target_pairs={{0,128},{1,129},{2,130},{3,131},{4,132},{5,133},{6,134},{7,135},{8... | collective-permute-start | bytes 245768 | tf_op jit(solution)/shard_map/ppermute | solution.py:30
  12.4 0.4 collective-permute-start.6
  12.8 2.3 %collective-permute-start.7 = (f32[10,8,256]{2,1,0:T(8,128)S(1)}, f32[10,8,256]{2,1,0:T(8,128)S(1)}, u32[]{:S(2)}, u32[]{:S(2)}) collective-permute-start(f32[10,8,256]{2,1,0:T(8,128)S(1)} %get-tuple-element.23), channel_id=1, source_target_pairs={{0,192},{1,193},{2,194},{3,195},{4,196},{5,197},{6,198},{7,199},{8... | collective-permute-start | bytes 245768 | tf_op jit(solution)/shard_map/ppermute | solution.py:30
  15.1 1.7 %collective-permute-done.got = bf16[2,5,64,256]{3,2,1,0:T(8,128)(2,1)S(1)} collective-permute-done((bf16[2,5,64,256]{3,2,1,0:T(8,128)(2,1)S(1)}, bf16[2,5,64,256]{3,2,1,0:T(8,128)(2,1)S(1)}, u32[]{:S(2)}, u32[]{:S(2)}) %collective-permute-start) | collective-permute-done | bytes 327712 | tf_op jit(solution)/shard_map/ppermute | solution.py:30
  16.7 0.3 shard_map.51
  17.0 0.1 collective-permute-start.2
  17.1 0.1 collective-permute-start.3
  17.2 0.0 collective-permute-done.5.r2
  17.2 2.7 %collective-permute-start.4 = (f32[9,8,256]{2,1,0:T(8,128)S(1)}, f32[9,8,256]{2,1,0:T(8,128)S(1)}, u32[]{:S(2)}, u32[]{:S(2)}) collective-permute-start(f32[9,8,256]{2,1,0:T(8,128)S(1)} %get-tuple-element.20), channel_id=1, source_target_pairs={{0,192},{1,193},{2,194},{3,195},{4,196},{5,197},{6,198},{7,199},{8... | collective-permute-start | bytes 221192 | tf_op jit(solution)/shard_map/ppermute | solution.py:30
  19.9 0.0 collective-permute-done.6.r1
  19.9 0.0 collective-permute-done.7.r3
  19.9 2.0 %collective-permute-done.2.r2 = f32[9,8,256]{2,1,0:T(8,128)S(1)} collective-permute-done((f32[9,8,256]{2,1,0:T(8,128)S(1)}, f32[9,8,256]{2,1,0:T(8,128)S(1)}, u32[]{:S(2)}, u32[]{:S(2)}) %collective-permute-start.2) | collective-permute-done | bytes 73760 | tf_op jit(solution)/shard_map/ppermute | solution.py:30
  21.9 0.5 collective-permute-done.3.r1
  22.4 0.0 collective-permute-done.4.r3
  22.4 6.2 %collective-permute-start.8 = (f32[13,8,256]{2,1,0:T(8,128)S(1)}, f32[13,8,256]{2,1,0:T(8,128)S(1)}, u32[]{:S(2)}, u32[]{:S(2)}) collective-permute-start(f32[13,8,256]{2,1,0:T(8,128)S(1)} %get-tuple-element.27), channel_id=1, source_target_pairs={{0,32},{1,33},{2,34},{3,35},{4,36},{5,37},{6,38},{7,39},{8,40},{9,... | collective-permute-start | bytes 319496 | tf_op jit(solution)/shard_map/ppermute | solution.py:30
  28.7 3.1 %collective-permute-done.8 = f32[13,8,256]{2,1,0:T(8,128)S(1)} collective-permute-done((f32[13,8,256]{2,1,0:T(8,128)S(1)}, f32[13,8,256]{2,1,0:T(8,128)S(1)}, u32[]{:S(2)}, u32[]{:S(2)}) %collective-permute-start.8) | collective-permute-done | bytes 106528 | tf_op jit(solution)/shard_map/ppermute | solution.py:30
  31.8 0.0 copy-done.2
  31.8 0.1 concatenate.10
  31.9 1.1 %collective-permute-start.9 = (f32[8,16,256]{2,1,0:T(8,128)S(1)}, f32[8,16,256]{2,1,0:T(8,128)S(1)}, u32[]{:S(2)}, u32[]{:S(2)}) collective-permute-start(f32[8,16,256]{2,1,0:T(8,128)S(1)} %pad_maximum_fusion.1.block), channel_id=1, source_target_pairs={{0,1},{1,0},{2,3},{3,2},{4,5},{5,4},{6,7},{7,6},{8,9},{9,8},{10,11... | collective-permute-start | bytes 393224 | tf_op jit(solution)/shard_map/ppermute | solution.py:30
  33.0 1.0 %collective-permute-done.9.mate = f32[8,16,256]{2,1,0:T(8,128)S(1)} collective-permute-done((f32[8,16,256]{2,1,0:T(8,128)S(1)}, f32[8,16,256]{2,1,0:T(8,128)S(1)}, u32[]{:S(2)}, u32[]{:S(2)}) %collective-permute-start.9) | collective-permute-done | bytes 131104 | tf_op jit(solution)/shard_map/ppermute | solution.py:30
  34.0 3.6 %collective-permute-start.10 = (f32[11,16,256]{2,1,0:T(8,128)S(1)}, f32[11,16,256]{2,1,0:T(8,128)S(1)}, u32[]{:S(2)}, u32[]{:S(2)}) collective-permute-start(f32[11,16,256]{2,1,0:T(8,128)S(1)} %pad_maximum_fusion), channel_id=1, source_target_pairs={{1,2},{2,1},{3,4},{4,3},{5,6},{6,5},{7,8},{8,7},{9,10},{10,9},{11,... | collective-permute-start | bytes 540680 | tf_op jit(solution)/shard_map/ppermute | solution.py:30
  37.6 3.2 %collective-permute-done.10.far = f32[11,16,256]{2,1,0:T(8,128)S(1)} collective-permute-done((f32[11,16,256]{2,1,0:T(8,128)S(1)}, f32[11,16,256]{2,1,0:T(8,128)S(1)}, u32[]{:S(2)}, u32[]{:S(2)}) %collective-permute-start.10) | collective-permute-done | bytes 180256 | tf_op jit(solution)/shard_map/ppermute | solution.py:30
  40.8 0.0 collective-permute-start.11
  40.8 1.2 %collective-permute-done.11.beyond = f32[3,16,256]{2,1,0:T(8,128)S(1)} collective-permute-done((f32[3,16,256]{2,1,0:T(8,128)S(1)}, f32[3,16,256]{2,1,0:T(8,128)S(1)}, u32[]{:S(2)}, u32[]{:S(2)}) %collective-permute-start.11) | collective-permute-done | bytes 49184 | tf_op jit(solution)/shard_map/ppermute | solution.py:30
  42.1 0.9 %shard_map.54 = (f32[4,3,2,8,256]{4,3,2,1,0:T(8,128)S(1)}, f32[8,128]{1,0:T(8,128)S(1)}) custom-call(f32[8,16,256]{2,1,0:T(8,128)S(1)} %pad_maximum_fusion.1.block, f32[8,16,256]{2,1,0:T(8,128)S(1)} %collective-permute-done.9.mate, f32[11,16,256]{2,1,0:T(8,128)S(1)} %collective-permute-done.10.far, f32[3,16,256]{2,1,0:T(8,128)S(1)} %collective-permute-done.11.beyond), custom_call_target="tpu_custom_call" | custom-call | tf_op jit(solution)/shard_map/pallas_call | solution.py:57
  42.9 19.6 %all_to_all.10 = f32[16,8,128]{2,1,0:T(8,128)S(1)} all-to-all(f32[16,8,128]{2,1,0:T(8,128)S(1)} %broadcast_in_dim.14), channel_id=1, replica_groups=mesh['y'=4,'zh'=2,'x'=4,'zl'=4,'core'=2] {'zh','zl','core'}, dimensions={0} | all-to-all | bytes 131072 | tf_op jit(solution)/shard_map/all_to_all | solution.py:330
  62.6 14.7 %all_to_all.11.parts = f32[16,8,128]{2,1,0:T(8,128)S(1)} all-to-all(f32[16,8,128]{2,1,0:T(8,128)S(1)} %broadcast_in_dim.15), channel_id=1, replica_groups=mesh['y'=4,'zh'=2,'x'=4,'zl'=4,'core'=2] {'y','x'}, dimensions={0} | all-to-all | bytes 131072 | tf_op jit(solution)/shard_map/all_to_all | solution.py:332
  77.3 1.3 %shard_map.55 = (f32[3,2,8,256]{3,2,1,0:T(8,128)}, f32[3,2,8,256]{3,2,1,0:T(8,128)}) custom-call(f32[16,8,128]{2,1,0:T(8,128)S(1)} %all_to_all.11.parts, f32[4,3,2,8,256]{4,3,2,1,0:T(8,128)S(1)} %get-tuple-element.29.basis), custom_call_target="tpu_custom_call" | custom-call | tf_op jit(solution)/shard_map/pallas_call | solution.py:57
  (15 shorter events, 0.2 us)
Async XLA Ops:
  1.8 5.2 %collective-permute-start.1 = (bf16[2,5,64,256]{3,2,1,0:T(8,128)(2,1)S(1)}, bf16[2,5,64,256]{3,2,1,0:T(8,128)(2,1)S(1)}, u32[]{:S(2)}, u32[]{:S(2)}) collective-permute-start(bf16[2,5,64,256]{3,2,1,0:T(8,128)(2,1)S(1)} %get-tuple-element.31.a), channel_id=1, source_target_pairs={{0,1},{1,0},{2,3},{3,2},{4,5},{5,4},{6,7},{7,6},{8,9},{9,8},{10,11... | collective-permute-start | bytes 983048 | tf_op jit(solution)/shard_map/ppermute | solution.py:30
  5.1 11.6 %collective-permute-start = (bf16[2,5,64,256]{3,2,1,0:T(8,128)(2,1)S(1)}, bf16[2,5,64,256]{3,2,1,0:T(8,128)(2,1)S(1)}, u32[]{:S(2)}, u32[]{:S(2)}) collective-permute-start(bf16[2,5,64,256]{3,2,1,0:T(8,128)(2,1)S(1)} %get-tuple-element.30.a), channel_id=1, source_target_pairs={{1,2},{2,1},{3,4},{4,3},{5,6},{6,5},{7,8},{8,7},{9,10},{10,9},{11,... | collective-permute-start | bytes 983048 | tf_op jit(solution)/shard_map/ppermute | solution.py:30
  7.0 1.5 %copy-start = (bf16[2,5,3,2,64,256]{5,4,3,2,1,0:T(8,128)(2,1)S(1)}, bf16[2,5,3,2,64,256]{5,4,3,2,1,0:T(8,128)(2,1)}, u32[]{:S(2)}) copy-start(bf16[2,5,3,2,64,256]{5,4,3,2,1,0:T(8,128)(2,1)} %f.3) | copy-start | bytes 5898244
  8.6 0.7 copy-start.1
  9.6 22.2 %copy-start.2 = (f32[2,8,256]{2,1,0:T(8,128)S(1)}, f32[2,8,256]{2,1,0:T(8,128)}, u32[]{:S(2)}) copy-start(f32[2,8,256]{2,1,0:T(8,128)} %shift.3) | copy-start | bytes 49156
  9.6 7.6 %collective-permute-start.5 = (f32[10,8,256]{2,1,0:T(8,128)S(1)}, f32[10,8,256]{2,1,0:T(8,128)S(1)}, u32[]{:S(2)}, u32[]{:S(2)}) collective-permute-start(f32[10,8,256]{2,1,0:T(8,128)S(1)} %get-tuple-element.21), channel_id=1, source_target_pairs={{0,128},{1,129},{2,130},{3,131},{4,132},{5,133},{6,134},{7,135},{8... | collective-permute-start | bytes 245768 | tf_op jit(solution)/shard_map/ppermute | solution.py:30
  12.4 7.5 %collective-permute-start.6 = (f32[10,8,256]{2,1,0:T(8,128)S(1)}, f32[10,8,256]{2,1,0:T(8,128)S(1)}, u32[]{:S(2)}, u32[]{:S(2)}) collective-permute-start(f32[10,8,256]{2,1,0:T(8,128)S(1)} %get-tuple-element.22), channel_id=1, source_target_pairs={{0,64},{1,65},{2,66},{3,67},{4,68},{5,69},{6,70},{7,71},{8,72},{9,... | collective-permute-start | bytes 245768 | tf_op jit(solution)/shard_map/ppermute | solution.py:30
  12.8 7.1 %collective-permute-start.7 = (f32[10,8,256]{2,1,0:T(8,128)S(1)}, f32[10,8,256]{2,1,0:T(8,128)S(1)}, u32[]{:S(2)}, u32[]{:S(2)}) collective-permute-start(f32[10,8,256]{2,1,0:T(8,128)S(1)} %get-tuple-element.23), channel_id=1, source_target_pairs={{0,192},{1,193},{2,194},{3,195},{4,196},{5,197},{6,198},{7,199},{8... | collective-permute-start | bytes 245768 | tf_op jit(solution)/shard_map/ppermute | solution.py:30
  17.0 4.9 %collective-permute-start.2 = (f32[9,8,256]{2,1,0:T(8,128)S(1)}, f32[9,8,256]{2,1,0:T(8,128)S(1)}, u32[]{:S(2)}, u32[]{:S(2)}) collective-permute-start(f32[9,8,256]{2,1,0:T(8,128)S(1)} %get-tuple-element.18), channel_id=1, source_target_pairs={{0,128},{1,129},{2,130},{3,131},{4,132},{5,133},{6,134},{7,135},{8... | collective-permute-start | bytes 221192 | tf_op jit(solution)/shard_map/ppermute | solution.py:30
  17.1 5.3 %collective-permute-start.3 = (f32[9,8,256]{2,1,0:T(8,128)S(1)}, f32[9,8,256]{2,1,0:T(8,128)S(1)}, u32[]{:S(2)}, u32[]{:S(2)}) collective-permute-start(f32[9,8,256]{2,1,0:T(8,128)S(1)} %get-tuple-element.19), channel_id=1, source_target_pairs={{0,64},{1,65},{2,66},{3,67},{4,68},{5,69},{6,70},{7,71},{8,72},{9,... | collective-permute-start | bytes 221192 | tf_op jit(solution)/shard_map/ppermute | solution.py:30
  17.2 5.2 %collective-permute-start.4 = (f32[9,8,256]{2,1,0:T(8,128)S(1)}, f32[9,8,256]{2,1,0:T(8,128)S(1)}, u32[]{:S(2)}, u32[]{:S(2)}) collective-permute-start(f32[9,8,256]{2,1,0:T(8,128)S(1)} %get-tuple-element.20), channel_id=1, source_target_pairs={{0,192},{1,193},{2,194},{3,195},{4,196},{5,197},{6,198},{7,199},{8... | collective-permute-start | bytes 221192 | tf_op jit(solution)/shard_map/ppermute | solution.py:30
  22.4 9.3 %collective-permute-start.8 = (f32[13,8,256]{2,1,0:T(8,128)S(1)}, f32[13,8,256]{2,1,0:T(8,128)S(1)}, u32[]{:S(2)}, u32[]{:S(2)}) collective-permute-start(f32[13,8,256]{2,1,0:T(8,128)S(1)} %get-tuple-element.27), channel_id=1, source_target_pairs={{0,32},{1,33},{2,34},{3,35},{4,36},{5,37},{6,38},{7,39},{8,40},{9,... | collective-permute-start | bytes 319496 | tf_op jit(solution)/shard_map/ppermute | solution.py:30
  31.9 2.0 %collective-permute-start.9 = (f32[8,16,256]{2,1,0:T(8,128)S(1)}, f32[8,16,256]{2,1,0:T(8,128)S(1)}, u32[]{:S(2)}, u32[]{:S(2)}) collective-permute-start(f32[8,16,256]{2,1,0:T(8,128)S(1)} %pad_maximum_fusion.1.block), channel_id=1, source_target_pairs={{0,1},{1,0},{2,3},{3,2},{4,5},{5,4},{6,7},{7,6},{8,9},{9,8},{10,11... | collective-permute-start | bytes 393224 | tf_op jit(solution)/shard_map/ppermute | solution.py:30
  34.0 6.8 %collective-permute-start.10 = (f32[11,16,256]{2,1,0:T(8,128)S(1)}, f32[11,16,256]{2,1,0:T(8,128)S(1)}, u32[]{:S(2)}, u32[]{:S(2)}) collective-permute-start(f32[11,16,256]{2,1,0:T(8,128)S(1)} %pad_maximum_fusion), channel_id=1, source_target_pairs={{1,2},{2,1},{3,4},{4,3},{5,6},{6,5},{7,8},{8,7},{9,10},{10,9},{11,... | collective-permute-start | bytes 540680 | tf_op jit(solution)/shard_map/ppermute | solution.py:30
  40.8 1.2 %collective-permute-start.11 = (f32[3,16,256]{2,1,0:T(8,128)S(1)}, f32[3,16,256]{2,1,0:T(8,128)S(1)}, u32[]{:S(2)}, u32[]{:S(2)}) collective-permute-start(f32[3,16,256]{2,1,0:T(8,128)S(1)} %slice.29), channel_id=1, source_target_pairs={{0,1},{1,0},{2,3},{3,2},{4,5},{5,4},{6,7},{7,6},{8,9},{9,8},{10,11... | collective-permute-start | bytes 147464 | tf_op jit(solution)/shard_map/ppermute | solution.py:30

commit v9 on v8

--- a/solution.py
+++ b/solution.py
@@ -242,9 +242,11 @@
             pairs.append((high, low if rest is None else low + (rest + more_rest)))
         sums = pairs
     high, low = sums[0]
-    for step in (64, 32, 16, 8, 4, 2, 1):
-        high, error = two_sum(high, pltpu.roll(high, step, 1))
-        low = (low + pltpu.roll(low, step, 1)) + error
+    cut = 4096.0 * jnp.max(jnp.abs(high), axis=1, keepdims=True)
+    lead = (high + cut) - cut
+    rest = jnp.sum((high - lead) + low, axis=1, keepdims=True)
+    high, low = two_sum(jnp.sum(lead, axis=1, keepdims=True), rest)
+    high, low = jnp.broadcast_to(high, (8, 128)), jnp.broadcast_to(low, (8, 128))
 
     def line(v, n):
         return jnp.broadcast_to(v[n : n + 1, :], (8, 128))

time: 78.9 us -> 78.6 us (level)
  no operation moved by 1% of the time
where the time goes in v9:
time: 78.6 us; the launch traced here: 78.2 us
  blocking collectives  34.3 us (44%)
  starting transfers between devices  24.4 us (31%)
  waiting for transfers between devices  12.6 us (16%)
  local copies, waits for them, and re-layouts  3.58 us (5%)
  Pallas kernels  2.5 us (3%)
    ppermute x12, starting transfers between devices, send(): return lax.ppermute(v, AXES, pairs)  24.4 us
    all_to_all x1, blocking collectives, local(): lax.all_to_all(jnp.broadcast_to(moments, (16, 8, 128)), ('zh', 'zl', 'cor...  19.6 us
    all_to_all x1, blocking collectives, local(): lax.all_to_all(jnp.broadcast_to(moments, (16, 8, 128)), ('y', 'x'), 0, 0)  14.7 us
    ppermute x12, waiting for transfers between devices, send(): return lax.ppermute(v, AXES, pairs)  12.6 us
    pallas_call x6, Pallas kernels, call(): pl.pallas_call(kernel, out_shape=[jax.ShapeDtypeStruct(s, F32) for s in o...  2.5 us
    unnamed x6, local copies, waits for them, and re-layouts  2.26 us
  transfers between devices with their start and end apart: 12, of which 7 were waited for; matrix products, arithmetic and copies ran while one was open for 0% of the time, Pallas kernels for 1%

profile of v9, /device:TPU:1, one launch (start us, length us, event | category | flops | bytes accessed | tf_op | source)
XLA Modules:
  0.0 78.2 jit_solution(18208770900031717406)
XLA Ops:
  0.6 1.1 %dynamic-slice_bitcast_fusion = (bf16[2,5,64,256]{3,2,1,0:T(8,128)(2,1)S(1)}, bf16[2,5,64,256]{3,2,1,0:T(8,128)(2,1)S(1)}) fusion(bf16[2,5,2,64,256]{4,3,2,1,0:T(8,128)(2,1)} %param.3, s32[]{:T(128)S(6)} %select_n.8, s32[]{:T(128)S(6)} %select_n.7), kind=kLoop, calls=%fused_computation | loop fusion | bytes 1310728 | tf_op jit(solution)/shard_map/jit(dynamic_index_in_dim)/squeeze | solution.py:301
  1.8 3.3 %collective-permute-start.1 = (bf16[2,5,64,256]{3,2,1,0:T(8,128)(2,1)S(1)}, bf16[2,5,64,256]{3,2,1,0:T(8,128)(2,1)S(1)}, u32[]{:S(2)}, u32[]{:S(2)}) collective-permute-start(bf16[2,5,64,256]{3,2,1,0:T(8,128)(2,1)S(1)} %get-tuple-element.31.a), channel_id=1, source_target_pairs={{0,1},{1,0},{2,3},{3,2},{4,5},{5,4},{6,7},{7,6},{8,9},{9,8},{10,11... | collective-permute-start | bytes 983048 | tf_op jit(solution)/shard_map/ppermute | solution.py:30
  5.1 1.9 %collective-permute-start = (bf16[2,5,64,256]{3,2,1,0:T(8,128)(2,1)S(1)}, bf16[2,5,64,256]{3,2,1,0:T(8,128)(2,1)S(1)}, u32[]{:S(2)}, u32[]{:S(2)}) collective-permute-start(bf16[2,5,64,256]{3,2,1,0:T(8,128)(2,1)S(1)} %get-tuple-element.30.a), channel_id=1, source_target_pairs={{1,2},{2,1},{3,4},{4,3},{5,6},{6,5},{7,8},{8,7},{9,10},{10,9},{11,... | collective-permute-start | bytes 983048 | tf_op jit(solution)/shard_map/ppermute | solution.py:30
  7.0 0.0 collective-permute-done.1.got
  7.0 0.0 copy-start
  7.0 1.5 %copy-done = bf16[2,5,3,2,64,256]{5,4,3,2,1,0:T(8,128)(2,1)S(1)} copy-done((bf16[2,5,3,2,64,256]{5,4,3,2,1,0:T(8,128)(2,1)S(1)}, bf16[2,5,3,2,64,256]{5,4,3,2,1,0:T(8,128)(2,1)}, u32[]{:S(2)}) %copy-start) | copy-done | bytes 1966104
  8.6 0.0 copy-start.1
  8.6 0.7 copy-done.1
  9.3 0.3 shard_map.50
  9.6 0.0 copy-start.2
  9.6 2.8 %collective-permute-start.5 = (f32[10,8,256]{2,1,0:T(8,128)S(1)}, f32[10,8,256]{2,1,0:T(8,128)S(1)}, u32[]{:S(2)}, u32[]{:S(2)}) collective-permute-start(f32[10,8,256]{2,1,0:T(8,128)S(1)} %get-tuple-element.21), channel_id=1, source_target_pairs={{0,128},{1,129},{2,130},{3,131},{4,132},{5,133},{6,134},{7,135},{8... | collective-permute-start | bytes 245768 | tf_op jit(solution)/shard_map/ppermute | solution.py:30
  12.4 0.4 collective-permute-start.6
  12.8 2.3 %collective-permute-start.7 = (f32[10,8,256]{2,1,0:T(8,128)S(1)}, f32[10,8,256]{2,1,0:T(8,128)S(1)}, u32[]{:S(2)}, u32[]{:S(2)}) collective-permute-start(f32[10,8,256]{2,1,0:T(8,128)S(1)} %get-tuple-element.23), channel_id=1, source_target_pairs={{0,192},{1,193},{2,194},{3,195},{4,196},{5,197},{6,198},{7,199},{8... | collective-permute-start | bytes 245768 | tf_op jit(solution)/shard_map/ppermute | solution.py:30
  15.1 1.7 %collective-permute-done.got = bf16[2,5,64,256]{3,2,1,0:T(8,128)(2,1)S(1)} collective-permute-done((bf16[2,5,64,256]{3,2,1,0:T(8,128)(2,1)S(1)}, bf16[2,5,64,256]{3,2,1,0:T(8,128)(2,1)S(1)}, u32[]{:S(2)}, u32[]{:S(2)}) %collective-permute-start) | collective-permute-done | bytes 327712 | tf_op jit(solution)/shard_map/ppermute | solution.py:30
  16.7 0.3 shard_map.51
  17.0 0.1 collective-permute-start.2
  17.1 0.1 collective-permute-start.3
  17.2 0.0 collective-permute-done.5.r2
  17.2 2.7 %collective-permute-start.4 = (f32[9,8,256]{2,1,0:T(8,128)S(1)}, f32[9,8,256]{2,1,0:T(8,128)S(1)}, u32[]{:S(2)}, u32[]{:S(2)}) collective-permute-start(f32[9,8,256]{2,1,0:T(8,128)S(1)} %get-tuple-element.20), channel_id=1, source_target_pairs={{0,192},{1,193},{2,194},{3,195},{4,196},{5,197},{6,198},{7,199},{8... | collective-permute-start | bytes 221192 | tf_op jit(solution)/shard_map/ppermute | solution.py:30
  19.9 0.0 collective-permute-done.6.r1
  19.9 0.0 collective-permute-done.7.r3
  19.9 2.0 %collective-permute-done.2.r2 = f32[9,8,256]{2,1,0:T(8,128)S(1)} collective-permute-done((f32[9,8,256]{2,1,0:T(8,128)S(1)}, f32[9,8,256]{2,1,0:T(8,128)S(1)}, u32[]{:S(2)}, u32[]{:S(2)}) %collective-permute-start.2) | collective-permute-done | bytes 73760 | tf_op jit(solution)/shard_map/ppermute | solution.py:30
  21.9 0.5 collective-permute-done.3.r1
  22.4 0.0 collective-permute-done.4.r3
  22.4 6.2 %collective-permute-start.8 = (f32[13,8,256]{2,1,0:T(8,128)S(1)}, f32[13,8,256]{2,1,0:T(8,128)S(1)}, u32[]{:S(2)}, u32[]{:S(2)}) collective-permute-start(f32[13,8,256]{2,1,0:T(8,128)S(1)} %get-tuple-element.27), channel_id=1, source_target_pairs={{0,32},{1,33},{2,34},{3,35},{4,36},{5,37},{6,38},{7,39},{8,40},{9,... | collective-permute-start | bytes 319496 | tf_op jit(solution)/shard_map/ppermute | solution.py:30
  28.7 3.1 %collective-permute-done.8 = f32[13,8,256]{2,1,0:T(8,128)S(1)} collective-permute-done((f32[13,8,256]{2,1,0:T(8,128)S(1)}, f32[13,8,256]{2,1,0:T(8,128)S(1)}, u32[]{:S(2)}, u32[]{:S(2)}) %collective-permute-start.8) | collective-permute-done | bytes 106528 | tf_op jit(solution)/shard_map/ppermute | solution.py:30
  31.8 0.0 copy-done.2
  31.8 0.1 concatenate.10
  31.9 1.1 %collective-permute-start.9 = (f32[8,16,256]{2,1,0:T(8,128)S(1)}, f32[8,16,256]{2,1,0:T(8,128)S(1)}, u32[]{:S(2)}, u32[]{:S(2)}) collective-permute-start(f32[8,16,256]{2,1,0:T(8,128)S(1)} %pad_maximum_fusion.1.block), channel_id=1, source_target_pairs={{0,1},{1,0},{2,3},{3,2},{4,5},{5,4},{6,7},{7,6},{8,9},{9,8},{10,11... | collective-permute-start | bytes 393224 | tf_op jit(solution)/shard_map/ppermute | solution.py:30
  33.0 1.0 %collective-permute-done.9.mate = f32[8,16,256]{2,1,0:T(8,128)S(1)} collective-permute-done((f32[8,16,256]{2,1,0:T(8,128)S(1)}, f32[8,16,256]{2,1,0:T(8,128)S(1)}, u32[]{:S(2)}, u32[]{:S(2)}) %collective-permute-start.9) | collective-permute-done | bytes 131104 | tf_op jit(solution)/shard_map/ppermute | solution.py:30
  34.0 3.6 %collective-permute-start.10 = (f32[11,16,256]{2,1,0:T(8,128)S(1)}, f32[11,16,256]{2,1,0:T(8,128)S(1)}, u32[]{:S(2)}, u32[]{:S(2)}) collective-permute-start(f32[11,16,256]{2,1,0:T(8,128)S(1)} %pad_maximum_fusion), channel_id=1, source_target_pairs={{1,2},{2,1},{3,4},{4,3},{5,6},{6,5},{7,8},{8,7},{9,10},{10,9},{11,... | collective-permute-start | bytes 540680 | tf_op jit(solution)/shard_map/ppermute | solution.py:30
  37.6 3.2 %collective-permute-done.10.far = f32[11,16,256]{2,1,0:T(8,128)S(1)} collective-permute-done((f32[11,16,256]{2,1,0:T(8,128)S(1)}, f32[11,16,256]{2,1,0:T(8,128)S(1)}, u32[]{:S(2)}, u32[]{:S(2)}) %collective-permute-start.10) | collective-permute-done | bytes 180256 | tf_op jit(solution)/shard_map/ppermute | solution.py:30
  40.8 0.0 collective-permute-start.11
  40.8 1.2 %collective-permute-done.11.beyond = f32[3,16,256]{2,1,0:T(8,128)S(1)} collective-permute-done((f32[3,16,256]{2,1,0:T(8,128)S(1)}, f32[3,16,256]{2,1,0:T(8,128)S(1)}, u32[]{:S(2)}, u32[]{:S(2)}) %collective-permute-start.11) | collective-permute-done | bytes 49184 | tf_op jit(solution)/shard_map/ppermute | solution.py:30
  42.1 0.9 %shard_map.54 = (f32[4,3,2,8,256]{4,3,2,1,0:T(8,128)S(1)}, f32[8,128]{1,0:T(8,128)S(1)}) custom-call(f32[8,16,256]{2,1,0:T(8,128)S(1)} %pad_maximum_fusion.1.block, f32[8,16,256]{2,1,0:T(8,128)S(1)} %collective-permute-done.9.mate, f32[11,16,256]{2,1,0:T(8,128)S(1)} %collective-permute-done.10.far, f32[3,16,256]{2,1,0:T(8,128)S(1)} %collective-permute-done.11.beyond), custom_call_target="tpu_custom_call" | custom-call | tf_op jit(solution)/shard_map/pallas_call | solution.py:57
  42.9 19.6 %all_to_all.10 = f32[16,8,128]{2,1,0:T(8,128)S(1)} all-to-all(f32[16,8,128]{2,1,0:T(8,128)S(1)} %broadcast_in_dim.14), channel_id=1, replica_groups=mesh['y'=4,'zh'=2,'x'=4,'zl'=4,'core'=2] {'zh','zl','core'}, dimensions={0} | all-to-all | bytes 131072 | tf_op jit(solution)/shard_map/all_to_all | solution.py:332
  62.6 14.7 %all_to_all.11.parts = f32[16,8,128]{2,1,0:T(8,128)S(1)} all-to-all(f32[16,8,128]{2,1,0:T(8,128)S(1)} %broadcast_in_dim.15), channel_id=1, replica_groups=mesh['y'=4,'zh'=2,'x'=4,'zl'=4,'core'=2] {'y','x'}, dimensions={0} | all-to-all | bytes 131072 | tf_op jit(solution)/shard_map/all_to_all | solution.py:334
  77.3 1.0 %shard_map.55 = (f32[3,2,8,256]{3,2,1,0:T(8,128)}, f32[3,2,8,256]{3,2,1,0:T(8,128)}) custom-call(f32[16,8,128]{2,1,0:T(8,128)S(1)} %all_to_all.11.parts, f32[4,3,2,8,256]{4,3,2,1,0:T(8,128)S(1)} %get-tuple-element.29.basis), custom_call_target="tpu_custom_call" | custom-call | tf_op jit(solution)/shard_map/pallas_call | solution.py:57
  (15 shorter events, 0.2 us)
Async XLA Ops:
  1.8 5.2 %collective-permute-start.1 = (bf16[2,5,64,256]{3,2,1,0:T(8,128)(2,1)S(1)}, bf16[2,5,64,256]{3,2,1,0:T(8,128)(2,1)S(1)}, u32[]{:S(2)}, u32[]{:S(2)}) collective-permute-start(bf16[2,5,64,256]{3,2,1,0:T(8,128)(2,1)S(1)} %get-tuple-element.31.a), channel_id=1, source_target_pairs={{0,1},{1,0},{2,3},{3,2},{4,5},{5,4},{6,7},{7,6},{8,9},{9,8},{10,11... | collective-permute-start | bytes 983048 | tf_op jit(solution)/shard_map/ppermute | solution.py:30
  5.1 11.6 %collective-permute-start = (bf16[2,5,64,256]{3,2,1,0:T(8,128)(2,1)S(1)}, bf16[2,5,64,256]{3,2,1,0:T(8,128)(2,1)S(1)}, u32[]{:S(2)}, u32[]{:S(2)}) collective-permute-start(bf16[2,5,64,256]{3,2,1,0:T(8,128)(2,1)S(1)} %get-tuple-element.30.a), channel_id=1, source_target_pairs={{1,2},{2,1},{3,4},{4,3},{5,6},{6,5},{7,8},{8,7},{9,10},{10,9},{11,... | collective-permute-start | bytes 983048 | tf_op jit(solution)/shard_map/ppermute | solution.py:30
  7.0 1.5 %copy-start = (bf16[2,5,3,2,64,256]{5,4,3,2,1,0:T(8,128)(2,1)S(1)}, bf16[2,5,3,2,64,256]{5,4,3,2,1,0:T(8,128)(2,1)}, u32[]{:S(2)}) copy-start(bf16[2,5,3,2,64,256]{5,4,3,2,1,0:T(8,128)(2,1)} %f.3) | copy-start | bytes 5898244
  8.6 0.7 copy-start.1
  9.6 22.2 %copy-start.2 = (f32[2,8,256]{2,1,0:T(8,128)S(1)}, f32[2,8,256]{2,1,0:T(8,128)}, u32[]{:S(2)}) copy-start(f32[2,8,256]{2,1,0:T(8,128)} %shift.3) | copy-start | bytes 49156
  9.6 7.6 %collective-permute-start.5 = (f32[10,8,256]{2,1,0:T(8,128)S(1)}, f32[10,8,256]{2,1,0:T(8,128)S(1)}, u32[]{:S(2)}, u32[]{:S(2)}) collective-permute-start(f32[10,8,256]{2,1,0:T(8,128)S(1)} %get-tuple-element.21), channel_id=1, source_target_pairs={{0,128},{1,129},{2,130},{3,131},{4,132},{5,133},{6,134},{7,135},{8... | collective-permute-start | bytes 245768 | tf_op jit(solution)/shard_map/ppermute | solution.py:30
  12.4 7.5 %collective-permute-start.6 = (f32[10,8,256]{2,1,0:T(8,128)S(1)}, f32[10,8,256]{2,1,0:T(8,128)S(1)}, u32[]{:S(2)}, u32[]{:S(2)}) collective-permute-start(f32[10,8,256]{2,1,0:T(8,128)S(1)} %get-tuple-element.22), channel_id=1, source_target_pairs={{0,64},{1,65},{2,66},{3,67},{4,68},{5,69},{6,70},{7,71},{8,72},{9,... | collective-permute-start | bytes 245768 | tf_op jit(solution)/shard_map/ppermute | solution.py:30
  12.8 7.1 %collective-permute-start.7 = (f32[10,8,256]{2,1,0:T(8,128)S(1)}, f32[10,8,256]{2,1,0:T(8,128)S(1)}, u32[]{:S(2)}, u32[]{:S(2)}) collective-permute-start(f32[10,8,256]{2,1,0:T(8,128)S(1)} %get-tuple-element.23), channel_id=1, source_target_pairs={{0,192},{1,193},{2,194},{3,195},{4,196},{5,197},{6,198},{7,199},{8... | collective-permute-start | bytes 245768 | tf_op jit(solution)/shard_map/ppermute | solution.py:30
  17.0 4.9 %collective-permute-start.2 = (f32[9,8,256]{2,1,0:T(8,128)S(1)}, f32[9,8,256]{2,1,0:T(8,128)S(1)}, u32[]{:S(2)}, u32[]{:S(2)}) collective-permute-start(f32[9,8,256]{2,1,0:T(8,128)S(1)} %get-tuple-element.18), channel_id=1, source_target_pairs={{0,128},{1,129},{2,130},{3,131},{4,132},{5,133},{6,134},{7,135},{8... | collective-permute-start | bytes 221192 | tf_op jit(solution)/shard_map/ppermute | solution.py:30
  17.1 5.3 %collective-permute-start.3 = (f32[9,8,256]{2,1,0:T(8,128)S(1)}, f32[9,8,256]{2,1,0:T(8,128)S(1)}, u32[]{:S(2)}, u32[]{:S(2)}) collective-permute-start(f32[9,8,256]{2,1,0:T(8,128)S(1)} %get-tuple-element.19), channel_id=1, source_target_pairs={{0,64},{1,65},{2,66},{3,67},{4,68},{5,69},{6,70},{7,71},{8,72},{9,... | collective-permute-start | bytes 221192 | tf_op jit(solution)/shard_map/ppermute | solution.py:30
  17.2 5.2 %collective-permute-start.4 = (f32[9,8,256]{2,1,0:T(8,128)S(1)}, f32[9,8,256]{2,1,0:T(8,128)S(1)}, u32[]{:S(2)}, u32[]{:S(2)}) collective-permute-start(f32[9,8,256]{2,1,0:T(8,128)S(1)} %get-tuple-element.20), channel_id=1, source_target_pairs={{0,192},{1,193},{2,194},{3,195},{4,196},{5,197},{6,198},{7,199},{8... | collective-permute-start | bytes 221192 | tf_op jit(solution)/shard_map/ppermute | solution.py:30
  22.4 9.3 %collective-permute-start.8 = (f32[13,8,256]{2,1,0:T(8,128)S(1)}, f32[13,8,256]{2,1,0:T(8,128)S(1)}, u32[]{:S(2)}, u32[]{:S(2)}) collective-permute-start(f32[13,8,256]{2,1,0:T(8,128)S(1)} %get-tuple-element.27), channel_id=1, source_target_pairs={{0,32},{1,33},{2,34},{3,35},{4,36},{5,37},{6,38},{7,39},{8,40},{9,... | collective-permute-start | bytes 319496 | tf_op jit(solution)/shard_map/ppermute | solution.py:30
  31.9 2.0 %collective-permute-start.9 = (f32[8,16,256]{2,1,0:T(8,128)S(1)}, f32[8,16,256]{2,1,0:T(8,128)S(1)}, u32[]{:S(2)}, u32[]{:S(2)}) collective-permute-start(f32[8,16,256]{2,1,0:T(8,128)S(1)} %pad_maximum_fusion.1.block), channel_id=1, source_target_pairs={{0,1},{1,0},{2,3},{3,2},{4,5},{5,4},{6,7},{7,6},{8,9},{9,8},{10,11... | collective-permute-start | bytes 393224 | tf_op jit(solution)/shard_map/ppermute | solution.py:30
  34.0 6.8 %collective-permute-start.10 = (f32[11,16,256]{2,1,0:T(8,128)S(1)}, f32[11,16,256]{2,1,0:T(8,128)S(1)}, u32[]{:S(2)}, u32[]{:S(2)}) collective-permute-start(f32[11,16,256]{2,1,0:T(8,128)S(1)} %pad_maximum_fusion), channel_id=1, source_target_pairs={{1,2},{2,1},{3,4},{4,3},{5,6},{6,5},{7,8},{8,7},{9,10},{10,9},{11,... | collective-permute-start | bytes 540680 | tf_op jit(solution)/shard_map/ppermute | solution.py:30
  40.8 1.2 %collective-permute-start.11 = (f32[3,16,256]{2,1,0:T(8,128)S(1)}, f32[3,16,256]{2,1,0:T(8,128)S(1)}, u32[]{:S(2)}, u32[]{:S(2)}) collective-permute-start(f32[3,16,256]{2,1,0:T(8,128)S(1)} %slice.29), channel_id=1, source_target_pairs={{0,1},{1,0},{2,3},{3,2},{4,5},{5,4},{6,7},{7,6},{8,9},{9,8},{10,11... | collective-permute-start | bytes 147464 | tf_op jit(solution)/shard_map/ppermute | solution.py:30

commit v10 on v9

--- a/solution.py
+++ b/solution.py
@@ -114,7 +114,7 @@
                 to[s * 2 + g] = (m0[k] + r1[k]) + (r2[k] + r3[k])
 
 
-def sum_y_early_kernel(m0, r2, r1, r3, shift, after, own, out):
+def sum_y_early_kernel(m0, r1, r3, r2, shift, after, own, out):
     sum_y(m0, r2, r1, r3, own, out)
     low = lax.axis_index("zh") == 0
     for x in range(2):
@@ -124,7 +124,7 @@
         out[6, x * 4 + 2 : x * 4 + 4, :] = above
 
 
-def sum_y_late_kernel(m0, r2, r1, r3, own_early, out_early, own, out):
+def sum_y_late_kernel(m0, r1, r3, r2, own_early, out_early, own, out):
     sum_y(m0, r2, r1, r3, own, out)
     own[6:12] = own_early[...]
     out[6:13] = out_early[...]
@@ -311,8 +311,8 @@
     r2, r1, r3 = send_y(m2, 2), send_y(m1, 1), send_y(m3, 3)
     n0, n1, n2, n3 = call(sens_late_kernel, [nine] * 4, (flux_jac, inner, got_outer, m0), wide)
     q2, q1, q3 = send_y(n2, 2), send_y(n1, 1), send_y(n3, 3)
-    own, out = call(sum_y_early_kernel, [six, (7, 8, 256)], (m0, r2, r1, r3, shift, n0))
-    own, out = call(sum_y_late_kernel, [(12, 8, 256), (13, 8, 256)], (n0, q2, q1, q3, own, out))
+    own, out = call(sum_y_early_kernel, [six, (7, 8, 256)], (m0, r1, r3, r2, shift, n0))
+    own, out = call(sum_y_late_kernel, [(12, 8, 256), (13, 8, 256)], (n0, q1, q3, q2, own, out))
     got = send_zh(out)
     sides = got[12].reshape(2, 4, 256)
     ends = [jnp.zeros((2, n, 256), F32) for n in (1, 3)]

time: 78.6 us -> 77.6 us (0.987)
  waiting for transfers between devices: 12.6 us -> 17.1 us
  blocking collectives: 34.3 us -> 31 us
  starting transfers between devices: 24.4 us -> 22.4 us
    ppermute x12, waiting for transfers between devices: 12.6 us -> 17.1 us  [send(): return lax.ppermute(v, AXES, pairs)]
    ppermute x12, starting transfers between devices: 24.4 us -> 22.4 us  [send(): return lax.ppermute(v, AXES, pairs)]
    all_to_all x1, blocking collectives: 14.7 us -> 13 us  [local(): lax.all_to_all(jnp.broadcast_to(moments, (16, 8, 128)), ('y', 'x'), 0, 0)]
    all_to_all x1, blocking collectives: 19.6 us -> 18 us  [local(): lax.all_to_all(jnp.broadcast_to(moments, (16, 8, 128)), ('zh', 'zl', 'cor...]
where the time goes in v10:
time: 77.6 us; the launch traced here: 77.3 us
  blocking collectives  31 us (40%)
  starting transfers between devices  22.4 us (29%)
  waiting for transfers between devices  17.1 us (22%)
  local copies, waits for them, and re-layouts  3.58 us (5%)
  Pallas kernels  2.51 us (3%)
    ppermute x12, starting transfers between devices, send(): return lax.ppermute(v, AXES, pairs)  22.4 us
    all_to_all x1, blocking collectives, local(): lax.all_to_all(jnp.broadcast_to(moments, (16, 8, 128)), ('zh', 'zl', 'cor...  18 us
    ppermute x12, waiting for transfers between devices, send(): return lax.ppermute(v, AXES, pairs)  17.1 us
    all_to_all x1, blocking collectives, local(): lax.all_to_all(jnp.broadcast_to(moments, (16, 8, 128)), ('y', 'x'), 0, 0)  13 us
    pallas_call x6, Pallas kernels, call(): pl.pallas_call(kernel, out_shape=[jax.ShapeDtypeStruct(s, F32) for s in o...  2.51 us
    unnamed x6, local copies, waits for them, and re-layouts  2.26 us
  transfers between devices with their start and end apart: 12, of which 7 were waited for; matrix products, arithmetic and copies ran while one was open for 0% of the time, Pallas kernels for 1%

profile of v10, /device:TPU:1, one launch (start us, length us, event | category | flops | bytes accessed | tf_op | source)
XLA Modules:
  0.0 77.3 jit_solution(2616053345807059097)
XLA Ops:
  0.6 1.1 %dynamic-slice_bitcast_fusion = (bf16[2,5,64,256]{3,2,1,0:T(8,128)(2,1)S(1)}, bf16[2,5,64,256]{3,2,1,0:T(8,128)(2,1)S(1)}) fusion(bf16[2,5,2,64,256]{4,3,2,1,0:T(8,128)(2,1)} %param.3, s32[]{:T(128)S(6)} %select_n.8, s32[]{:T(128)S(6)} %select_n.7), kind=kLoop, calls=%fused_computation | loop fusion | bytes 1310728 | tf_op jit(solution)/shard_map/jit(dynamic_index_in_dim)/squeeze | solution.py:301
  1.8 3.3 %collective-permute-start.1 = (bf16[2,5,64,256]{3,2,1,0:T(8,128)(2,1)S(1)}, bf16[2,5,64,256]{3,2,1,0:T(8,128)(2,1)S(1)}, u32[]{:S(2)}, u32[]{:S(2)}) collective-permute-start(bf16[2,5,64,256]{3,2,1,0:T(8,128)(2,1)S(1)} %get-tuple-element.31.a), channel_id=1, source_target_pairs={{0,1},{1,0},{2,3},{3,2},{4,5},{5,4},{6,7},{7,6},{8,9},{9,8},{10,11... | collective-permute-start | bytes 983048 | tf_op jit(solution)/shard_map/ppermute | solution.py:30
  5.1 1.9 %collective-permute-start = (bf16[2,5,64,256]{3,2,1,0:T(8,128)(2,1)S(1)}, bf16[2,5,64,256]{3,2,1,0:T(8,128)(2,1)S(1)}, u32[]{:S(2)}, u32[]{:S(2)}) collective-permute-start(bf16[2,5,64,256]{3,2,1,0:T(8,128)(2,1)S(1)} %get-tuple-element.30.a), channel_id=1, source_target_pairs={{1,2},{2,1},{3,4},{4,3},{5,6},{6,5},{7,8},{8,7},{9,10},{10,9},{11,... | collective-permute-start | bytes 983048 | tf_op jit(solution)/shard_map/ppermute | solution.py:30
  7.0 0.0 collective-permute-done.1.got
  7.0 0.0 copy-start
  7.0 1.5 %copy-done = bf16[2,5,3,2,64,256]{5,4,3,2,1,0:T(8,128)(2,1)S(1)} copy-done((bf16[2,5,3,2,64,256]{5,4,3,2,1,0:T(8,128)(2,1)S(1)}, bf16[2,5,3,2,64,256]{5,4,3,2,1,0:T(8,128)(2,1)}, u32[]{:S(2)}) %copy-start) | copy-done | bytes 1966104
  8.6 0.0 copy-start.1
  8.6 0.7 copy-done.1
  9.3 0.3 shard_map.50
  9.6 0.0 copy-start.2
  9.6 1.2 %collective-permute-start.5 = (f32[10,8,256]{2,1,0:T(8,128)S(1)}, f32[10,8,256]{2,1,0:T(8,128)S(1)}, u32[]{:S(2)}, u32[]{:S(2)}) collective-permute-start(f32[10,8,256]{2,1,0:T(8,128)S(1)} %get-tuple-element.21), channel_id=1, source_target_pairs={{0,64},{1,65},{2,66},{3,67},{4,68},{5,69},{6,70},{7,71},{8,72},{9,... | collective-permute-start | bytes 245768 | tf_op jit(solution)/shard_map/ppermute | solution.py:30
  10.8 1.6 %collective-permute-start.6 = (f32[10,8,256]{2,1,0:T(8,128)S(1)}, f32[10,8,256]{2,1,0:T(8,128)S(1)}, u32[]{:S(2)}, u32[]{:S(2)}) collective-permute-start(f32[10,8,256]{2,1,0:T(8,128)S(1)} %get-tuple-element.22), channel_id=1, source_target_pairs={{0,192},{1,193},{2,194},{3,195},{4,196},{5,197},{6,198},{7,199},{8... | collective-permute-start | bytes 245768 | tf_op jit(solution)/shard_map/ppermute | solution.py:30
  12.3 1.5 %collective-permute-start.7 = (f32[10,8,256]{2,1,0:T(8,128)S(1)}, f32[10,8,256]{2,1,0:T(8,128)S(1)}, u32[]{:S(2)}, u32[]{:S(2)}) collective-permute-start(f32[10,8,256]{2,1,0:T(8,128)S(1)} %get-tuple-element.23), channel_id=1, source_target_pairs={{0,128},{1,129},{2,130},{3,131},{4,132},{5,133},{6,134},{7,135},{8... | collective-permute-start | bytes 245768 | tf_op jit(solution)/shard_map/ppermute | solution.py:30
  13.8 2.9 %collective-permute-done.got = bf16[2,5,64,256]{3,2,1,0:T(8,128)(2,1)S(1)} collective-permute-done((bf16[2,5,64,256]{3,2,1,0:T(8,128)(2,1)S(1)}, bf16[2,5,64,256]{3,2,1,0:T(8,128)(2,1)S(1)}, u32[]{:S(2)}, u32[]{:S(2)}) %collective-permute-start) | collective-permute-done | bytes 327712 | tf_op jit(solution)/shard_map/ppermute | solution.py:30
  16.7 0.3 shard_map.51
  17.0 0.1 collective-permute-start.2
  17.1 2.7 %collective-permute-start.3 = (f32[9,8,256]{2,1,0:T(8,128)S(1)}, f32[9,8,256]{2,1,0:T(8,128)S(1)}, u32[]{:S(2)}, u32[]{:S(2)}) collective-permute-start(f32[9,8,256]{2,1,0:T(8,128)S(1)} %get-tuple-element.19), channel_id=1, source_target_pairs={{0,192},{1,193},{2,194},{3,195},{4,196},{5,197},{6,198},{7,199},{8... | collective-permute-start | bytes 221192 | tf_op jit(solution)/shard_map/ppermute | solution.py:30
  19.8 0.0 collective-permute-done.5.r1
  19.8 0.0 collective-permute-start.4
  19.8 0.0 collective-permute-done.6.r3
  19.8 0.0 collective-permute-done.7.r2
  19.8 2.5 %collective-permute-done.2.r1 = f32[9,8,256]{2,1,0:T(8,128)S(1)} collective-permute-done((f32[9,8,256]{2,1,0:T(8,128)S(1)}, f32[9,8,256]{2,1,0:T(8,128)S(1)}, u32[]{:S(2)}, u32[]{:S(2)}) %collective-permute-start.2) | collective-permute-done | bytes 73760 | tf_op jit(solution)/shard_map/ppermute | solution.py:30
  22.3 0.0 collective-permute-done.3.r3
  22.3 2.2 %collective-permute-done.4.r2 = f32[9,8,256]{2,1,0:T(8,128)S(1)} collective-permute-done((f32[9,8,256]{2,1,0:T(8,128)S(1)}, f32[9,8,256]{2,1,0:T(8,128)S(1)}, u32[]{:S(2)}, u32[]{:S(2)}) %collective-permute-start.4) | collective-permute-done | bytes 73760 | tf_op jit(solution)/shard_map/ppermute | solution.py:30
  24.5 4.7 %collective-permute-start.8 = (f32[13,8,256]{2,1,0:T(8,128)S(1)}, f32[13,8,256]{2,1,0:T(8,128)S(1)}, u32[]{:S(2)}, u32[]{:S(2)}) collective-permute-start(f32[13,8,256]{2,1,0:T(8,128)S(1)} %get-tuple-element.27), channel_id=1, source_target_pairs={{0,32},{1,33},{2,34},{3,35},{4,36},{5,37},{6,38},{7,39},{8,40},{9,... | collective-permute-start | bytes 319496 | tf_op jit(solution)/shard_map/ppermute | solution.py:30
  29.2 4.2 %collective-permute-done.8 = f32[13,8,256]{2,1,0:T(8,128)S(1)} collective-permute-done((f32[13,8,256]{2,1,0:T(8,128)S(1)}, f32[13,8,256]{2,1,0:T(8,128)S(1)}, u32[]{:S(2)}, u32[]{:S(2)}) %collective-permute-start.8) | collective-permute-done | bytes 106528 | tf_op jit(solution)/shard_map/ppermute | solution.py:30
  33.4 0.0 copy-done.2
  33.4 0.1 concatenate.10
  33.6 0.7 collective-permute-start.9
  34.3 1.0 %collective-permute-done.9.mate = f32[8,16,256]{2,1,0:T(8,128)S(1)} collective-permute-done((f32[8,16,256]{2,1,0:T(8,128)S(1)}, f32[8,16,256]{2,1,0:T(8,128)S(1)}, u32[]{:S(2)}, u32[]{:S(2)}) %collective-permute-start.9) | collective-permute-done | bytes 131104 | tf_op jit(solution)/shard_map/ppermute | solution.py:30
  35.3 4.7 %collective-permute-start.10 = (f32[11,16,256]{2,1,0:T(8,128)S(1)}, f32[11,16,256]{2,1,0:T(8,128)S(1)}, u32[]{:S(2)}, u32[]{:S(2)}) collective-permute-start(f32[11,16,256]{2,1,0:T(8,128)S(1)} %pad_maximum_fusion), channel_id=1, source_target_pairs={{1,2},{2,1},{3,4},{4,3},{5,6},{6,5},{7,8},{8,7},{9,10},{10,9},{11,... | collective-permute-start | bytes 540680 | tf_op jit(solution)/shard_map/ppermute | solution.py:30
  40.0 3.2 %collective-permute-done.10.far = f32[11,16,256]{2,1,0:T(8,128)S(1)} collective-permute-done((f32[11,16,256]{2,1,0:T(8,128)S(1)}, f32[11,16,256]{2,1,0:T(8,128)S(1)}, u32[]{:S(2)}, u32[]{:S(2)}) %collective-permute-start.10) | collective-permute-done | bytes 180256 | tf_op jit(solution)/shard_map/ppermute | solution.py:30
  43.2 0.0 collective-permute-start.11
  43.2 1.2 %collective-permute-done.11.beyond = f32[3,16,256]{2,1,0:T(8,128)S(1)} collective-permute-done((f32[3,16,256]{2,1,0:T(8,128)S(1)}, f32[3,16,256]{2,1,0:T(8,128)S(1)}, u32[]{:S(2)}, u32[]{:S(2)}) %collective-permute-start.11) | collective-permute-done | bytes 49184 | tf_op jit(solution)/shard_map/ppermute | solution.py:30
  44.5 0.9 %shard_map.54 = (f32[4,3,2,8,256]{4,3,2,1,0:T(8,128)S(1)}, f32[8,128]{1,0:T(8,128)S(1)}) custom-call(f32[8,16,256]{2,1,0:T(8,128)S(1)} %pad_maximum_fusion.1.block, f32[8,16,256]{2,1,0:T(8,128)S(1)} %collective-permute-done.9.mate, f32[11,16,256]{2,1,0:T(8,128)S(1)} %collective-permute-done.10.far, f32[3,16,256]{2,1,0:T(8,128)S(1)} %collective-permute-done.11.beyond), custom_call_target="tpu_custom_call" | custom-call | tf_op jit(solution)/shard_map/pallas_call | solution.py:57
  45.3 18.0 %all_to_all.10 = f32[16,8,128]{2,1,0:T(8,128)S(1)} all-to-all(f32[16,8,128]{2,1,0:T(8,128)S(1)} %broadcast_in_dim.14), channel_id=1, replica_groups=mesh['y'=4,'zh'=2,'x'=4,'zl'=4,'core'=2] {'zh','zl','core'}, dimensions={0} | all-to-all | bytes 131072 | tf_op jit(solution)/shard_map/all_to_all | solution.py:332
  63.4 13.0 %all_to_all.11.parts = f32[16,8,128]{2,1,0:T(8,128)S(1)} all-to-all(f32[16,8,128]{2,1,0:T(8,128)S(1)} %broadcast_in_dim.15), channel_id=1, replica_groups=mesh['y'=4,'zh'=2,'x'=4,'zl'=4,'core'=2] {'y','x'}, dimensions={0} | all-to-all | bytes 131072 | tf_op jit(solution)/shard_map/all_to_all | solution.py:334
  76.3 1.0 %shard_map.55 = (f32[3,2,8,256]{3,2,1,0:T(8,128)}, f32[3,2,8,256]{3,2,1,0:T(8,128)}) custom-call(f32[16,8,128]{2,1,0:T(8,128)S(1)} %all_to_all.11.parts, f32[4,3,2,8,256]{4,3,2,1,0:T(8,128)S(1)} %get-tuple-element.29.basis), custom_call_target="tpu_custom_call" | custom-call | tf_op jit(solution)/shard_map/pallas_call | solution.py:57
  (15 shorter events, 0.2 us)
Async XLA Ops:
  1.8 5.2 %collective-permute-start.1 = (bf16[2,5,64,256]{3,2,1,0:T(8,128)(2,1)S(1)}, bf16[2,5,64,256]{3,2,1,0:T(8,128)(2,1)S(1)}, u32[]{:S(2)}, u32[]{:S(2)}) collective-permute-start(bf16[2,5,64,256]{3,2,1,0:T(8,128)(2,1)S(1)} %get-tuple-element.31.a), channel_id=1, source_target_pairs={{0,1},{1,0},{2,3},{3,2},{4,5},{5,4},{6,7},{7,6},{8,9},{9,8},{10,11... | collective-permute-start | bytes 983048 | tf_op jit(solution)/shard_map/ppermute | solution.py:30
  5.1 11.6 %collective-permute-start = (bf16[2,5,64,256]{3,2,1,0:T(8,128)(2,1)S(1)}, bf16[2,5,64,256]{3,2,1,0:T(8,128)(2,1)S(1)}, u32[]{:S(2)}, u32[]{:S(2)}) collective-permute-start(bf16[2,5,64,256]{3,2,1,0:T(8,128)(2,1)S(1)} %get-tuple-element.30.a), channel_id=1, source_target_pairs={{1,2},{2,1},{3,4},{4,3},{5,6},{6,5},{7,8},{8,7},{9,10},{10,9},{11,... | collective-permute-start | bytes 983048 | tf_op jit(solution)/shard_map/ppermute | solution.py:30
  7.0 1.5 %copy-start = (bf16[2,5,3,2,64,256]{5,4,3,2,1,0:T(8,128)(2,1)S(1)}, bf16[2,5,3,2,64,256]{5,4,3,2,1,0:T(8,128)(2,1)}, u32[]{:S(2)}) copy-start(bf16[2,5,3,2,64,256]{5,4,3,2,1,0:T(8,128)(2,1)} %f.3) | copy-start | bytes 5898244
  8.6 0.7 copy-start.1
  9.6 23.8 %copy-start.2 = (f32[2,8,256]{2,1,0:T(8,128)S(1)}, f32[2,8,256]{2,1,0:T(8,128)}, u32[]{:S(2)}) copy-start(f32[2,8,256]{2,1,0:T(8,128)} %shift.3) | copy-start | bytes 49156
  9.6 10.2 %collective-permute-start.5 = (f32[10,8,256]{2,1,0:T(8,128)S(1)}, f32[10,8,256]{2,1,0:T(8,128)S(1)}, u32[]{:S(2)}, u32[]{:S(2)}) collective-permute-start(f32[10,8,256]{2,1,0:T(8,128)S(1)} %get-tuple-element.21), channel_id=1, source_target_pairs={{0,64},{1,65},{2,66},{3,67},{4,68},{5,69},{6,70},{7,71},{8,72},{9,... | collective-permute-start | bytes 245768 | tf_op jit(solution)/shard_map/ppermute | solution.py:30
  10.8 9.0 %collective-permute-start.6 = (f32[10,8,256]{2,1,0:T(8,128)S(1)}, f32[10,8,256]{2,1,0:T(8,128)S(1)}, u32[]{:S(2)}, u32[]{:S(2)}) collective-permute-start(f32[10,8,256]{2,1,0:T(8,128)S(1)} %get-tuple-element.22), channel_id=1, source_target_pairs={{0,192},{1,193},{2,194},{3,195},{4,196},{5,197},{6,198},{7,199},{8... | collective-permute-start | bytes 245768 | tf_op jit(solution)/shard_map/ppermute | solution.py:30
  12.3 7.4 %collective-permute-start.7 = (f32[10,8,256]{2,1,0:T(8,128)S(1)}, f32[10,8,256]{2,1,0:T(8,128)S(1)}, u32[]{:S(2)}, u32[]{:S(2)}) collective-permute-start(f32[10,8,256]{2,1,0:T(8,128)S(1)} %get-tuple-element.23), channel_id=1, source_target_pairs={{0,128},{1,129},{2,130},{3,131},{4,132},{5,133},{6,134},{7,135},{8... | collective-permute-start | bytes 245768 | tf_op jit(solution)/shard_map/ppermute | solution.py:30
  17.0 5.3 %collective-permute-start.2 = (f32[9,8,256]{2,1,0:T(8,128)S(1)}, f32[9,8,256]{2,1,0:T(8,128)S(1)}, u32[]{:S(2)}, u32[]{:S(2)}) collective-permute-start(f32[9,8,256]{2,1,0:T(8,128)S(1)} %get-tuple-element.18), channel_id=1, source_target_pairs={{0,64},{1,65},{2,66},{3,67},{4,68},{5,69},{6,70},{7,71},{8,72},{9,... | collective-permute-start | bytes 221192 | tf_op jit(solution)/shard_map/ppermute | solution.py:30
  17.1 5.2 %collective-permute-start.3 = (f32[9,8,256]{2,1,0:T(8,128)S(1)}, f32[9,8,256]{2,1,0:T(8,128)S(1)}, u32[]{:S(2)}, u32[]{:S(2)}) collective-permute-start(f32[9,8,256]{2,1,0:T(8,128)S(1)} %get-tuple-element.19), channel_id=1, source_target_pairs={{0,192},{1,193},{2,194},{3,195},{4,196},{5,197},{6,198},{7,199},{8... | collective-permute-start | bytes 221192 | tf_op jit(solution)/shard_map/ppermute | solution.py:30
  19.8 4.7 %collective-permute-start.4 = (f32[9,8,256]{2,1,0:T(8,128)S(1)}, f32[9,8,256]{2,1,0:T(8,128)S(1)}, u32[]{:S(2)}, u32[]{:S(2)}) collective-permute-start(f32[9,8,256]{2,1,0:T(8,128)S(1)} %get-tuple-element.20), channel_id=1, source_target_pairs={{0,128},{1,129},{2,130},{3,131},{4,132},{5,133},{6,134},{7,135},{8... | collective-permute-start | bytes 221192 | tf_op jit(solution)/shard_map/ppermute | solution.py:30
  24.5 8.9 %collective-permute-start.8 = (f32[13,8,256]{2,1,0:T(8,128)S(1)}, f32[13,8,256]{2,1,0:T(8,128)S(1)}, u32[]{:S(2)}, u32[]{:S(2)}) collective-permute-start(f32[13,8,256]{2,1,0:T(8,128)S(1)} %get-tuple-element.27), channel_id=1, source_target_pairs={{0,32},{1,33},{2,34},{3,35},{4,36},{5,37},{6,38},{7,39},{8,40},{9,... | collective-permute-start | bytes 319496 | tf_op jit(solution)/shard_map/ppermute | solution.py:30
  33.6 1.7 %collective-permute-start.9 = (f32[8,16,256]{2,1,0:T(8,128)S(1)}, f32[8,16,256]{2,1,0:T(8,128)S(1)}, u32[]{:S(2)}, u32[]{:S(2)}) collective-permute-start(f32[8,16,256]{2,1,0:T(8,128)S(1)} %pad_maximum_fusion.1.block), channel_id=1, source_target_pairs={{0,1},{1,0},{2,3},{3,2},{4,5},{5,4},{6,7},{7,6},{8,9},{9,8},{10,11... | collective-permute-start | bytes 393224 | tf_op jit(solution)/shard_map/ppermute | solution.py:30
  35.3 7.9 %collective-permute-start.10 = (f32[11,16,256]{2,1,0:T(8,128)S(1)}, f32[11,16,256]{2,1,0:T(8,128)S(1)}, u32[]{:S(2)}, u32[]{:S(2)}) collective-permute-start(f32[11,16,256]{2,1,0:T(8,128)S(1)} %pad_maximum_fusion), channel_id=1, source_target_pairs={{1,2},{2,1},{3,4},{4,3},{5,6},{6,5},{7,8},{8,7},{9,10},{10,9},{11,... | collective-permute-start | bytes 540680 | tf_op jit(solution)/shard_map/ppermute | solution.py:30
  43.2 1.2 %collective-permute-start.11 = (f32[3,16,256]{2,1,0:T(8,128)S(1)}, f32[3,16,256]{2,1,0:T(8,128)S(1)}, u32[]{:S(2)}, u32[]{:S(2)}) collective-permute-start(f32[3,16,256]{2,1,0:T(8,128)S(1)} %slice.29), channel_id=1, source_target_pairs={{0,1},{1,0},{2,3},{3,2},{4,5},{5,4},{6,7},{7,6},{8,9},{9,8},{10,11... | collective-permute-start | bytes 147464 | tf_op jit(solution)/shard_map/ppermute | solution.py:30

commit v11 on v10

--- a/solution.py
+++ b/solution.py
@@ -74,7 +74,7 @@
         total = [None] * 3
         for i in range(2):
             for v in range(5):
-                step = got[i, v, span, :].astype(F32) - a[i, v, span, :].astype(F32)
+                step = got[i][v, span, :].astype(F32) - a[i, v, span, :].astype(F32)
                 for k in range(3):
                     term = f[i, v, k, slab, span, :].astype(F32) * step
                     total[k] = term if total[k] is None else total[k] + term
@@ -89,9 +89,9 @@
             out[k * 3 : k * 3 + 3] = wide[k, pl.ds(first, 24), :].reshape(3, 8, 256)
 
 
-def sens_early_kernel(f, a, got, shift, m0, m1, m2, m3, wide):
+def sens_early_kernel(f, a, got0, got1, shift, m0, m1, m2, m3, wide):
     core = lax.axis_index("core")
-    sens_of_slab(1 - core, jnp.where(core == 0, 1.0, -1.0), f, a, got, wide)
+    sens_of_slab(1 - core, jnp.where(core == 0, 1.0, -1.0), f, a, (got0, got1), wide)
     cut(lax.axis_index("y"), wide, (m0, m1, m2, m3))
     for out, span in ((m1, slice(6, 8)), (m2, slice(6, 8)), (m3, slice(0, 2))):
         for x in range(2):
@@ -101,7 +101,7 @@
 
 def sens_late_kernel(f, a, got, after, m0, m1, m2, m3, wide):
     core = lax.axis_index("core")
-    sens_of_slab(core, jnp.where(core == 0, -1.0, 1.0), f, a, got, wide)
+    sens_of_slab(core, jnp.where(core == 0, -1.0, 1.0), f, a, (got.at[0], got.at[1]), wide)
     cut(lax.axis_index("y"), wide, (m0, m1, m2, m3))
 
 
@@ -301,12 +301,12 @@
     outer = lax.dynamic_index_in_dim(adjoint, core, 2, False)
     inner = lax.dynamic_index_in_dim(adjoint, 1 - core, 2, False)
     got_outer = send_pair(outer)
-    got_inner = send_core(inner)
+    got_inner = [send_core(inner[i]) for i in range(2)]
 
     six, nine, ten = (6, 8, 256), (9, 8, 256), (10, 8, 256)
     wide = [pltpu.VMEM((3, 72, 256), F32)]
     m0, m1, m2, m3 = call(
-        sens_early_kernel, [nine, ten, ten, ten], (flux_jac, outer, got_inner, shift), wide
+        sens_early_kernel, [nine, ten, ten, ten], (flux_jac, outer, *got_inner, shift), wide
     )
     r2, r1, r3 = send_y(m2, 2), send_y(m1, 1), send_y(m3, 3)
     n0, n1, n2, n3 = call(sens_late_kernel, [nine] * 4, (flux_jac, inner, got_outer, m0), wide)

time: 77.6 us -> 77.1 us (level)
  starting transfers between devices: 22.4 us -> 27.8 us
  waiting for transfers between devices: 17.1 us -> 12.8 us
  local copies, waits for them, and re-layouts: 3.58 us -> 1.54 us
    ppermute x12 -> x13, starting transfers between devices: 22.4 us -> 27.8 us  [send(): return lax.ppermute(v, AXES, pairs)]
    ppermute x12 -> x13, waiting for transfers between devices: 17.1 us -> 12.8 us  [send(): return lax.ppermute(v, AXES, pairs)]
    squeeze x1, local copies, waits for them, and re-layouts: 1.13 us -> 0.02 us  [local(): got_inner = [send_core(inner[i]) for i in range(2)]]
    unnamed x6 -> x5, local copies, waits for them, and re-layouts: 2.26 us -> 1.33 us
  transfers between devices with their start and end apart: 12 -> 13, of which waited for: 7 -> 8; matrix products, arithmetic and copies ran while one was open for 0% -> 0% of each run, Pallas kernels for 1% -> 1%
where the time goes in v11:
time: 77.1 us; the launch traced here: 76.9 us
  blocking collectives  31.4 us (41%)
  starting transfers between devices  27.8 us (36%)
  waiting for transfers between devices  12.8 us (17%)
  Pallas kernels  2.5 us (3%)
  local copies, waits for them, and re-layouts  1.54 us (2%)
    ppermute x13, starting transfers between devices, send(): return lax.ppermute(v, AXES, pairs)  27.8 us
    all_to_all x1, blocking collectives, local(): lax.all_to_all(jnp.broadcast_to(moments, (16, 8, 128)), ('zh', 'zl', 'cor...  18 us
    all_to_all x1, blocking collectives, local(): lax.all_to_all(jnp.broadcast_to(moments, (16, 8, 128)), ('y', 'x'), 0, 0)  13.5 us
    ppermute x13, waiting for transfers between devices, send(): return lax.ppermute(v, AXES, pairs)  12.8 us
    pallas_call x6, Pallas kernels, call(): pl.pallas_call(kernel, out_shape=[jax.ShapeDtypeStruct(s, F32) for s in o...  2.5 us
  transfers between devices with their start and end apart: 13, of which 8 were waited for; matrix products, arithmetic and copies ran while one was open for 0% of the time, Pallas kernels for 1%

profile of v11, /device:TPU:1, one launch (start us, length us, event | category | flops | bytes accessed | tf_op | source)
XLA Modules:
  0.0 76.9 jit_solution(2756897642787606553)
XLA Ops:
  0.6 0.0 copy-start
  0.6 0.0 copy-start.1
  0.7 1.3 %dynamic-slice_bitcast_fusion.2 = (bf16[2,5,1,64,256]{4,3,1,2,0:T(8,128)(2,1)S(1)}, bf16[2,5,64,256]{3,2,1,0:T(8,128)(2,1)S(1)}, bf16[2,5,64,256]{3,2,1,0:T(8,128)(2,1)S(1)}) fusion(bf16[2,5,2,64,256]{4,3,2,1,0:T(8,128)(2,1)} %param.3, s32[]{:T(128)S(6)} %select_n.7, s32[]{:T(128)S(6)} %select_n.8), kind=kLoop, calls=%fused_computation.2 | loop fusion | bytes 1638408
  2.0 4.9 %collective-permute-start = (bf16[2,5,64,256]{3,2,1,0:T(8,128)(2,1)S(1)}, bf16[2,5,64,256]{3,2,1,0:T(8,128)(2,1)S(1)}, u32[]{:S(2)}, u32[]{:S(2)}) collective-permute-start(bf16[2,5,64,256]{3,2,1,0:T(8,128)(2,1)S(1)} %get-tuple-element.32.a), channel_id=1, source_target_pairs={{1,2},{2,1},{3,4},{4,3},{5,6},{6,5},{7,8},{8,7},{9,10},{10,9},{11,... | collective-permute-start | bytes 983048 | tf_op jit(solution)/shard_map/ppermute | solution.py:30
  7.0 0.1 collective-permute-start.1
  7.1 0.5 collective-permute-start.2
  7.6 0.9 %collective-permute-done.1.got0 = bf16[5,64,256]{2,1,0:T(8,128)(2,1)S(1)} collective-permute-done((bf16[5,64,256]{2,1,0:T(8,128)(2,1)S(1)}, bf16[5,64,256]{2,1,0:T(8,128)(2,1)S(1)}, u32[]{:S(2)}, u32[]{:S(2)}) %collective-permute-start.1) | collective-permute-done | bytes 163872 | tf_op jit(solution)/shard_map/ppermute | solution.py:30
  8.4 0.2 collective-permute-done.2.got1
  8.7 0.0 copy-done
  8.7 0.0 copy-done.1
  8.7 0.3 shard_map.50
  9.0 1.4 %collective-permute-start.6 = (f32[10,8,256]{2,1,0:T(8,128)S(1)}, f32[10,8,256]{2,1,0:T(8,128)S(1)}, u32[]{:S(2)}, u32[]{:S(2)}) collective-permute-start(f32[10,8,256]{2,1,0:T(8,128)S(1)} %get-tuple-element.21), channel_id=1, source_target_pairs={{0,64},{1,65},{2,66},{3,67},{4,68},{5,69},{6,70},{7,71},{8,72},{9,... | collective-permute-start | bytes 245768 | tf_op jit(solution)/shard_map/ppermute | solution.py:30
  10.4 1.5 %collective-permute-start.7 = (f32[10,8,256]{2,1,0:T(8,128)S(1)}, f32[10,8,256]{2,1,0:T(8,128)S(1)}, u32[]{:S(2)}, u32[]{:S(2)}) collective-permute-start(f32[10,8,256]{2,1,0:T(8,128)S(1)} %get-tuple-element.22), channel_id=1, source_target_pairs={{0,192},{1,193},{2,194},{3,195},{4,196},{5,197},{6,198},{7,199},{8... | collective-permute-start | bytes 245768 | tf_op jit(solution)/shard_map/ppermute | solution.py:30
  11.9 1.6 %collective-permute-start.8 = (f32[10,8,256]{2,1,0:T(8,128)S(1)}, f32[10,8,256]{2,1,0:T(8,128)S(1)}, u32[]{:S(2)}, u32[]{:S(2)}) collective-permute-start(f32[10,8,256]{2,1,0:T(8,128)S(1)} %get-tuple-element.23), channel_id=1, source_target_pairs={{0,128},{1,129},{2,130},{3,131},{4,132},{5,133},{6,134},{7,135},{8... | collective-permute-start | bytes 245768 | tf_op jit(solution)/shard_map/ppermute | solution.py:30
  13.4 0.0 collective-permute-done.got
  13.4 0.3 shard_map.51
  13.7 1.5 %collective-permute-start.3 = (f32[9,8,256]{2,1,0:T(8,128)S(1)}, f32[9,8,256]{2,1,0:T(8,128)S(1)}, u32[]{:S(2)}, u32[]{:S(2)}) collective-permute-start(f32[9,8,256]{2,1,0:T(8,128)S(1)} %get-tuple-element.18), channel_id=1, source_target_pairs={{0,64},{1,65},{2,66},{3,67},{4,68},{5,69},{6,70},{7,71},{8,72},{9,... | collective-permute-start | bytes 221192 | tf_op jit(solution)/shard_map/ppermute | solution.py:30
  15.2 1.5 %collective-permute-start.4 = (f32[9,8,256]{2,1,0:T(8,128)S(1)}, f32[9,8,256]{2,1,0:T(8,128)S(1)}, u32[]{:S(2)}, u32[]{:S(2)}) collective-permute-start(f32[9,8,256]{2,1,0:T(8,128)S(1)} %get-tuple-element.19), channel_id=1, source_target_pairs={{0,192},{1,193},{2,194},{3,195},{4,196},{5,197},{6,198},{7,199},{8... | collective-permute-start | bytes 221192 | tf_op jit(solution)/shard_map/ppermute | solution.py:30
  16.7 0.0 collective-permute-done.6.r1
  16.7 1.6 %collective-permute-start.5 = (f32[9,8,256]{2,1,0:T(8,128)S(1)}, f32[9,8,256]{2,1,0:T(8,128)S(1)}, u32[]{:S(2)}, u32[]{:S(2)}) collective-permute-start(f32[9,8,256]{2,1,0:T(8,128)S(1)} %get-tuple-element.20), channel_id=1, source_target_pairs={{0,128},{1,129},{2,130},{3,131},{4,132},{5,133},{6,134},{7,135},{8... | collective-permute-start | bytes 221192 | tf_op jit(solution)/shard_map/ppermute | solution.py:30
  18.3 0.0 collective-permute-done.7.r3
  18.3 0.0 collective-permute-done.8.r2
  18.3 0.3 collective-permute-done.3.r1
  18.6 0.0 collective-permute-done.4.r3
  18.6 2.8 %collective-permute-done.5.r2 = f32[9,8,256]{2,1,0:T(8,128)S(1)} collective-permute-done((f32[9,8,256]{2,1,0:T(8,128)S(1)}, f32[9,8,256]{2,1,0:T(8,128)S(1)}, u32[]{:S(2)}, u32[]{:S(2)}) %collective-permute-start.5) | collective-permute-done | bytes 73760 | tf_op jit(solution)/shard_map/ppermute | solution.py:30
  21.5 5.9 %collective-permute-start.9 = (f32[13,8,256]{2,1,0:T(8,128)S(1)}, f32[13,8,256]{2,1,0:T(8,128)S(1)}, u32[]{:S(2)}, u32[]{:S(2)}) collective-permute-start(f32[13,8,256]{2,1,0:T(8,128)S(1)} %get-tuple-element.27), channel_id=1, source_target_pairs={{0,32},{1,33},{2,34},{3,35},{4,36},{5,37},{6,38},{7,39},{8,40},{9,... | collective-permute-start | bytes 319496 | tf_op jit(solution)/shard_map/ppermute | solution.py:30
  27.3 2.1 %collective-permute-done.9 = f32[13,8,256]{2,1,0:T(8,128)S(1)} collective-permute-done((f32[13,8,256]{2,1,0:T(8,128)S(1)}, f32[13,8,256]{2,1,0:T(8,128)S(1)}, u32[]{:S(2)}, u32[]{:S(2)}) %collective-permute-start.9) | collective-permute-done | bytes 106528 | tf_op jit(solution)/shard_map/ppermute | solution.py:30
  29.5 0.1 concatenate.10
  29.6 4.9 %collective-permute-start.10 = (f32[8,16,256]{2,1,0:T(8,128)S(1)}, f32[8,16,256]{2,1,0:T(8,128)S(1)}, u32[]{:S(2)}, u32[]{:S(2)}) collective-permute-start(f32[8,16,256]{2,1,0:T(8,128)S(1)} %pad_maximum_fusion.1.block), channel_id=1, source_target_pairs={{0,1},{1,0},{2,3},{3,2},{4,5},{5,4},{6,7},{7,6},{8,9},{9,8},{10,11... | collective-permute-start | bytes 393224 | tf_op jit(solution)/shard_map/ppermute | solution.py:30
  34.5 1.0 %collective-permute-done.10.mate = f32[8,16,256]{2,1,0:T(8,128)S(1)} collective-permute-done((f32[8,16,256]{2,1,0:T(8,128)S(1)}, f32[8,16,256]{2,1,0:T(8,128)S(1)}, u32[]{:S(2)}, u32[]{:S(2)}) %collective-permute-start.10) | collective-permute-done | bytes 131104 | tf_op jit(solution)/shard_map/ppermute | solution.py:30
  35.5 2.5 %collective-permute-start.11 = (f32[11,16,256]{2,1,0:T(8,128)S(1)}, f32[11,16,256]{2,1,0:T(8,128)S(1)}, u32[]{:S(2)}, u32[]{:S(2)}) collective-permute-start(f32[11,16,256]{2,1,0:T(8,128)S(1)} %pad_maximum_fusion), channel_id=1, source_target_pairs={{1,2},{2,1},{3,4},{4,3},{5,6},{6,5},{7,8},{8,7},{9,10},{10,9},{11,... | collective-permute-start | bytes 540680 | tf_op jit(solution)/shard_map/ppermute | solution.py:30
  38.1 4.3 %collective-permute-done.11.far = f32[11,16,256]{2,1,0:T(8,128)S(1)} collective-permute-done((f32[11,16,256]{2,1,0:T(8,128)S(1)}, f32[11,16,256]{2,1,0:T(8,128)S(1)}, u32[]{:S(2)}, u32[]{:S(2)}) %collective-permute-start.11) | collective-permute-done | bytes 180256 | tf_op jit(solution)/shard_map/ppermute | solution.py:30
  42.3 0.0 collective-permute-start.12
  42.3 1.2 %collective-permute-done.12.beyond = f32[3,16,256]{2,1,0:T(8,128)S(1)} collective-permute-done((f32[3,16,256]{2,1,0:T(8,128)S(1)}, f32[3,16,256]{2,1,0:T(8,128)S(1)}, u32[]{:S(2)}, u32[]{:S(2)}) %collective-permute-start.12) | collective-permute-done | bytes 49184 | tf_op jit(solution)/shard_map/ppermute | solution.py:30
  43.6 0.9 %shard_map.54 = (f32[4,3,2,8,256]{4,3,2,1,0:T(8,128)S(1)}, f32[8,128]{1,0:T(8,128)S(1)}) custom-call(f32[8,16,256]{2,1,0:T(8,128)S(1)} %pad_maximum_fusion.1.block, f32[8,16,256]{2,1,0:T(8,128)S(1)} %collective-permute-done.10.mate, f32[11,16,256]{2,1,0:T(8,128)S(1)} %collective-permute-done.11.far, f32[3,16,256]{2,1,0:T(8,128)S(1)} %collective-permute-done.12.beyond), custom_call_target="tpu_custom_call" | custom-call | tf_op jit(solution)/shard_map/pallas_call | solution.py:57
  44.4 18.0 %all_to_all.10 = f32[16,8,128]{2,1,0:T(8,128)S(1)} all-to-all(f32[16,8,128]{2,1,0:T(8,128)S(1)} %broadcast_in_dim.14), channel_id=1, replica_groups=mesh['y'=4,'zh'=2,'x'=4,'zl'=4,'core'=2] {'zh','zl','core'}, dimensions={0} | all-to-all | bytes 131072 | tf_op jit(solution)/shard_map/all_to_all | solution.py:332
  62.4 13.5 %all_to_all.11.parts = f32[16,8,128]{2,1,0:T(8,128)S(1)} all-to-all(f32[16,8,128]{2,1,0:T(8,128)S(1)} %broadcast_in_dim.15), channel_id=1, replica_groups=mesh['y'=4,'zh'=2,'x'=4,'zl'=4,'core'=2] {'y','x'}, dimensions={0} | all-to-all | bytes 131072 | tf_op jit(solution)/shard_map/all_to_all | solution.py:334
  75.9 1.0 %shard_map.55 = (f32[3,2,8,256]{3,2,1,0:T(8,128)}, f32[3,2,8,256]{3,2,1,0:T(8,128)}) custom-call(f32[16,8,128]{2,1,0:T(8,128)S(1)} %all_to_all.11.parts, f32[4,3,2,8,256]{4,3,2,1,0:T(8,128)S(1)} %get-tuple-element.29.basis), custom_call_target="tpu_custom_call" | custom-call | tf_op jit(solution)/shard_map/pallas_call | solution.py:57
  (16 shorter events, 0.2 us)
Async XLA Ops:
  0.6 8.1 %copy-start = (bf16[2,5,3,2,64,256]{5,4,3,2,1,0:T(8,128)(2,1)S(1)}, bf16[2,5,3,2,64,256]{5,4,3,2,1,0:T(8,128)(2,1)}, u32[]{:S(2)}) copy-start(bf16[2,5,3,2,64,256]{5,4,3,2,1,0:T(8,128)(2,1)} %f.3) | copy-start | bytes 5898244
  0.6 8.0 %copy-start.1 = (f32[2,8,256]{2,1,0:T(8,128)S(1)}, f32[2,8,256]{2,1,0:T(8,128)}, u32[]{:S(2)}) copy-start(f32[2,8,256]{2,1,0:T(8,128)} %shift.3) | copy-start | bytes 49156
  2.0 11.5 %collective-permute-start = (bf16[2,5,64,256]{3,2,1,0:T(8,128)(2,1)S(1)}, bf16[2,5,64,256]{3,2,1,0:T(8,128)(2,1)S(1)}, u32[]{:S(2)}, u32[]{:S(2)}) collective-permute-start(bf16[2,5,64,256]{3,2,1,0:T(8,128)(2,1)S(1)} %get-tuple-element.32.a), channel_id=1, source_target_pairs={{1,2},{2,1},{3,4},{4,3},{5,6},{6,5},{7,8},{8,7},{9,10},{10,9},{11,... | collective-permute-start | bytes 983048 | tf_op jit(solution)/shard_map/ppermute | solution.py:30
  7.0 1.5 %collective-permute-start.1 = (bf16[5,64,256]{2,1,0:T(8,128)(2,1)S(1)}, bf16[5,64,256]{2,1,0:T(8,128)(2,1)S(1)}, u32[]{:S(2)}, u32[]{:S(2)}) collective-permute-start(bf16[5,64,256]{2,1,0:T(8,128)(2,1)S(1)} %get-tuple-element.34), channel_id=1, source_target_pairs={{0,1},{1,0},{2,3},{3,2},{4,5},{5,4},{6,7},{7,6},{8,9},{9,8},{10,11... | collective-permute-start | bytes 491528 | tf_op jit(solution)/shard_map/ppermute | solution.py:30
  7.1 1.6 %collective-permute-start.2 = (bf16[5,64,256]{2,1,0:T(8,128)(2,1)S(1)}, bf16[5,64,256]{2,1,0:T(8,128)(2,1)S(1)}, u32[]{:S(2)}, u32[]{:S(2)}) collective-permute-start(bf16[5,64,256]{2,1,0:T(8,128)(2,1)S(1)} %get-tuple-element.33), channel_id=1, source_target_pairs={{0,1},{1,0},{2,3},{3,2},{4,5},{5,4},{6,7},{7,6},{8,9},{9,8},{10,11... | collective-permute-start | bytes 491528 | tf_op jit(solution)/shard_map/ppermute | solution.py:30
  9.0 7.7 %collective-permute-start.6 = (f32[10,8,256]{2,1,0:T(8,128)S(1)}, f32[10,8,256]{2,1,0:T(8,128)S(1)}, u32[]{:S(2)}, u32[]{:S(2)}) collective-permute-start(f32[10,8,256]{2,1,0:T(8,128)S(1)} %get-tuple-element.21), channel_id=1, source_target_pairs={{0,64},{1,65},{2,66},{3,67},{4,68},{5,69},{6,70},{7,71},{8,72},{9,... | collective-permute-start | bytes 245768 | tf_op jit(solution)/shard_map/ppermute | solution.py:30
  10.4 7.9 %collective-permute-start.7 = (f32[10,8,256]{2,1,0:T(8,128)S(1)}, f32[10,8,256]{2,1,0:T(8,128)S(1)}, u32[]{:S(2)}, u32[]{:S(2)}) collective-permute-start(f32[10,8,256]{2,1,0:T(8,128)S(1)} %get-tuple-element.22), channel_id=1, source_target_pairs={{0,192},{1,193},{2,194},{3,195},{4,196},{5,197},{6,198},{7,199},{8... | collective-permute-start | bytes 245768 | tf_op jit(solution)/shard_map/ppermute | solution.py:30
  11.9 6.4 %collective-permute-start.8 = (f32[10,8,256]{2,1,0:T(8,128)S(1)}, f32[10,8,256]{2,1,0:T(8,128)S(1)}, u32[]{:S(2)}, u32[]{:S(2)}) collective-permute-start(f32[10,8,256]{2,1,0:T(8,128)S(1)} %get-tuple-element.23), channel_id=1, source_target_pairs={{0,128},{1,129},{2,130},{3,131},{4,132},{5,133},{6,134},{7,135},{8... | collective-permute-start | bytes 245768 | tf_op jit(solution)/shard_map/ppermute | solution.py:30
  13.7 4.9 %collective-permute-start.3 = (f32[9,8,256]{2,1,0:T(8,128)S(1)}, f32[9,8,256]{2,1,0:T(8,128)S(1)}, u32[]{:S(2)}, u32[]{:S(2)}) collective-permute-start(f32[9,8,256]{2,1,0:T(8,128)S(1)} %get-tuple-element.18), channel_id=1, source_target_pairs={{0,64},{1,65},{2,66},{3,67},{4,68},{5,69},{6,70},{7,71},{8,72},{9,... | collective-permute-start | bytes 221192 | tf_op jit(solution)/shard_map/ppermute | solution.py:30
  15.2 3.4 %collective-permute-start.4 = (f32[9,8,256]{2,1,0:T(8,128)S(1)}, f32[9,8,256]{2,1,0:T(8,128)S(1)}, u32[]{:S(2)}, u32[]{:S(2)}) collective-permute-start(f32[9,8,256]{2,1,0:T(8,128)S(1)} %get-tuple-element.19), channel_id=1, source_target_pairs={{0,192},{1,193},{2,194},{3,195},{4,196},{5,197},{6,198},{7,199},{8... | collective-permute-start | bytes 221192 | tf_op jit(solution)/shard_map/ppermute | solution.py:30
  16.7 4.7 %collective-permute-start.5 = (f32[9,8,256]{2,1,0:T(8,128)S(1)}, f32[9,8,256]{2,1,0:T(8,128)S(1)}, u32[]{:S(2)}, u32[]{:S(2)}) collective-permute-start(f32[9,8,256]{2,1,0:T(8,128)S(1)} %get-tuple-element.20), channel_id=1, source_target_pairs={{0,128},{1,129},{2,130},{3,131},{4,132},{5,133},{6,134},{7,135},{8... | collective-permute-start | bytes 221192 | tf_op jit(solution)/shard_map/ppermute | solution.py:30
  21.5 8.0 %collective-permute-start.9 = (f32[13,8,256]{2,1,0:T(8,128)S(1)}, f32[13,8,256]{2,1,0:T(8,128)S(1)}, u32[]{:S(2)}, u32[]{:S(2)}) collective-permute-start(f32[13,8,256]{2,1,0:T(8,128)S(1)} %get-tuple-element.27), channel_id=1, source_target_pairs={{0,32},{1,33},{2,34},{3,35},{4,36},{5,37},{6,38},{7,39},{8,40},{9,... | collective-permute-start | bytes 319496 | tf_op jit(solution)/shard_map/ppermute | solution.py:30
  29.6 5.8 %collective-permute-start.10 = (f32[8,16,256]{2,1,0:T(8,128)S(1)}, f32[8,16,256]{2,1,0:T(8,128)S(1)}, u32[]{:S(2)}, u32[]{:S(2)}) collective-permute-start(f32[8,16,256]{2,1,0:T(8,128)S(1)} %pad_maximum_fusion.1.block), channel_id=1, source_target_pairs={{0,1},{1,0},{2,3},{3,2},{4,5},{5,4},{6,7},{7,6},{8,9},{9,8},{10,11... | collective-permute-start | bytes 393224 | tf_op jit(solution)/shard_map/ppermute | solution.py:30
  35.5 6.8 %collective-permute-start.11 = (f32[11,16,256]{2,1,0:T(8,128)S(1)}, f32[11,16,256]{2,1,0:T(8,128)S(1)}, u32[]{:S(2)}, u32[]{:S(2)}) collective-permute-start(f32[11,16,256]{2,1,0:T(8,128)S(1)} %pad_maximum_fusion), channel_id=1, source_target_pairs={{1,2},{2,1},{3,4},{4,3},{5,6},{6,5},{7,8},{8,7},{9,10},{10,9},{11,... | collective-permute-start | bytes 540680 | tf_op jit(solution)/shard_map/ppermute | solution.py:30
  42.3 1.2 %collective-permute-start.12 = (f32[3,16,256]{2,1,0:T(8,128)S(1)}, f32[3,16,256]{2,1,0:T(8,128)S(1)}, u32[]{:S(2)}, u32[]{:S(2)}) collective-permute-start(f32[3,16,256]{2,1,0:T(8,128)S(1)} %slice.41), channel_id=1, source_target_pairs={{0,1},{1,0},{2,3},{3,2},{4,5},{5,4},{6,7},{7,6},{8,9},{9,8},{10,11... | collective-permute-start | bytes 147464 | tf_op jit(solution)/shard_map/ppermute | solution.py:30

commit v12 on v11

--- a/solution.py
+++ b/solution.py
@@ -74,7 +74,7 @@
         total = [None] * 3
         for i in range(2):
             for v in range(5):
-                step = got[i][v, span, :].astype(F32) - a[i, v, span, :].astype(F32)
+                step = got[i][v, span, :].astype(F32) - a[i][v, span, :].astype(F32)
                 for k in range(3):
                     term = f[i, v, k, slab, span, :].astype(F32) * step
                     total[k] = term if total[k] is None else total[k] + term
@@ -91,7 +91,7 @@
 
 def sens_early_kernel(f, a, got0, got1, shift, m0, m1, m2, m3, wide):
     core = lax.axis_index("core")
-    sens_of_slab(1 - core, jnp.where(core == 0, 1.0, -1.0), f, a, (got0, got1), wide)
+    sens_of_slab(1 - core, jnp.where(core == 0, 1.0, -1.0), f, (a.at[0], a.at[1]), (got0, got1), wide)
     cut(lax.axis_index("y"), wide, (m0, m1, m2, m3))
     for out, span in ((m1, slice(6, 8)), (m2, slice(6, 8)), (m3, slice(0, 2))):
         for x in range(2):
@@ -99,9 +99,9 @@
         out[9, 4:8, :] = jnp.zeros((4, 256), F32)
 
 
-def sens_late_kernel(f, a, got, after, m0, m1, m2, m3, wide):
+def sens_late_kernel(f, a0, a1, got, after, m0, m1, m2, m3, wide):
     core = lax.axis_index("core")
-    sens_of_slab(core, jnp.where(core == 0, -1.0, 1.0), f, a, (got.at[0], got.at[1]), wide)
+    sens_of_slab(core, jnp.where(core == 0, -1.0, 1.0), f, (a0, a1), (got.at[0], got.at[1]), wide)
     cut(lax.axis_index("y"), wide, (m0, m1, m2, m3))
 
 
@@ -299,9 +299,12 @@
 def local(adjoint, flux_jac, shift):
     core = lax.axis_index("core")
     outer = lax.dynamic_index_in_dim(adjoint, core, 2, False)
-    inner = lax.dynamic_index_in_dim(adjoint, 1 - core, 2, False)
+    inner = [
+        lax.dynamic_slice(adjoint, (i, 0, 1 - core, 0, 0), (1, 5, 1, 64, 256)).reshape(5, 64, 256)
+        for i in range(2)
+    ]
     got_outer = send_pair(outer)
-    got_inner = [send_core(inner[i]) for i in range(2)]
+    got_inner = [send_core(v) for v in inner]
 
     six, nine, ten = (6, 8, 256), (9, 8, 256), (10, 8, 256)
     wide = [pltpu.VMEM((3, 72, 256), F32)]
@@ -309,7 +312,7 @@
         sens_early_kernel, [nine, ten, ten, ten], (flux_jac, outer, *got_inner, shift), wide
     )
     r2, r1, r3 = send_y(m2, 2), send_y(m1, 1), send_y(m3, 3)
-    n0, n1, n2, n3 = call(sens_late_kernel, [nine] * 4, (flux_jac, inner, got_outer, m0), wide)
+    n0, n1, n2, n3 = call(sens_late_kernel, [nine] * 4, (flux_jac, *inner, got_outer, m0), wide)
     q2, q1, q3 = send_y(n2, 2), send_y(n1, 1), send_y(n3, 3)
     own, out = call(sum_y_early_kernel, [six, (7, 8, 256)], (m0, r1, r3, r2, shift, n0))
     own, out = call(sum_y_late_kernel, [(12, 8, 256), (13, 8, 256)], (n0, q1, q3, q2, own, out))

time: 77.1 us -> 77.6 us (level)
  local copies, waits for them, and re-layouts: 1.54 us -> 4.48 us
  blocking collectives: 31.4 us -> 29.2 us
  starting transfers between devices: 27.8 us -> 26.6 us
  waiting for transfers between devices: 12.8 us -> 13.6 us
    all_to_all x1, blocking collectives: 13.5 us -> 11.8 us  [local(): lax.all_to_all(jnp.broadcast_to(moments, (16, 8, 128)), ('y', 'x'), 0, 0)]
    ppermute x13, starting transfers between devices: 27.8 us -> 26.6 us  [send(): return lax.ppermute(v, AXES, pairs)]
    reshape x0 -> x1, local copies, waits for them, and re-layouts: none -> 1.03 us  [local(): lax.dynamic_slice(adjoint, (i, 0, 1 - core, 0, 0), (1, 5, 1, 64, 256))]
    squeeze x1, local copies, waits for them, and re-layouts: 0.02 us -> 1 us  [local(): outer = lax.dynamic_index_in_dim(adjoint, core, 2, False)]
    unnamed x5 -> x6, local copies, waits for them, and re-layouts: 1.33 us -> 2.27 us
    ppermute x13, waiting for transfers between devices: 12.8 us -> 13.6 us  [send(): return lax.ppermute(v, AXES, pairs)]
  transfers between devices with their start and end apart: 13 -> 13, of which waited for: 8 -> 8; matrix products, arithmetic and copies ran while one was open for 0% -> 1% of each run, Pallas kernels for 1% -> 1%
where the time goes in v12:
time: 77.6 us; the launch traced here: 77.3 us
  blocking collectives  29.2 us (38%)
  starting transfers between devices  26.6 us (34%)
  waiting for transfers between devices  13.6 us (18%)
  local copies, waits for them, and re-layouts  4.48 us (6%)
  Pallas kernels  2.51 us (3%)
    ppermute x13, starting transfers between devices, send(): return lax.ppermute(v, AXES, pairs)  26.6 us
    all_to_all x1, blocking collectives, local(): lax.all_to_all(jnp.broadcast_to(moments, (16, 8, 128)), ('zh', 'zl', 'cor...  17.4 us
    ppermute x13, waiting for transfers between devices, send(): return lax.ppermute(v, AXES, pairs)  13.6 us
    all_to_all x1, blocking collectives, local(): lax.all_to_all(jnp.broadcast_to(moments, (16, 8, 128)), ('y', 'x'), 0, 0)  11.8 us
    pallas_call x6, Pallas kernels, call(): pl.pallas_call(kernel, out_shape=[jax.ShapeDtypeStruct(s, F32) for s in o...  2.51 us
    unnamed x6, local copies, waits for them, and re-layouts  2.27 us
  transfers between devices with their start and end apart: 13, of which 8 were waited for; matrix products, arithmetic and copies ran while one was open for 1% of the time, Pallas kernels for 1%

profile of v12, /device:TPU:1, one launch (start us, length us, event | category | flops | bytes accessed | tf_op | source)
XLA Modules:
  0.0 77.3 jit_solution(3960056944276647148)
XLA Ops:
  0.6 1.0 %dynamic-slice_bitcast_fusion.a = bf16[2,5,64,256]{3,2,1,0:T(8,128)(2,1)S(1)} fusion(bf16[2,5,2,64,256]{4,3,2,1,0:T(8,128)(2,1)} %param.3, s32[]{:T(128)S(6)} %select_n.9), kind=kLoop, calls=%fused_computation | loop fusion | bytes 655364 | tf_op jit(solution)/shard_map/jit(dynamic_index_in_dim)/squeeze | solution.py:301
  1.6 4.9 %collective-permute-start = (bf16[2,5,64,256]{3,2,1,0:T(8,128)(2,1)S(1)}, bf16[2,5,64,256]{3,2,1,0:T(8,128)(2,1)S(1)}, u32[]{:S(2)}, u32[]{:S(2)}) collective-permute-start(bf16[2,5,64,256]{3,2,1,0:T(8,128)(2,1)S(1)} %dynamic-slice_bitcast_fusion.a), channel_id=1, source_target_pairs={{1,2},{2,1},{3,4},{4,3},{5,6},{6,5},{7,8},{8,7},{9,10},{10,9},{11,... | collective-permute-start | bytes 983048 | tf_op jit(solution)/shard_map/ppermute | solution.py:30
  6.6 1.0 %dynamic-slice_bitcast_fusion.1 = (bf16[5,64,256]{2,1,0:T(8,128)(2,1)S(1)}, bf16[5,64,256]{2,1,0:T(8,128)(2,1)S(1)}) fusion(bf16[2,5,2,64,256]{4,3,2,1,0:T(8,128)(2,1)} %param.3, s32[]{:T(128)S(6)} %select_n.8), kind=kLoop, calls=%fused_computation.2 | loop fusion | bytes 655364 | tf_op jit(solution)/shard_map/reshape | solution.py:303
  7.6 0.1 collective-permute-start.1
  7.7 0.5 collective-permute-start.2
  8.2 0.9 %collective-permute-done.1.got0 = bf16[5,64,256]{2,1,0:T(8,128)(2,1)S(1)} collective-permute-done((bf16[5,64,256]{2,1,0:T(8,128)(2,1)S(1)}, bf16[5,64,256]{2,1,0:T(8,128)(2,1)S(1)}, u32[]{:S(2)}, u32[]{:S(2)}) %collective-permute-start.1) | collective-permute-done | bytes 163872 | tf_op jit(solution)/shard_map/ppermute | solution.py:30
  9.1 0.2 collective-permute-done.2.got1
  9.3 0.0 copy-start
  9.3 1.5 %copy-done = bf16[2,5,3,2,64,256]{5,4,3,2,1,0:T(8,128)(2,1)S(1)} copy-done((bf16[2,5,3,2,64,256]{5,4,3,2,1,0:T(8,128)(2,1)S(1)}, bf16[2,5,3,2,64,256]{5,4,3,2,1,0:T(8,128)(2,1)}, u32[]{:S(2)}) %copy-start) | copy-done | bytes 1966104
  10.9 0.0 copy-start.1
  10.9 0.7 copy-done.1
  11.6 0.3 shard_map.50
  11.9 0.0 copy-start.2
  11.9 1.4 %collective-permute-start.6 = (f32[10,8,256]{2,1,0:T(8,128)S(1)}, f32[10,8,256]{2,1,0:T(8,128)S(1)}, u32[]{:S(2)}, u32[]{:S(2)}) collective-permute-start(f32[10,8,256]{2,1,0:T(8,128)S(1)} %get-tuple-element.21), channel_id=1, source_target_pairs={{0,64},{1,65},{2,66},{3,67},{4,68},{5,69},{6,70},{7,71},{8,72},{9,... | collective-permute-start | bytes 245768 | tf_op jit(solution)/shard_map/ppermute | solution.py:30
  13.3 1.5 %collective-permute-start.7 = (f32[10,8,256]{2,1,0:T(8,128)S(1)}, f32[10,8,256]{2,1,0:T(8,128)S(1)}, u32[]{:S(2)}, u32[]{:S(2)}) collective-permute-start(f32[10,8,256]{2,1,0:T(8,128)S(1)} %get-tuple-element.22), channel_id=1, source_target_pairs={{0,192},{1,193},{2,194},{3,195},{4,196},{5,197},{6,198},{7,199},{8... | collective-permute-start | bytes 245768 | tf_op jit(solution)/shard_map/ppermute | solution.py:30
  14.8 1.6 %collective-permute-start.8 = (f32[10,8,256]{2,1,0:T(8,128)S(1)}, f32[10,8,256]{2,1,0:T(8,128)S(1)}, u32[]{:S(2)}, u32[]{:S(2)}) collective-permute-start(f32[10,8,256]{2,1,0:T(8,128)S(1)} %get-tuple-element.23), channel_id=1, source_target_pairs={{0,128},{1,129},{2,130},{3,131},{4,132},{5,133},{6,134},{7,135},{8... | collective-permute-start | bytes 245768 | tf_op jit(solution)/shard_map/ppermute | solution.py:30
  16.4 0.0 collective-permute-done.got
  16.4 0.3 shard_map.51
  16.7 0.5 collective-permute-start.3
  17.1 2.3 %collective-permute-start.4 = (f32[9,8,256]{2,1,0:T(8,128)S(1)}, f32[9,8,256]{2,1,0:T(8,128)S(1)}, u32[]{:S(2)}, u32[]{:S(2)}) collective-permute-start(f32[9,8,256]{2,1,0:T(8,128)S(1)} %get-tuple-element.19), channel_id=1, source_target_pairs={{0,192},{1,193},{2,194},{3,195},{4,196},{5,197},{6,198},{7,199},{8... | collective-permute-start | bytes 221192 | tf_op jit(solution)/shard_map/ppermute | solution.py:30
  19.4 0.0 collective-permute-done.6.r1
  19.4 0.2 collective-permute-start.5
  19.6 0.0 collective-permute-done.7.r3
  19.6 0.0 collective-permute-done.8.r2
  19.6 0.0 copy-done.2
  19.7 2.1 %collective-permute-done.3.r1 = f32[9,8,256]{2,1,0:T(8,128)S(1)} collective-permute-done((f32[9,8,256]{2,1,0:T(8,128)S(1)}, f32[9,8,256]{2,1,0:T(8,128)S(1)}, u32[]{:S(2)}, u32[]{:S(2)}) %collective-permute-start.3) | collective-permute-done | bytes 73760 | tf_op jit(solution)/shard_map/ppermute | solution.py:30
  21.8 0.0 collective-permute-done.4.r3
  21.8 2.3 %collective-permute-done.5.r2 = f32[9,8,256]{2,1,0:T(8,128)S(1)} collective-permute-done((f32[9,8,256]{2,1,0:T(8,128)S(1)}, f32[9,8,256]{2,1,0:T(8,128)S(1)}, u32[]{:S(2)}, u32[]{:S(2)}) %collective-permute-start.5) | collective-permute-done | bytes 73760 | tf_op jit(solution)/shard_map/ppermute | solution.py:30
  24.2 6.1 %collective-permute-start.9 = (f32[13,8,256]{2,1,0:T(8,128)S(1)}, f32[13,8,256]{2,1,0:T(8,128)S(1)}, u32[]{:S(2)}, u32[]{:S(2)}) collective-permute-start(f32[13,8,256]{2,1,0:T(8,128)S(1)} %get-tuple-element.27), channel_id=1, source_target_pairs={{0,32},{1,33},{2,34},{3,35},{4,36},{5,37},{6,38},{7,39},{8,40},{9,... | collective-permute-start | bytes 319496 | tf_op jit(solution)/shard_map/ppermute | solution.py:30
  30.3 2.2 %collective-permute-done.9 = f32[13,8,256]{2,1,0:T(8,128)S(1)} collective-permute-done((f32[13,8,256]{2,1,0:T(8,128)S(1)}, f32[13,8,256]{2,1,0:T(8,128)S(1)}, u32[]{:S(2)}, u32[]{:S(2)}) %collective-permute-start.9) | collective-permute-done | bytes 106528 | tf_op jit(solution)/shard_map/ppermute | solution.py:30
  32.5 0.1 concatenate.10
  32.7 4.4 %collective-permute-start.10 = (f32[8,16,256]{2,1,0:T(8,128)S(1)}, f32[8,16,256]{2,1,0:T(8,128)S(1)}, u32[]{:S(2)}, u32[]{:S(2)}) collective-permute-start(f32[8,16,256]{2,1,0:T(8,128)S(1)} %pad_maximum_fusion.1.block), channel_id=1, source_target_pairs={{0,1},{1,0},{2,3},{3,2},{4,5},{5,4},{6,7},{7,6},{8,9},{9,8},{10,11... | collective-permute-start | bytes 393224 | tf_op jit(solution)/shard_map/ppermute | solution.py:30
  37.1 1.0 %collective-permute-done.10.mate = f32[8,16,256]{2,1,0:T(8,128)S(1)} collective-permute-done((f32[8,16,256]{2,1,0:T(8,128)S(1)}, f32[8,16,256]{2,1,0:T(8,128)S(1)}, u32[]{:S(2)}, u32[]{:S(2)}) %collective-permute-start.10) | collective-permute-done | bytes 131104 | tf_op jit(solution)/shard_map/ppermute | solution.py:30
  38.1 3.1 %collective-permute-start.11 = (f32[11,16,256]{2,1,0:T(8,128)S(1)}, f32[11,16,256]{2,1,0:T(8,128)S(1)}, u32[]{:S(2)}, u32[]{:S(2)}) collective-permute-start(f32[11,16,256]{2,1,0:T(8,128)S(1)} %pad_maximum_fusion), channel_id=1, source_target_pairs={{1,2},{2,1},{3,4},{4,3},{5,6},{6,5},{7,8},{8,7},{9,10},{10,9},{11,... | collective-permute-start | bytes 540680 | tf_op jit(solution)/shard_map/ppermute | solution.py:30
  41.2 3.7 %collective-permute-done.11.far = f32[11,16,256]{2,1,0:T(8,128)S(1)} collective-permute-done((f32[11,16,256]{2,1,0:T(8,128)S(1)}, f32[11,16,256]{2,1,0:T(8,128)S(1)}, u32[]{:S(2)}, u32[]{:S(2)}) %collective-permute-start.11) | collective-permute-done | bytes 180256 | tf_op jit(solution)/shard_map/ppermute | solution.py:30
  44.9 0.0 collective-permute-start.12
  44.9 1.2 %collective-permute-done.12.beyond = f32[3,16,256]{2,1,0:T(8,128)S(1)} collective-permute-done((f32[3,16,256]{2,1,0:T(8,128)S(1)}, f32[3,16,256]{2,1,0:T(8,128)S(1)}, u32[]{:S(2)}, u32[]{:S(2)}) %collective-permute-start.12) | collective-permute-done | bytes 49184 | tf_op jit(solution)/shard_map/ppermute | solution.py:30
  46.1 0.9 %shard_map.54 = (f32[4,3,2,8,256]{4,3,2,1,0:T(8,128)S(1)}, f32[8,128]{1,0:T(8,128)S(1)}) custom-call(f32[8,16,256]{2,1,0:T(8,128)S(1)} %pad_maximum_fusion.1.block, f32[8,16,256]{2,1,0:T(8,128)S(1)} %collective-permute-done.10.mate, f32[11,16,256]{2,1,0:T(8,128)S(1)} %collective-permute-done.11.far, f32[3,16,256]{2,1,0:T(8,128)S(1)} %collective-permute-done.12.beyond), custom_call_target="tpu_custom_call" | custom-call | tf_op jit(solution)/shard_map/pallas_call | solution.py:57
  47.0 17.4 %all_to_all.10 = f32[16,8,128]{2,1,0:T(8,128)S(1)} all-to-all(f32[16,8,128]{2,1,0:T(8,128)S(1)} %broadcast_in_dim.14), channel_id=1, replica_groups=mesh['y'=4,'zh'=2,'x'=4,'zl'=4,'core'=2] {'zh','zl','core'}, dimensions={0} | all-to-all | bytes 131072 | tf_op jit(solution)/shard_map/all_to_all | solution.py:335
  64.5 11.8 %all_to_all.11.parts = f32[16,8,128]{2,1,0:T(8,128)S(1)} all-to-all(f32[16,8,128]{2,1,0:T(8,128)S(1)} %broadcast_in_dim.15), channel_id=1, replica_groups=mesh['y'=4,'zh'=2,'x'=4,'zl'=4,'core'=2] {'y','x'}, dimensions={0} | all-to-all | bytes 131072 | tf_op jit(solution)/shard_map/all_to_all | solution.py:337
  76.3 1.0 %shard_map.55 = (f32[3,2,8,256]{3,2,1,0:T(8,128)}, f32[3,2,8,256]{3,2,1,0:T(8,128)}) custom-call(f32[16,8,128]{2,1,0:T(8,128)S(1)} %all_to_all.11.parts, f32[4,3,2,8,256]{4,3,2,1,0:T(8,128)S(1)} %get-tuple-element.29.basis), custom_call_target="tpu_custom_call" | custom-call | tf_op jit(solution)/shard_map/pallas_call | solution.py:57
  (15 shorter events, 0.2 us)
Async XLA Ops:
  1.6 14.7 %collective-permute-start = (bf16[2,5,64,256]{3,2,1,0:T(8,128)(2,1)S(1)}, bf16[2,5,64,256]{3,2,1,0:T(8,128)(2,1)S(1)}, u32[]{:S(2)}, u32[]{:S(2)}) collective-permute-start(bf16[2,5,64,256]{3,2,1,0:T(8,128)(2,1)S(1)} %dynamic-slice_bitcast_fusion.a), channel_id=1, source_target_pairs={{1,2},{2,1},{3,4},{4,3},{5,6},{6,5},{7,8},{8,7},{9,10},{10,9},{11,... | collective-permute-start | bytes 983048 | tf_op jit(solution)/shard_map/ppermute | solution.py:30
  7.6 1.5 %collective-permute-start.1 = (bf16[5,64,256]{2,1,0:T(8,128)(2,1)S(1)}, bf16[5,64,256]{2,1,0:T(8,128)(2,1)S(1)}, u32[]{:S(2)}, u32[]{:S(2)}) collective-permute-start(bf16[5,64,256]{2,1,0:T(8,128)(2,1)S(1)} %get-tuple-element.31.a0), channel_id=1, source_target_pairs={{0,1},{1,0},{2,3},{3,2},{4,5},{5,4},{6,7},{7,6},{8,9},{9,8},{10,11... | collective-permute-start | bytes 491528 | tf_op jit(solution)/shard_map/ppermute | solution.py:30
  7.7 1.6 %collective-permute-start.2 = (bf16[5,64,256]{2,1,0:T(8,128)(2,1)S(1)}, bf16[5,64,256]{2,1,0:T(8,128)(2,1)S(1)}, u32[]{:S(2)}, u32[]{:S(2)}) collective-permute-start(bf16[5,64,256]{2,1,0:T(8,128)(2,1)S(1)} %get-tuple-element.30.a1), channel_id=1, source_target_pairs={{0,1},{1,0},{2,3},{3,2},{4,5},{5,4},{6,7},{7,6},{8,9},{9,8},{10,11... | collective-permute-start | bytes 491528 | tf_op jit(solution)/shard_map/ppermute | solution.py:30
  9.3 1.5 %copy-start = (bf16[2,5,3,2,64,256]{5,4,3,2,1,0:T(8,128)(2,1)S(1)}, bf16[2,5,3,2,64,256]{5,4,3,2,1,0:T(8,128)(2,1)}, u32[]{:S(2)}) copy-start(bf16[2,5,3,2,64,256]{5,4,3,2,1,0:T(8,128)(2,1)} %f.3) | copy-start | bytes 5898244
  10.9 0.7 copy-start.1
  11.9 7.7 %copy-start.2 = (f32[2,8,256]{2,1,0:T(8,128)S(1)}, f32[2,8,256]{2,1,0:T(8,128)}, u32[]{:S(2)}) copy-start(f32[2,8,256]{2,1,0:T(8,128)} %shift.3) | copy-start | bytes 49156
  11.9 7.5 %collective-permute-start.6 = (f32[10,8,256]{2,1,0:T(8,128)S(1)}, f32[10,8,256]{2,1,0:T(8,128)S(1)}, u32[]{:S(2)}, u32[]{:S(2)}) collective-permute-start(f32[10,8,256]{2,1,0:T(8,128)S(1)} %get-tuple-element.21), channel_id=1, source_target_pairs={{0,64},{1,65},{2,66},{3,67},{4,68},{5,69},{6,70},{7,71},{8,72},{9,... | collective-permute-start | bytes 245768 | tf_op jit(solution)/shard_map/ppermute | solution.py:30
  13.3 6.3 %collective-permute-start.7 = (f32[10,8,256]{2,1,0:T(8,128)S(1)}, f32[10,8,256]{2,1,0:T(8,128)S(1)}, u32[]{:S(2)}, u32[]{:S(2)}) collective-permute-start(f32[10,8,256]{2,1,0:T(8,128)S(1)} %get-tuple-element.22), channel_id=1, source_target_pairs={{0,192},{1,193},{2,194},{3,195},{4,196},{5,197},{6,198},{7,199},{8... | collective-permute-start | bytes 245768 | tf_op jit(solution)/shard_map/ppermute | solution.py:30
  14.8 4.8 %collective-permute-start.8 = (f32[10,8,256]{2,1,0:T(8,128)S(1)}, f32[10,8,256]{2,1,0:T(8,128)S(1)}, u32[]{:S(2)}, u32[]{:S(2)}) collective-permute-start(f32[10,8,256]{2,1,0:T(8,128)S(1)} %get-tuple-element.23), channel_id=1, source_target_pairs={{0,128},{1,129},{2,130},{3,131},{4,132},{5,133},{6,134},{7,135},{8... | collective-permute-start | bytes 245768 | tf_op jit(solution)/shard_map/ppermute | solution.py:30
  16.7 5.1 %collective-permute-start.3 = (f32[9,8,256]{2,1,0:T(8,128)S(1)}, f32[9,8,256]{2,1,0:T(8,128)S(1)}, u32[]{:S(2)}, u32[]{:S(2)}) collective-permute-start(f32[9,8,256]{2,1,0:T(8,128)S(1)} %get-tuple-element.18), channel_id=1, source_target_pairs={{0,64},{1,65},{2,66},{3,67},{4,68},{5,69},{6,70},{7,71},{8,72},{9,... | collective-permute-start | bytes 221192 | tf_op jit(solution)/shard_map/ppermute | solution.py:30
  17.1 4.7 %collective-permute-start.4 = (f32[9,8,256]{2,1,0:T(8,128)S(1)}, f32[9,8,256]{2,1,0:T(8,128)S(1)}, u32[]{:S(2)}, u32[]{:S(2)}) collective-permute-start(f32[9,8,256]{2,1,0:T(8,128)S(1)} %get-tuple-element.19), channel_id=1, source_target_pairs={{0,192},{1,193},{2,194},{3,195},{4,196},{5,197},{6,198},{7,199},{8... | collective-permute-start | bytes 221192 | tf_op jit(solution)/shard_map/ppermute | solution.py:30
  19.4 4.7 %collective-permute-start.5 = (f32[9,8,256]{2,1,0:T(8,128)S(1)}, f32[9,8,256]{2,1,0:T(8,128)S(1)}, u32[]{:S(2)}, u32[]{:S(2)}) collective-permute-start(f32[9,8,256]{2,1,0:T(8,128)S(1)} %get-tuple-element.20), channel_id=1, source_target_pairs={{0,128},{1,129},{2,130},{3,131},{4,132},{5,133},{6,134},{7,135},{8... | collective-permute-start | bytes 221192 | tf_op jit(solution)/shard_map/ppermute | solution.py:30
  24.2 8.3 %collective-permute-start.9 = (f32[13,8,256]{2,1,0:T(8,128)S(1)}, f32[13,8,256]{2,1,0:T(8,128)S(1)}, u32[]{:S(2)}, u32[]{:S(2)}) collective-permute-start(f32[13,8,256]{2,1,0:T(8,128)S(1)} %get-tuple-element.27), channel_id=1, source_target_pairs={{0,32},{1,33},{2,34},{3,35},{4,36},{5,37},{6,38},{7,39},{8,40},{9,... | collective-permute-start | bytes 319496 | tf_op jit(solution)/shard_map/ppermute | solution.py:30
  32.7 5.4 %collective-permute-start.10 = (f32[8,16,256]{2,1,0:T(8,128)S(1)}, f32[8,16,256]{2,1,0:T(8,128)S(1)}, u32[]{:S(2)}, u32[]{:S(2)}) collective-permute-start(f32[8,16,256]{2,1,0:T(8,128)S(1)} %pad_maximum_fusion.1.block), channel_id=1, source_target_pairs={{0,1},{1,0},{2,3},{3,2},{4,5},{5,4},{6,7},{7,6},{8,9},{9,8},{10,11... | collective-permute-start | bytes 393224 | tf_op jit(solution)/shard_map/ppermute | solution.py:30
  38.1 6.8 %collective-permute-start.11 = (f32[11,16,256]{2,1,0:T(8,128)S(1)}, f32[11,16,256]{2,1,0:T(8,128)S(1)}, u32[]{:S(2)}, u32[]{:S(2)}) collective-permute-start(f32[11,16,256]{2,1,0:T(8,128)S(1)} %pad_maximum_fusion), channel_id=1, source_target_pairs={{1,2},{2,1},{3,4},{4,3},{5,6},{6,5},{7,8},{8,7},{9,10},{10,9},{11,... | collective-permute-start | bytes 540680 | tf_op jit(solution)/shard_map/ppermute | solution.py:30
  44.9 1.2 %collective-permute-start.12 = (f32[3,16,256]{2,1,0:T(8,128)S(1)}, f32[3,16,256]{2,1,0:T(8,128)S(1)}, u32[]{:S(2)}, u32[]{:S(2)}) collective-permute-start(f32[3,16,256]{2,1,0:T(8,128)S(1)} %slice.29), channel_id=1, source_target_pairs={{0,1},{1,0},{2,3},{3,2},{4,5},{5,4},{6,7},{7,6},{8,9},{9,8},{10,11... | collective-permute-start | bytes 147464 | tf_op jit(solution)/shard_map/ppermute | solution.py:30
